TPU v7x, 256 devices: a whole 4x4x8 slice. The times are simulated.
256 devices in a mesh: seq: 128 (over z, y, x), grp: 2 (over core).
Axes of the slice: x: 4, y: 4, z: 8, core: 2. Of those that a mesh axis runs over, the one named last changes fastest.
Arguments:
- queries: bfloat16 [65536, 3072], P('seq', 'grp'), parts along dimension 1, may hold values from -124 to 124
- keys: bfloat16 [65536, 384], P('seq', 'grp'), parts along dimension 1, may hold values from -4.2 to 4.2
- values: bfloat16 [65536, 256], P('seq', 'grp'), parts along dimension 1, may hold values from -6 to 6
- selected: int32 [1024, 32], P('seq', 'grp'), parts along dimension 1, may hold values from 0 to 1023, as said below
- d_out: bfloat16 [65536, 2048], P('seq', 'grp'), parts along dimension 1, may hold values from -6 to 6
Outputs:
- attended: bfloat16 [65536, 2048], P('seq', 'grp'), parts along dimension 1
- d_queries: bfloat16 [65536, 3072], P('seq', 'grp'), parts along dimension 1
- d_keys: bfloat16 [65536, 384], P('seq', 'grp'), parts along dimension 1
- d_values: bfloat16 [65536, 256], P('seq', 'grp'), parts along dimension 1
There are 2 independent parts, one for each index of `grp`. A program takes and returns all parts, laid end to end along the dimension named above; each array names one. Nothing has to cross between parts.
Inputs may be any that keep to these rules, and one draw needn't show every extreme that they name: `selected`: entry 0 of each list is the query block itself; every other entry names a block that ends before the query block starts, or repeats the query block itself. Over the 8 rows of one device, the entries that lie on any one other device name at most one distinct block, and some other device is named. Over the rows of one device, no other device is named by more than 1 entries, and in every draw some device's rows name some other device exactly 1 times.
All inputs are finite; a program needn't handle non-finite values.
Results may differ from a plain program's by a relative error of at most 0.03.
Values may be sent and summed in bfloat16 or wider, within the bound.
No kernel may reach another device: no remote copies, remote signals or barrier semaphores. Data moves between devices by JAX's collectives and lax.ppermute only.
A program may use at most 128 MiB of HBM per device.

v0:
```python
import jax
import jax.numpy as jnp
from jax import lax
from jax.sharding import PartitionSpec as P

BLK = 64
SEL = 16


def block_grads(q_rows, k_rows, v_rows, do_rows, q_pos, k_pos):
    width_k = k_rows.shape[1]
    width_v = v_rows.shape[1]
    head_count = q_rows.shape[1] // width_k
    block_len = q_rows.shape[0]
    score_scale = width_k ** (-0.5)
    query_mat = (
        q_rows.reshape(block_len, head_count, width_k)
        .transpose(1, 0, 2)
        .reshape(head_count * block_len, width_k)
    )
    grad_mat = (
        do_rows.reshape(block_len, head_count, width_v)
        .transpose(1, 0, 2)
        .reshape(head_count * block_len, width_v)
    )
    visible = jnp.tile(k_pos[None, :] <= q_pos[:, None], (head_count, 1))
    scores = (
        lax.dot_general(
            query_mat, k_rows, (((1,), (1,)), ((), ())), preferred_element_type=jnp.float32
        )
        * score_scale
    )
    scores = jnp.where(visible, scores, -jnp.inf)
    row_max = jnp.max(scores, axis=1, keepdims=True)
    expons = jnp.exp(scores - row_max)
    probs = expons / jnp.sum(expons, axis=1, keepdims=True)
    probs_low = probs.astype(jnp.bfloat16)
    attended = jnp.dot(probs_low, v_rows, preferred_element_type=jnp.float32).astype(jnp.bfloat16)
    d_probs = lax.dot_general(
        grad_mat, v_rows, (((1,), (1,)), ((), ())), preferred_element_type=jnp.float32
    )
    row_delta = jnp.sum(
        grad_mat.astype(jnp.float32) * attended.astype(jnp.float32), axis=1, keepdims=True
    )
    d_scores = (probs * (d_probs - row_delta)).astype(jnp.bfloat16)
    d_query = (jnp.dot(d_scores, k_rows, preferred_element_type=jnp.float32) * score_scale).astype(
        jnp.bfloat16
    )
    d_key = (
        lax.dot_general(
            d_scores, query_mat, (((0,), (0,)), ((), ())), preferred_element_type=jnp.float32
        )
        * score_scale
    )
    d_value = lax.dot_general(
        probs_low, grad_mat, (((0,), (0,)), ((), ())), preferred_element_type=jnp.float32
    )
    attended = (
        attended.reshape(head_count, block_len, width_v)
        .transpose(1, 0, 2)
        .reshape(block_len, head_count * width_v)
    )
    d_query = (
        d_query.reshape(head_count, block_len, width_k)
        .transpose(1, 0, 2)
        .reshape(block_len, head_count * width_k)
    )
    return (attended, d_query, d_key, d_value)


def shards(queries, keys, values, selected, d_out):
    seq_count = lax.axis_size("seq")
    my_index = lax.axis_index("seq")
    tok_rows = keys.shape[0]
    width_k = keys.shape[1]
    row_width = width_k + values.shape[1]
    half_len = tok_rows // 2
    local_blocks = tok_rows // BLK
    per_half = local_blocks // 2
    offsets = jnp.arange(BLK, dtype=jnp.int32)
    row_ids = jnp.arange(tok_rows, dtype=jnp.int32)
    positions = jnp.where(
        row_ids < half_len,
        my_index * half_len + row_ids,
        (2 * seq_count - 1 - my_index) * half_len + row_ids - half_len,
    )
    slots_each = 1
    half_index = selected // per_half
    is_late = half_index >= seq_count
    owners = jnp.where(is_late, 2 * seq_count - 1 - half_index, half_index)
    inner_block = selected % per_half + jnp.where(is_late, per_half, 0)
    owners, inner_block = (owners, inner_block)
    flat_owner = owners.reshape(-1)
    flat_inner = inner_block.reshape(-1)
    flat_remote = flat_owner != my_index
    peer_ids = jnp.arange(seq_count, dtype=jnp.int32)
    rank_ids = jnp.arange(slots_each, dtype=jnp.int32)
    matches = (flat_owner[:, None] == peer_ids[None, :]) & flat_remote[:, None]
    order = jnp.zeros(matches.shape, jnp.int32)
    entry_rank = jnp.sum(jnp.where(matches, order, 0), axis=1)
    picks = matches[:, :, None] & (order[:, :, None] == rank_ids[None, None, :])
    wanted = jnp.max(jnp.where(picks, flat_inner[:, None, None] + 1, 0), axis=0)
    asked = lax.all_to_all(wanted, "seq", split_axis=0, concat_axis=0, tiled=True) - 1
    asked_flat = asked.reshape(seq_count * slots_each)
    joined = jnp.concatenate([keys, values], axis=1).reshape(local_blocks, BLK, row_width)
    outgoing = jnp.where(
        (asked_flat >= 0)[:, None, None],
        joined[jnp.maximum(asked_flat, 0)],
        jnp.zeros((), jnp.bfloat16),
    )
    fetched = lax.all_to_all(outgoing, "seq", split_axis=0, concat_axis=0, tiled=True)
    table = jnp.concatenate([joined, fetched], axis=0)
    slot_ids = jnp.where(
        flat_remote, local_blocks + flat_owner * slots_each + entry_rank, flat_inner
    ).reshape(local_blocks, SEL)
    query_blocks = queries.reshape(local_blocks, BLK, -1)
    grad_blocks = d_out.reshape(local_blocks, BLK, -1)

    def visit_block(block_index):
        key_tiles = table[slot_ids[block_index]].reshape(SEL * BLK, row_width)
        k_pos = (selected[block_index][:, None] * BLK + offsets[None, :]).reshape(-1)
        q_pos = lax.dynamic_slice_in_dim(positions, block_index * BLK, BLK)
        attended, d_query, d_key, d_value = block_grads(
            query_blocks[block_index],
            key_tiles[:, :width_k],
            key_tiles[:, width_k:],
            grad_blocks[block_index],
            q_pos,
            k_pos,
        )
        return (attended, d_query, jnp.concatenate([d_key, d_value], axis=1))

    attended, d_query, partials = lax.map(visit_block, jnp.arange(local_blocks, dtype=jnp.int32))
    remote_slots = seq_count * slots_each
    summed = jax.ops.segment_sum(
        partials.reshape(local_blocks * SEL, BLK * row_width),
        slot_ids.reshape(-1),
        num_segments=local_blocks + remote_slots,
    )
    sending = summed[local_blocks:].reshape(remote_slots, BLK, row_width)
    returned = lax.all_to_all(sending, "seq", split_axis=0, concat_axis=0, tiled=True)
    landing = jnp.where(asked_flat >= 0, asked_flat, local_blocks)
    own_grads = (
        summed[:local_blocks]
        + jax.ops.segment_sum(
            returned.reshape(remote_slots, BLK * row_width), landing, num_segments=local_blocks + 1
        )[:local_blocks]
    )
    own_grads = own_grads.reshape(tok_rows, row_width)
    return (
        attended.reshape(tok_rows, -1),
        d_query.reshape(tok_rows, -1),
        own_grads[:, :width_k].astype(jnp.bfloat16),
        own_grads[:, width_k:].astype(jnp.bfloat16),
    )


def solution(mesh):
    return jax.shard_map(
        shards,
        mesh=mesh,
        in_specs=(
            P("seq", "grp"),
            P("seq", "grp"),
            P("seq", "grp"),
            P("seq", "grp"),
            P("seq", "grp"),
        ),
        out_specs=(P("seq", "grp"), P("seq", "grp"), P("seq", "grp"), P("seq", "grp")),
        check_vma=False,
    )
```

profile of v0, /device:TPU:2, one launch (start us, length us, event | category | flops | bytes accessed | tf_op | source)
XLA Modules:
  0.0 757.3 jit_solution(5277004550030942455)
XLA Ops:
  2.4 15.4 %all-to-all-start = ((s32[128,1,1]{2,1,0:T(1,128)}), s32[128,1,1]{2,1,0:T(1,128)S(1)}, u32[]{:S(2)}, u32[]{:S(2)}) async-start(s32[128,1,1]{2,1,0:T(1,128)} %copy.68), calls=%async_computation | async-start | bytes 131072 | tf_op jit(solution)/shard_map/all_to_all | solution.py:103
  17.8 1.0 copy.66
  18.8 1.0 pad_maximum_fusion.1
  20.0 9.1 %all-to-all-done = s32[128,1,1]{2,1,0:T(1,128)S(1)} async-done(((s32[128,1,1]{2,1,0:T(1,128)}), s32[128,1,1]{2,1,0:T(1,128)S(1)}, u32[]{:S(2)}, u32[]{:S(2)}) %all-to-all-start) | async-done | bytes 544 | tf_op jit(solution)/shard_map/all_to_all | solution.py:103
  29.1 2.4 add_reduce_fusion
  32.0 4.1 gather_fusion.1
  36.0 2.4 compare_reduce_fusion
  38.4 6.1 broadcast_select_fusion
  44.5 8.4 %all-to-all-start.1 = ((bf16[128,64,320]{2,1,0:T(8,128)(2,1)}), bf16[128,64,320]{2,1,0:T(8,128)(2,1)}, u32[]{:S(2)}, u32[]{:S(2)}) async-start(bf16[128,64,320]{2,1,0:T(8,128)(2,1)} %broadcast_select_fusion), calls=%async_computation.1 | async-start | bytes 12582912 | tf_op jit(solution)/shard_map/all_to_all | solution.py:111
  53.0 139.3 %all-to-all-done.1 = bf16[128,64,320]{2,1,0:T(8,128)(2,1)} async-done(((bf16[128,64,320]{2,1,0:T(8,128)(2,1)}), bf16[128,64,320]{2,1,0:T(8,128)(2,1)}, u32[]{:S(2)}, u32[]{:S(2)}) %all-to-all-start.1) | async-done | bytes 5242912 | tf_op jit(solution)/shard_map/all_to_all | solution.py:111
  192.4 6.7 pad_maximum_fusion
  199.6 153.9 %while.15 = (s32[]{:T(128)}, bf16[8,64,1024]{2,1,0:T(8,128)(2,1)}, bf16[8,64,1536]{2,1,0:T(8,128)(2,1)}, f32[8,1024,320]{1,2,0:T(8,128)}, s32[8]{0:T(128)}, /*in...) while((s32[]{:T(128)}, bf16[8,64,1024]{2,1,0:T(8,128)(2,1)}, ...), condition=%wide.region_5.6_spmd.clone, body=%wide.region_1.5_spmd.clone.sunk | while | flops 1016136256 | bytes 32542196 | solution.py:133
  199.6 1.3 dynamic_slice.49
  204.7 0.9 dynamic-slice_bitcast_fusion.2
  205.7 0.9 constant_dynamic-slice_fusion.4
  206.9 3.6 gather_fusion
  213.1 1.2 fusion.68
  217.7 1.2 fusion.69
  218.9 1.3 dynamic_slice.49
  225.0 0.9 constant_dynamic-slice_fusion.4
  226.2 3.6 gather_fusion
  232.4 1.2 fusion.68
  237.0 1.2 fusion.69
  238.1 1.3 dynamic_slice.49
  244.2 0.9 constant_dynamic-slice_fusion.4
  245.4 3.6 gather_fusion
  251.6 1.1 fusion.68
  256.2 1.2 fusion.69
  257.3 1.3 dynamic_slice.49
  263.4 0.9 constant_dynamic-slice_fusion.4
  264.7 3.6 gather_fusion
  270.9 1.2 fusion.68
  275.4 1.2 fusion.69
  276.6 1.3 dynamic_slice.49
  282.7 0.9 constant_dynamic-slice_fusion.4
  283.9 3.6 gather_fusion
  290.1 1.2 fusion.68
  294.6 1.2 fusion.69
  295.8 1.3 dynamic_slice.49
  301.9 0.9 constant_dynamic-slice_fusion.4
  303.1 3.6 gather_fusion
  309.3 1.2 fusion.68
  313.9 1.2 fusion.69
  315.0 1.3 dynamic_slice.49
  321.1 0.9 constant_dynamic-slice_fusion.4
  322.4 3.6 gather_fusion
  328.6 1.2 fusion.68
  333.1 1.2 fusion.69
  334.3 1.3 dynamic_slice.49
  340.4 0.9 constant_dynamic-slice_fusion.4
  341.6 3.6 gather_fusion
  347.8 1.2 fusion.68
  352.3 1.2 fusion.69
  353.5 11.8 %copy.69 = f32[8,1024,320]{2,1,0:T(8,128)} copy(f32[8,1024,320]{1,2,0:T(8,128)} %get-tuple-element.70) | data formatting | bytes 20971520 | tf_op jit(solution)/shard_map/while | solution.py:133
  365.3 12.8 %reshape.337 = f32[128,20480]{1,0:T(8,128)} reshape(f32[8,1024,320]{2,1,0:T(8,128)} %copy.69) | data formatting | bytes 20971520 | tf_op jit(solution)/shard_map/reshape | solution.py:136
  378.1 20.2 %scatter_custom_fusion = f32[136,20480]{1,0:T(8,128)} fusion(s32[128]{0:T(128)S(1)} %reshape.335, f32[128,20480]{1,0:T(8,128)} %reshape.337, f32[]{:T(128)} %constant.42.clone.1), kind=kCustom, calls=%fused_computation.42 | custom fusion | flops 2621440 | bytes 11141632 | tf_op jit(solution)/shard_map/scatter-add | solution.py:135
  398.3 9.0 %slice.37 = f32[128,20480]{1,0:T(8,128)} slice(f32[136,20480]{1,0:T(8,128)} %scatter_custom_fusion), slice={[8:136], [0:20480]} | slice | bytes 20971520 | tf_op jit(solution)/shard_map/slice | solution.py:140
  407.3 11.8 %copy.70 = f32[128,20480]{0,1:T(8,128)} copy(f32[128,20480]{1,0:T(8,128)} %slice.37) | data formatting | bytes 20971520 | tf_op jit(solution)/shard_map/slice | solution.py:140
  419.0 12.1 %copy.71 = f32[128,64,320]{2,1,0:T(8,128)} copy(f32[128,64,320]{0,2,1:T(8,128)} %bitcast.121) | data formatting | bytes 20971520 | tf_op jit(solution)/shard_map/reshape | solution.py:140
  431.1 283.1 %all_to_all.19 = f32[128,64,320]{2,1,0:T(8,128)} all-to-all(f32[128,64,320]{2,1,0:T(8,128)} %copy.71), channel_id=1, replica_groups=mesh['seq'=128,'grp'=2] {'seq'}, dimensions={0} | all-to-all | bytes 20971520 | tf_op jit(solution)/shard_map/all_to_all | solution.py:141
  714.1 11.9 %copy.72 = f32[128,64,320]{0,2,1:T(8,128)} copy(f32[128,64,320]{2,1,0:T(8,128)} %all_to_all.19) | data formatting | bytes 20971520 | tf_op jit(solution)/shard_map/all_to_all | solution.py:141
  726.1 11.8 %copy.73 = f32[128,20480]{1,0:T(8,128)} copy(f32[128,20480]{0,1:T(8,128)} %bitcast.122) | data formatting | bytes 20971520 | tf_op jit(solution)/shard_map/reshape | solution.py:146
  737.8 15.8 %scatter_custom_fusion.1 = f32[9,20480]{1,0:T(8,128)S(1)} fusion(s32[128]{0:T(128)} %get-tuple-element.148, f32[128,20480]{1,0:T(8,128)} %copy.73, f32[]{:T(128)} %constant.42.clone.1), kind=kCustom, calls=%fused_computation.46 | custom fusion | flops 2621440 | bytes 737792 | tf_op jit(solution)/shard_map/scatter-add | solution.py:145
  753.7 1.1 fusion.21
  (242 shorter events, 69.5 us)
Async XLA Ops:
  2.4 26.7 %all-to-all-start = ((s32[128,1,1]{2,1,0:T(1,128)}), s32[128,1,1]{2,1,0:T(1,128)S(1)}, u32[]{:S(2)}, u32[]{:S(2)}) async-start(s32[128,1,1]{2,1,0:T(1,128)} %copy.68), calls=%async_computation | async-start | bytes 131072 | tf_op jit(solution)/shard_map/all_to_all | solution.py:103
  44.5 147.9 %all-to-all-start.1 = ((bf16[128,64,320]{2,1,0:T(8,128)(2,1)}), bf16[128,64,320]{2,1,0:T(8,128)(2,1)}, u32[]{:S(2)}, u32[]{:S(2)}) async-start(bf16[128,64,320]{2,1,0:T(8,128)(2,1)} %broadcast_select_fusion), calls=%async_computation.1 | async-start | bytes 12582912 | tf_op jit(solution)/shard_map/all_to_all | solution.py:111
  215.3 2.3 copy-start
  234.6 2.3 copy-start
  253.8 2.3 copy-start
  273.1 2.3 copy-start
  292.3 2.3 copy-start
  311.5 2.3 copy-start
  330.8 2.3 copy-start
  350.0 2.3 copy-start
where the time goes:
time: 767 us; the launch traced here: 757 us
  blocking collectives  283 us (37%)
  local copies, waits for them, and re-layouts  164 us (21%)
  waiting for transfers between devices  148 us (19%)
  other arithmetic  83.4 us (11%)
  matrix products  30.2 us (4%)
  starting transfers between devices  23.8 us (3%)
  loops' own time  23.1 us (3%)
    all_to_all x1, blocking collectives, shards(): lax.all_to_all(sending, 'seq', split_axis=0, concat_axis=0, tiled=True)  283 us
    all_to_all x1, waiting for transfers between devices, shards(): lax.all_to_all(outgoing, 'seq', split_axis=0, concat_axis=0, tiled=True)  139 us
    gather x8, local copies, waits for them, and re-layouts, visit_block(): key_tiles = table[slot_ids[block_index]].reshape(SEL * BLK, row_width)  28.9 us
    another operation x1, loops' own time, shards(): lax.map(visit_block, jnp.arange(local_blocks, dtype=jnp.int32))  23.1 us
    slice x2, local copies, waits for them, and re-layouts, shards(): sending = summed[local_blocks:].reshape(remote_slots, BLK, row_width)  20.7 us
    scatter-add x1, other arithmetic, shards(): jax.ops.segment_sum(partials.reshape(local_blocks * SEL, BLK * row_width)...  20.2 us
    scatter-add x1, other arithmetic, shards(): jax.ops.segment_sum(returned.reshape(remote_slots, BLK * row_width), land...  15.8 us
    all_to_all x1, starting transfers between devices, shards(): lax.all_to_all(wanted, 'seq', split_axis=0, concat_axis=0, tiled=True) - 1  15.4 us
  transfers between devices with their start and end apart: 2, of which 2 were waited for; matrix products, arithmetic and copies ran while one was open for 0% of the time, Pallas kernels for 0%

commit v1 on v0

v1 whole, which is shorter than its diff:
```python
import functools

import jax
import jax.numpy as jnp
from jax import lax
from jax.experimental import pallas as pl
from jax.experimental.pallas import tpu as pltpu
from jax.sharding import Mesh, PartitionSpec as P

BLK = 64
SEL = 16
HEADS = 8
DK = 192
DV = 128
ROWS = 160
SIDES = (8, 4, 4)
LOCAL = 8
CHUNK = 256
LOG2E = 1.4426950408889634
NEG = -1e30
BF = jnp.bfloat16
F32 = jnp.float32


def params(mib=56):
    return pltpu.CompilerParams(vmem_limit_bytes=mib * 1024 * 1024)


def pack_kernel(k_ref, v_ref, out_ref):
    for b in range(LOCAL):
        rows = slice(b * BLK, (b + 1) * BLK)
        k = k_ref[rows, :]
        out_ref[b, 0:BLK] = v_ref[rows, :]
        out_ref[b, BLK : 2 * BLK] = k[:, :128]
        low = k[:, 128:]
        out_ref[b, 2 * BLK :] = jnp.concatenate([low[:32], low[32:]], axis=1)


def pack(keys, values):
    return pl.pallas_call(
        pack_kernel,
        out_shape=jax.ShapeDtypeStruct((LOCAL, ROWS, 128), BF),
        compiler_params=params(),
        name="pack",
    )(keys, values)


def build_kernel(req_ref, table_ref, out_ref):
    c = pl.program_id(0)
    for z in range(table_ref.shape[0]):
        r = req_ref[c, z]

        @pl.when(r > 0)
        def _():
            out_ref[0, z] = table_ref[z, r - 1]


def build(req, table, plane):
    depth = table.shape[0]
    return pl.pallas_call(
        build_kernel,
        grid_spec=pltpu.PrefetchScalarGridSpec(
            num_scalar_prefetch=1,
            grid=(plane,),
            in_specs=[pl.BlockSpec((depth, LOCAL, ROWS, 128), lambda c, req: (0, 0, 0, 0))],
            out_specs=pl.BlockSpec((1, depth, ROWS, 128), lambda c, req: (c, 0, 0, 0)),
        ),
        out_shape=jax.ShapeDtypeStruct((plane, depth, ROWS, 128), BF),
        compiler_params=params(),
        name="build",
    )(req, table)


def sum_kernel(req_ref, ret_ref, out_ref, acc_ref):
    z = pl.program_id(0)
    acc_ref[...] = jnp.zeros_like(acc_ref)
    for c in range(ret_ref.shape[0]):
        r = req_ref[c, z]

        @pl.when(r > 0)
        def _():
            acc_ref[r - 1] += ret_ref[c, 0].astype(F32)

    out_ref[0] = acc_ref[...].astype(BF)


def sum_returned(req, returned):
    plane, depth = returned.shape[:2]
    return pl.pallas_call(
        sum_kernel,
        grid_spec=pltpu.PrefetchScalarGridSpec(
            num_scalar_prefetch=1,
            grid=(depth,),
            in_specs=[pl.BlockSpec((plane, 1, ROWS, 128), lambda z, req: (0, z, 0, 0))],
            out_specs=pl.BlockSpec((1, LOCAL, ROWS, 128), lambda z, req: (z, 0, 0, 0)),
            scratch_shapes=[pltpu.VMEM((LOCAL, ROWS, 128), F32)],
        ),
        out_shape=jax.ShapeDtypeStruct((depth, LOCAL, ROWS, 128), BF),
        compiler_params=params(),
        name="sum_returned",
    )(req, returned)


def finish_kernel(own_ref, got_ref, dk_ref, dv_ref):
    for b in range(LOCAL):
        rows = slice(b * BLK, (b + 1) * BLK)
        total = own_ref[b] + got_ref[b].astype(F32)
        dv_ref[rows, :] = total[0:BLK].astype(BF)
        low = total[2 * BLK :]
        low = jnp.concatenate([low[:, :64], low[:, 64:]], axis=0)
        dk_ref[rows, :] = jnp.concatenate([total[BLK : 2 * BLK], low], axis=1).astype(BF)


def finish(own, got):
    return pl.pallas_call(
        finish_kernel,
        out_shape=(
            jax.ShapeDtypeStruct((LOCAL * BLK, DK), BF),
            jax.ShapeDtypeStruct((LOCAL * BLK, DV), BF),
        ),
        compiler_params=params(),
        name="finish",
    )(own, got)


def dot(a, b, da, db):
    return lax.dot_general(a, b, (((da,), (db,)), ((), ())), preferred_element_type=F32)


def attend_kernel(
    src_ref,
    q_ref,
    do_ref,
    local_ref,
    got_ref,
    att_ref,
    dq_ref,
    part_ref,
    own_ref,
    k_buf,
    v_buf,
    q_buf,
    do_buf,
    p_buf,
    pb_buf,
):
    b = pl.program_id(0)
    depth = got_ref.shape[1]
    scale = DK**-0.5
    queries = HEADS * BLK

    @pl.when(b == 0)
    def _():
        own_ref[...] = jnp.zeros_like(own_ref)
        v_buf[:, 128:] = jnp.ones((SEL * BLK, 128), BF)
        row = lax.broadcasted_iota(jnp.int32, (BLK, BLK), 0)
        col = lax.broadcasted_iota(jnp.int32, (BLK, BLK), 1)
        one_hot = (row == col).astype(BF)
        for h in range(HEADS):
            q_buf[h * BLK : (h + 1) * BLK, DK:] = one_hot

    def place(e, tile, hidden):
        rows = slice(e * BLK, (e + 1) * BLK)
        v_buf[rows, 0:128] = tile[0:BLK]
        k_buf[rows, 0:128] = tile[BLK : 2 * BLK]
        low = tile[2 * BLK :]
        low = jnp.concatenate([low[:, :64], low[:, 64:]], axis=0)
        k_buf[rows, 128:] = jnp.concatenate([low, hidden], axis=1)

    nothing = jnp.zeros((BLK, BLK), BF)
    key_id = lax.broadcasted_iota(jnp.int32, (BLK, BLK), 0)
    query_id = lax.broadcasted_iota(jnp.int32, (BLK, BLK), 1)
    later = jnp.where(key_id > query_id, NEG, 0.0).astype(BF)
    for e in range(SEL):
        s = src_ref[b, e]

        @pl.when(s >= 0)
        def _():
            place(e, got_ref[s // depth, s % depth], nothing)

        @pl.when(s < 0)
        def _():
            place(e, local_ref[-1 - s], jnp.where(-1 - s == b, later, nothing))

    for h in range(HEADS):
        q_buf[h * BLK : (h + 1) * BLK, 0:DK] = q_ref[:, h * DK : (h + 1) * DK]

    q_all = q_buf[...]
    top = None
    for i in range(0, SEL * BLK, CHUNK):
        s = dot(k_buf[i : i + CHUNK, :], q_all, 1, 1)
        p_buf[i : i + CHUNK, :] = s
        m = jnp.max(s, axis=0, keepdims=True)
        top = m if top is None else jnp.maximum(top, m)
    out_t = None
    for i in range(0, SEL * BLK, CHUNK):
        p = jnp.exp2((p_buf[i : i + CHUNK, :] - top) * (scale * LOG2E))
        p_buf[i : i + CHUNK, :] = p
        pb = p.astype(BF)
        pb_buf[i : i + CHUNK, :] = pb
        o = dot(v_buf[i : i + CHUNK, :], pb, 0, 0)
        out_t = o if out_t is None else out_t + o
    out = jnp.transpose(out_t)
    inverse = 1.0 / out[:, 128:129]
    att = (out[:, :128] * inverse).astype(BF)
    for h in range(HEADS):
        rows = slice(h * BLK, (h + 1) * BLK)
        att_ref[:, h * DV : (h + 1) * DV] = att[rows]
        do = (do_ref[:, h * DV : (h + 1) * DV].astype(F32) * inverse[rows]).astype(BF)
        delta = jnp.sum(do.astype(F32) * att[rows].astype(F32), axis=1, keepdims=True)
        high = delta.astype(BF)
        rest = delta - high.astype(F32)
        mid = rest.astype(BF)
        last = (rest - mid.astype(F32)).astype(BF)
        lane = lax.broadcasted_iota(jnp.int32, (BLK, 128), 1)
        extra = jnp.where(
            lane == 0,
            high.astype(F32),
            jnp.where(lane == 1, mid.astype(F32), jnp.where(lane == 2, last.astype(F32), 0.0)),
        )
        do_buf[rows, 0:128] = do
        do_buf[rows, 128:] = (-extra).astype(BF)
    do_all = do_buf[...]
    dq_t = None
    for i in range(0, SEL * BLK, CHUNK):
        dp = dot(v_buf[i : i + CHUNK, :], do_all, 1, 1)
        ds = (p_buf[i : i + CHUNK, :] * dp).astype(BF)
        dv = dot(pb_buf[i : i + CHUNK, :], do_buf[:, 0:128], 1, 0)
        dk = dot(ds, q_all, 1, 0) * scale
        g = dot(k_buf[i : i + CHUNK, :], ds, 0, 0)
        dq_t = g if dq_t is None else dq_t + g
        for j in range(CHUNK // BLK):
            e = i // BLK + j
            rows = slice(j * BLK, (j + 1) * BLK)
            low = dk[rows, 128:DK]
            low = jnp.concatenate([low[:32], low[32:]], axis=1)
            tile = jnp.concatenate([dv[rows], dk[rows, :128], low], axis=0)
            s = src_ref[b, e]

            @pl.when(s >= 0)
            def _():
                part_ref[s // depth, s % depth] = tile.astype(BF)

            @pl.when(s < 0)
            def _():
                own_ref[-1 - s] += tile
    dq = (jnp.transpose(dq_t[:DK]) * scale).astype(BF)
    for h in range(0, HEADS, 2):
        dq_ref[:, h * DK : (h + 2) * DK] = jnp.concatenate(
            [dq[h * BLK : (h + 1) * BLK], dq[(h + 1) * BLK : (h + 2) * BLK]], axis=1
        )


def attend(src, queries, d_out, local, got):
    plane, depth = got.shape[:2]
    tokens = LOCAL * BLK
    keys = SEL * BLK
    rows = HEADS * BLK
    whole = pl.BlockSpec(got.shape, lambda b, src: (0, 0, 0, 0))
    return pl.pallas_call(
        attend_kernel,
        grid_spec=pltpu.PrefetchScalarGridSpec(
            num_scalar_prefetch=1,
            grid=(LOCAL,),
            in_specs=[
                pl.BlockSpec((BLK, HEADS * DK), lambda b, src: (b, 0)),
                pl.BlockSpec((BLK, HEADS * DV), lambda b, src: (b, 0)),
                pl.BlockSpec((LOCAL, ROWS, 128), lambda b, src: (0, 0, 0)),
                whole,
            ],
            out_specs=[
                pl.BlockSpec((BLK, HEADS * DV), lambda b, src: (b, 0)),
                pl.BlockSpec((BLK, HEADS * DK), lambda b, src: (b, 0)),
                whole,
                pl.BlockSpec((LOCAL, ROWS, 128), lambda b, src: (0, 0, 0)),
            ],
            scratch_shapes=[
                pltpu.VMEM((keys, 256), BF),
                pltpu.VMEM((keys, 256), BF),
                pltpu.VMEM((rows, 256), BF),
                pltpu.VMEM((rows, 256), BF),
                pltpu.VMEM((keys, rows), F32),
                pltpu.VMEM((keys, rows), BF),
            ],
        ),
        out_shape=(
            jax.ShapeDtypeStruct((tokens, HEADS * DV), BF),
            jax.ShapeDtypeStruct((tokens, HEADS * DK), BF),
            jax.ShapeDtypeStruct(got.shape, BF),
            jax.ShapeDtypeStruct((LOCAL, ROWS, 128), F32),
        ),
        compiler_params=params(),
        name="attend",
    )(src, queries, d_out, local, got)


def shards(depth, plane, queries, keys, values, selected, d_out):
    me = lax.axis_index(("z", "y", "x"))
    seq_count = depth * plane
    per_half = LOCAL // 2
    half_index = selected // per_half
    is_late = half_index >= seq_count
    owners = jnp.where(is_late, 2 * seq_count - 1 - half_index, half_index)
    inner = selected % per_half + jnp.where(is_late, per_half, 0)
    remote = owners != me
    slots = (owners % plane) * depth + owners // plane
    src = jnp.where(remote, slots, -1 - inner).astype(jnp.int32)
    flat = src.reshape(-1)
    hits = flat[:, None] == jnp.arange(seq_count, dtype=jnp.int32)[None, :]
    wanted = jnp.max(jnp.where(hits, inner.reshape(-1)[:, None] + 1, 0), axis=0)
    asked = lax.all_to_all(
        wanted.reshape(plane, 1, depth), ("y", "x"), split_axis=0, concat_axis=0, tiled=True
    ).reshape(plane, depth)
    local = pack(keys, values)
    table = lax.all_gather(local, "z")
    outgoing = build(asked, table, plane)
    got = lax.all_to_all(outgoing, ("y", "x"), split_axis=0, concat_axis=0, tiled=True)
    attended, d_queries, partial, own = attend(src, queries, d_out, local, got)
    returned = lax.all_to_all(partial, ("y", "x"), split_axis=0, concat_axis=0, tiled=True)
    sums = sum_returned(asked, returned)
    mine = lax.psum_scatter(sums, "z", scatter_dimension=0)
    d_keys, d_values = finish(own, mine)
    return attended, d_queries, d_keys, d_values


def solution(mesh):
    grid = Mesh(mesh.devices.reshape(SIDES + (-1,)), ("z", "y", "x", "grp"))
    spec = P(("z", "y", "x"), "grp")
    return jax.shard_map(
        functools.partial(shards, SIDES[0], SIDES[1] * SIDES[2]),
        mesh=grid,
        in_specs=(spec,) * 5,
        out_specs=(spec,) * 4,
        check_vma=False,
    )
```

time: 767 us -> 312 us (0.41); the launches traced: 757 us -> 311 us
  local copies, waits for them, and re-layouts: 164 us -> 3.77 us
  blocking collectives: 283 us -> 142 us
  other arithmetic: 83.4 us -> 0.83 us
  Pallas kernels: 0 us -> 79.3 us
  waiting for transfers between devices: 148 us -> 70.7 us
  matrix products: 30.2 us -> 0 us
  starting transfers between devices: 23.8 us -> 0.08 us
  loops' own time: 23.1 us -> 0 us
  between operations: 1.12 us -> 14.1 us
    all_to_all x2 -> x0, waiting for transfers between devices: 148 us -> none  [the longest x1 139 us: shards(): lax.all_to_all(outgoing, 'seq', split_axis=0, concat_axis=0, tiled=True)]
    all_to_all x1 -> x3, blocking collectives: 283 us -> 142 us  [the longest x1 65.2 us: shards(): lax.all_to_all(outgoing, ('y', 'x'), split_axis=0, concat_axis=0, tiled=T...]
    pallas_call x0 -> x5, Pallas kernels: none -> 79.3 us  [the longest x1 58.5 us: attend(): pl.pallas_call(attend_kernel, grid_spec=pltpu.PrefetchScalarGridSpec(num_...]
    reduce_scatter x0 -> x1, waiting for transfers between devices: none -> 39.9 us  [shards(): mine = lax.psum_scatter(sums, 'z', scatter_dimension=0)]
    reshape x3 -> x1, local copies, waits for them, and re-layouts: 36.6 us -> 0.08 us  [shards(): wanted.reshape(plane, 1, depth)]
    scatter-add x2 -> x0, other arithmetic: 36 us -> none  [the longest x1 20.2 us: shards(): jax.ops.segment_sum(partials.reshape(local_blocks * SEL, BLK * row_width)...]
    gather x9 -> x0, local copies, waits for them, and re-layouts: 33 us -> none  [the longest x8 28.9 us: visit_block(): key_tiles = table[slot_ids[block_index]].reshape(SEL * BLK, row_width)]
    all_gather x0 -> x1, waiting for transfers between devices: none -> 30.8 us  [shards(): table = lax.all_gather(local, 'z')]
where the time goes in v1:
time: 312 us; the launch traced here: 311 us
  blocking collectives  142 us (46%)
  Pallas kernels  79.3 us (25%)
  waiting for transfers between devices  70.7 us (23%)
  between operations  14.1 us (5%)
  local copies, waits for them, and re-layouts  3.77 us (1%)
    all_to_all x1, blocking collectives, shards(): lax.all_to_all(outgoing, ('y', 'x'), split_axis=0, concat_axis=0, tiled=T...  65.2 us
    all_to_all x1, blocking collectives, shards(): lax.all_to_all(partial, ('y', 'x'), split_axis=0, concat_axis=0, tiled=True)  63.4 us
    pallas_call x1, Pallas kernels, attend(): pl.pallas_call(attend_kernel, grid_spec=pltpu.PrefetchScalarGridSpec(num_...  58.5 us
    reduce_scatter x1, waiting for transfers between devices, shards(): mine = lax.psum_scatter(sums, 'z', scatter_dimension=0)  39.9 us
    all_gather x1, waiting for transfers between devices, shards(): table = lax.all_gather(local, 'z')  30.8 us
    all_to_all x1, blocking collectives, shards(): lax.all_to_all(wanted.reshape(plane, 1, depth), ('y', 'x'), split_axis=0,...  13.4 us
    pallas_call x1, Pallas kernels, build(): pl.pallas_call(build_kernel, grid_spec=pltpu.PrefetchScalarGridSpec(num_s...  8.87 us
    pallas_call x1, Pallas kernels, sum_returned(): pl.pallas_call(sum_kernel, grid_spec=pltpu.PrefetchScalarGridSpec(num_sca...  8.14 us
  transfers between devices with their start and end apart: 2, of which 2 were waited for; matrix products, arithmetic and copies ran while one was open for 0% of the time, Pallas kernels for 0%

profile of v1, /device:TPU:2, one launch (start us, length us, event | category | flops | bytes accessed | tf_op | source)
XLA Modules:
  0.0 310.8 jit_solution(18275460496308887065)
XLA Ops:
  7.2 0.0 all-gather.3.cloned.1.call-start
  7.2 1.8 copy.25.k_ref
  9.0 1.8 pack.1.local_ref
  10.8 0.0 all-gather.3.cloned.1.call-update
  10.8 0.0 reduce-scatter.2.cloned.1.call-start
  10.9 0.7 broadcast_add_fusion
  11.6 0.0 copy-start
  11.6 0.1 add.45
  11.7 0.1 eq.18
  11.7 0.1 select_reduce_fusion
  11.9 0.1 reshape.24
  11.9 13.4 %all_to_all.15 = s32[16,1,8]{2,1,0:T(1,128)} all-to-all(s32[16,1,8]{2,1,0:T(1,128)S(1)} %bitcast.8), channel_id=1, replica_groups=mesh['z'=8,'y'=4,'x'=4,'grp'=2] {'y','x'}, dimensions={0} | all-to-all | bytes 1024 | tf_op jit(solution)/shard_map/all_to_all | solution.py:311
  25.4 30.8 %all-gather.3.cloned.1.call-done = bf16[64,160,128]{2,1,0:T(8,128)(2,1)} async-done(((bf16[8,160,128]{2,1,0:T(8,128)(2,1)}), bf16[64,160,128]{2,1,0:T(8,128)(2,1)}) %all-gather.3.cloned.1.call-update) | async-done | bytes 2621456 | tf_op jit(solution)/shard_map/all_gather | solution.py:315
  56.2 8.9 %build.1 = bf16[16,8,160,128]{3,2,1,0:T(8,128)(2,1)} custom-call(s32[16,8]{1,0:T(8,128)} %bitcast.6, bf16[8,8,160,128]{3,2,1,0:T(8,128)(2,1)} %bitcast.4), custom_call_target="tpu_custom_call" | custom-call | tf_op jit(solution)/shard_map/build/pallas_call | solution.py:60
  65.1 65.2 %all_to_all.16.got_ref = bf16[16,8,160,128]{3,2,1,0:T(8,128)(2,1)} all-to-all(bf16[16,8,160,128]{3,2,1,0:T(8,128)(2,1)} %build.1), channel_id=1, replica_groups=mesh['z'=8,'y'=4,'x'=4,'grp'=2] {'y','x'}, dimensions={0} | all-to-all | bytes 10485760 | tf_op jit(solution)/shard_map/all_to_all | solution.py:317
  130.3 0.0 copy-done
  130.3 58.5 %attend.1 = (bf16[512,1024]{1,0:T(8,128)(2,1)}, bf16[512,1536]{1,0:T(8,128)(2,1)}, bf16[16,8,160,128]{3,2,1,0:T(8,128)(2,1)}, f32[8,160,128]{2,1,0:T(8,128)}) custom-call(s32[8,16]{1,0:T(8,128)} %copy-done, bf16[512,1536]{1,0:T(8,128)(2,1)} %q_ref.1, bf16[512,1024]{1,0:T(8,128)(2,1)} %do_ref.1, bf16[8,160,128]{2,1,0:T(8,128)(2,1)} %pack.1.local_ref, ...), custom_call_target="tpu_custom_call" | custom-call | tf_op jit(solution)/shard_map/attend/pallas_call | solution.py:260
  188.8 63.4 %all_to_all.17.ret_ref = bf16[16,8,160,128]{3,2,1,0:T(8,128)(2,1)} all-to-all(bf16[16,8,160,128]{3,2,1,0:T(8,128)(2,1)} %get-tuple-element.13), channel_id=1, replica_groups=mesh['z'=8,'y'=4,'x'=4,'grp'=2] {'y','x'}, dimensions={0} | all-to-all | bytes 10485760 | tf_op jit(solution)/shard_map/all_to_all | solution.py:319
  252.2 8.1 %sum_returned.1 = bf16[8,8,160,128]{3,2,1,0:T(8,128)(2,1)} custom-call(s32[16,8]{1,0:T(8,128)} %bitcast.7, bf16[16,8,160,128]{3,2,1,0:T(8,128)(2,1)} %all_to_all.17.ret_ref), custom_call_target="tpu_custom_call" | custom-call | tf_op jit(solution)/shard_map/sum_returned/pallas_call | solution.py:89
  260.3 0.0 reduce-scatter.2.cloned.1.call-update
  260.3 39.9 %reduce-scatter.2.cloned.1.call-done = bf16[1,8,160,128]{3,2,1,0:T(8,128)(2,1)} async-done(((bf16[8,8,160,128]{3,2,1,0:T(8,128)(2,1)}), bf16[1,8,160,128]{3,2,1,0:T(8,128)(2,1)}) %reduce-scatter.2.cloned.1.call-update) | async-done | bytes 327696 | tf_op jit(solution)/shard_map/reduce_scatter | solution.py:321
  300.2 2.0 finish.1
  302.2 1.8 copy.30
Async XLA Ops:
  7.2 49.0 %all-gather.3.cloned.1.call-start = ((), (), s32[]{:S(2)}) async-start(), calls=%async_computation.5 | async-start | bytes 2949120 | tf_op jit(solution)/shard_map/all_gather | solution.py:315
  10.8 289.4 %reduce-scatter.2.cloned.1.call-start = ((), (), s32[]{:S(2)}) async-start(), calls=%async_computation.4 | async-start | bytes 2949120 | tf_op jit(solution)/shard_map/reduce_scatter | solution.py:321
  11.6 118.7 %copy-start = (s32[8,16]{1,0:T(8,128)}, s32[8,16]{1,0:T(8,128)S(1)}, u32[]{:S(2)}) copy-start(s32[8,16]{1,0:T(8,128)S(1)} %get-tuple-element.33.src_ref) | copy-start | bytes 1540
Sparse Core Ops, SparseCore 0:
  10.9 45.2 all-gather.2
  260.5 39.7 reduce-scatter.1

commit v2 on v1

v2 whole, which is shorter than its diff:
```python
import functools

import jax
import jax.numpy as jnp
from jax import lax
from jax.experimental import pallas as pl
from jax.experimental.pallas import tpu as pltpu
from jax.sharding import Mesh, PartitionSpec as P

BLK = 64
SEL = 16
HEADS = 8
DK = 192
DV = 128
ROWS = 160
SIDES = (8, 4, 4)
LOCAL = 8
LOG2E = 1.4426950408889634
NEG = -1e30
BF = jnp.bfloat16
F32 = jnp.float32


def params(mib=56):
    return pltpu.CompilerParams(vmem_limit_bytes=mib * 1024 * 1024)


def pack_kernel(k_ref, v_ref, out_ref):
    for b in range(LOCAL):
        rows = slice(b * BLK, (b + 1) * BLK)
        k = k_ref[rows, :]
        out_ref[b, 0:BLK] = v_ref[rows, :]
        out_ref[b, BLK : 2 * BLK] = k[:, :128]
        low = k[:, 128:]
        out_ref[b, 2 * BLK :] = jnp.concatenate([low[:32], low[32:]], axis=1)


def pack(keys, values):
    return pl.pallas_call(
        pack_kernel,
        out_shape=jax.ShapeDtypeStruct((LOCAL, ROWS, 128), BF),
        compiler_params=params(),
        name="pack",
    )(keys, values)


def build_kernel(first, z_ref, req_ref, *refs):
    tables, out_ref = refs[:-1], refs[-1]
    c = pl.program_id(0)
    for d in range(out_ref.shape[1]):
        r = req_ref[c, first + d]

        @pl.when(r > 0)
        def _():
            if len(tables) > 1:
                out_ref[0, d] = tables[d][r - 1]
            else:
                out_ref[0, d] = tables[0][(z_ref[0] + d + 2) % tables[0].shape[0], r - 1]


def build(first, count, z, req, *tables):
    plane = req.shape[0]
    return pl.pallas_call(
        functools.partial(build_kernel, first),
        grid_spec=pltpu.PrefetchScalarGridSpec(
            num_scalar_prefetch=2,
            grid=(plane,),
            in_specs=[
                pl.BlockSpec(t.shape, functools.partial(lambda n, c, z, req: (0,) * n, t.ndim))
                for t in tables
            ],
            out_specs=pl.BlockSpec((1, count, ROWS, 128), lambda c, z, req: (c, 0, 0, 0)),
        ),
        out_shape=jax.ShapeDtypeStruct((plane, count, ROWS, 128), BF),
        compiler_params=params(),
        name="build",
    )(z, req, *tables)


def sum_block(first, d, req_ref, ret_ref, acc_ref):
    acc_ref[...] = jnp.zeros_like(acc_ref)
    for c in range(ret_ref.shape[0]):
        r = req_ref[c, first + d]

        @pl.when(r > 0)
        def _():
            acc_ref[r - 1] += ret_ref[c, 0].astype(F32)


def sum_near_kernel(z_ref, req_ref, ret_ref, out_ref, acc_ref):
    sum_block(0, pl.program_id(0), req_ref, ret_ref, acc_ref)
    out_ref[0] = acc_ref[...].astype(BF)


def sum_far_kernel(z_ref, req_ref, ret_ref, hold_ref, out_ref, held_ref, acc_ref):
    d = pl.program_id(0)
    far = d >= 3

    @pl.when(far)
    def _():
        sum_block(3, d - 3, req_ref, ret_ref, acc_ref)
        out_ref[0] = acc_ref[...].astype(BF)

    @pl.when(jnp.logical_not(far))
    def _():
        out_ref[0] = jnp.zeros_like(out_ref[0])


def far_step(depth, d):
    return jnp.where(d < 2, d, jnp.where(d == 2, depth - 1, d - 1))


def sum_near(z, req, returned):
    plane, count = returned.shape[:2]
    return pl.pallas_call(
        sum_near_kernel,
        grid_spec=pltpu.PrefetchScalarGridSpec(
            num_scalar_prefetch=2,
            grid=(count,),
            in_specs=[pl.BlockSpec((plane, 1, ROWS, 128), lambda d, z, req: (0, d, 0, 0))],
            out_specs=pl.BlockSpec((1, LOCAL, ROWS, 128), lambda d, z, req: (d, 0, 0, 0)),
            scratch_shapes=[pltpu.VMEM((LOCAL, ROWS, 128), F32)],
        ),
        out_shape=jax.ShapeDtypeStruct((count, LOCAL, ROWS, 128), BF),
        compiler_params=params(),
        name="sum_near",
    )(z, req, returned)


def sum_far(depth, z, req, returned, held):
    plane = returned.shape[0]
    return pl.pallas_call(
        sum_far_kernel,
        grid_spec=pltpu.PrefetchScalarGridSpec(
            num_scalar_prefetch=2,
            grid=(depth,),
            in_specs=[
                pl.BlockSpec(
                    (plane, 1, ROWS, 128), lambda d, z, req: (0, jnp.maximum(d - 3, 0), 0, 0)
                ),
                pl.BlockSpec(memory_space=pl.ANY),
            ],
            out_specs=[
                pl.BlockSpec(
                    (1, LOCAL, ROWS, 128),
                    lambda d, z, req: ((z[0] + far_step(depth, d)) % depth, 0, 0, 0),
                ),
                pl.BlockSpec(memory_space=pl.ANY),
            ],
            scratch_shapes=[pltpu.VMEM((LOCAL, ROWS, 128), F32)],
        ),
        out_shape=(
            jax.ShapeDtypeStruct((depth, LOCAL, ROWS, 128), BF),
            jax.ShapeDtypeStruct(held.shape, BF),
        ),
        input_output_aliases={3: 1},
        compiler_params=params(),
        name="sum_far",
    )(z, req, returned, held)


def finish_kernel(own_ref, *refs):
    got_refs, (dk_ref, dv_ref) = refs[:-2], refs[-2:]
    for b in range(LOCAL):
        rows = slice(b * BLK, (b + 1) * BLK)
        total = own_ref[b]
        for got_ref in got_refs:
            total = total + got_ref[b].astype(F32)
        dv_ref[rows, :] = total[0:BLK].astype(BF)
        low = total[2 * BLK :]
        low = jnp.concatenate([low[:, :64], low[:, 64:]], axis=0)
        dk_ref[rows, :] = jnp.concatenate([total[BLK : 2 * BLK], low], axis=1).astype(BF)


def finish(own, *got):
    return pl.pallas_call(
        finish_kernel,
        out_shape=(
            jax.ShapeDtypeStruct((LOCAL * BLK, DK), BF),
            jax.ShapeDtypeStruct((LOCAL * BLK, DV), BF),
        ),
        compiler_params=params(),
        name="finish",
    )(own, *got)


def dot(a, b, da, db):
    return lax.dot_general(a, b, (((da,), (db,)), ((), ())), preferred_element_type=F32)


def swap(x):
    return jnp.concatenate([x[:, 64:], x[:, :64]], axis=1)


def attend_kernel(
    src_ref,
    q_ref,
    do_ref,
    local_hbm,
    near_hbm,
    far_hbm,
    att_ref,
    dq_ref,
    part_near_hbm,
    part_far_hbm,
    own_ref,
    table,
    part,
    k_buf,
    v_buf,
    q_buf,
    do_buf,
    p_buf,
    pb_buf,
    dk_buf,
    dv_buf,
    sems,
):
    b = pl.program_id(0)
    n_near, n_far = near_hbm.shape[0], far_hbm.shape[0]
    n_remote = n_near + n_far
    scale = DK**-0.5
    half = BLK // 2
    group = SEL * half
    left = lax.broadcasted_iota(jnp.int32, (half, 128), 1) < 64

    @pl.when(b == 0)
    def _():
        places = ((near_hbm, 0, n_near), (far_hbm, n_near, n_far), (local_hbm, n_remote, LOCAL))
        copies = [
            pltpu.make_async_copy(ref, table.at[pl.ds(at, n)], sems.at[i])
            for i, (ref, at, n) in enumerate(places)
        ]
        for copy in copies:
            copy.start()
        own_ref[...] = jnp.zeros_like(own_ref)
        v_buf[:, 128:] = jnp.ones((2 * group, 128), BF)
        for copy in copies:
            copy.wait()

    key_id = lax.broadcasted_iota(jnp.int32, (half, 128), 0)
    query_id = lax.broadcasted_iota(jnp.int32, (half, 128), 1) % BLK
    none = jnp.zeros((half, 128), BF)
    masks = [
        jnp.where(key_id + g * half > query_id, NEG, 0.0).astype(BF) for g in range(2)
    ]
    for e in range(SEL):
        s = src_ref[b, e]
        mine = s == n_remote + b
        low = table[s, 2 * BLK :]
        for g in range(2):
            at = g * group + e * half
            rows = slice(at, at + half)
            v_buf[rows, 0:128] = table[s, g * half : (g + 1) * half]
            k_buf[rows, 0:128] = table[s, BLK + g * half : BLK + (g + 1) * half]
            mask = jnp.where(mine, masks[g], none)
            k_buf[rows, 128:] = jnp.where(left, low, mask) if g == 0 else jnp.where(left, mask, low)

    lane = lax.broadcasted_iota(jnp.int32, (BLK, 128), 1)
    first = lane < 64
    one_hot = (lax.broadcasted_iota(jnp.int32, (BLK, 128), 0) == lane % BLK).astype(BF)
    for h in range(0, HEADS, 2):
        t0, t1, t2 = (q_ref[:, h * DK + i * 128 : h * DK + (i + 1) * 128] for i in range(3))
        r1, r2 = swap(t1), swap(t2)
        for k, (high, low, swapped) in enumerate(((t0, t1, r1), (jnp.where(first, r1, r2), r2, t2))):
            rows = slice((h + k) * BLK, (h + k + 1) * BLK)
            for g in range(2):
                q_buf[g, rows, 0:128] = high
            q_buf[0, rows, 128:] = jnp.where(first, low, one_hot)
            q_buf[1, rows, 128:] = jnp.where(first, one_hot, swapped)

    groups = [slice(0, group), slice(group, 2 * group)]
    top = None
    for g in range(2):
        s = dot(k_buf[groups[g], :], q_buf[g], 1, 1)
        p_buf[groups[g], :] = s
        m = jnp.max(s, axis=0, keepdims=True)
        top = m if top is None else jnp.maximum(top, m)
    out_t = None
    for g in range(2):
        p = jnp.exp2((p_buf[groups[g], :] - top) * (scale * LOG2E))
        p_buf[groups[g], :] = p
        pb = p.astype(BF)
        pb_buf[groups[g], :] = pb
        o = dot(v_buf[groups[g], :], pb, 0, 0)
        out_t = o if out_t is None else out_t + o
    out = jnp.transpose(out_t)
    inverse = 1.0 / out[:, 128:129]
    att = (out[:, :128] * inverse).astype(BF)
    for h in range(HEADS):
        rows = slice(h * BLK, (h + 1) * BLK)
        att_ref[:, h * DV : (h + 1) * DV] = att[rows]
        do = (do_ref[:, h * DV : (h + 1) * DV].astype(F32) * inverse[rows]).astype(BF)
        delta = jnp.sum(do.astype(F32) * att[rows].astype(F32), axis=1, keepdims=True)
        high = delta.astype(BF)
        rest = delta - high.astype(F32)
        mid = rest.astype(BF)
        last = (rest - mid.astype(F32)).astype(BF)
        extra = jnp.where(
            lane == 0,
            high.astype(F32),
            jnp.where(lane == 1, mid.astype(F32), jnp.where(lane == 2, last.astype(F32), 0.0)),
        )
        do_buf[rows, 0:128] = do
        do_buf[rows, 128:] = (-extra).astype(BF)
    do_all = do_buf[...]
    dq_t = []
    for g in range(2):
        dp = dot(v_buf[groups[g], :], do_all, 1, 1)
        ds = (p_buf[groups[g], :] * dp).astype(BF)
        dv_buf[groups[g], :] = dot(pb_buf[groups[g], :], do_buf[:, 0:128], 1, 0)
        dk_buf[groups[g], :] = dot(ds, q_buf[g], 1, 0) * scale
        dq_t.append(dot(k_buf[groups[g], :], ds, 0, 0))
    for e in range(SEL):
        s = src_ref[b, e]
        at = jnp.minimum(s, n_remote)
        r1 = slice(e * half, (e + 1) * half)
        r2 = slice(group + e * half, group + (e + 1) * half)
        part[at, 0:half] = dv_buf[r1, :].astype(BF)
        part[at, half:BLK] = dv_buf[r2, :].astype(BF)
        part[at, BLK : BLK + half] = dk_buf[r1, 0:128].astype(BF)
        part[at, BLK + half : 2 * BLK] = dk_buf[r2, 0:128].astype(BF)
        part[at, 2 * BLK :] = jnp.where(left, dk_buf[r1, 128:], dk_buf[r2, 128:]).astype(BF)
    for e in range(SEL):
        s = src_ref[b, e]
        r1 = slice(e * half, (e + 1) * half)
        r2 = slice(group + e * half, group + (e + 1) * half)

        @pl.when(s >= n_remote)
        def _():
            i = s - n_remote
            own_ref[i, 0:half] += dv_buf[r1, :]
            own_ref[i, half:BLK] += dv_buf[r2, :]
            own_ref[i, BLK : BLK + half] += dk_buf[r1, 0:128]
            own_ref[i, BLK + half : 2 * BLK] += dk_buf[r2, 0:128]
            own_ref[i, 2 * BLK :] += jnp.where(left, dk_buf[r1, 128:], dk_buf[r2, 128:])

    high = jnp.transpose(dq_t[0][:128] + dq_t[1][:128]) * scale
    low = dq_t[0][128:192] + dq_t[1][192:]
    low = jnp.transpose(jnp.concatenate([low, low], axis=0)) * scale
    for h in range(0, HEADS, 2):
        even, odd = slice(h * BLK, (h + 1) * BLK), slice((h + 1) * BLK, (h + 2) * BLK)
        turned = swap(high[odd])
        parts = (high[even], jnp.where(first, low[even], turned), jnp.where(first, turned, low[odd]))
        for i, x in enumerate(parts):
            dq_ref[:, h * DK + i * 128 : h * DK + (i + 1) * 128] = x.astype(BF)

    @pl.when(b == LOCAL - 1)
    def _():
        places = ((part_near_hbm, 0, n_near), (part_far_hbm, n_near, n_far))
        copies = [
            pltpu.make_async_copy(part.at[pl.ds(at, n)], ref, sems.at[i])
            for i, (ref, at, n) in enumerate(places)
        ]
        for copy in copies:
            copy.start()
        for copy in copies:
            copy.wait()


def attend(src, queries, d_out, local, near, far):
    tokens = LOCAL * BLK
    keys = SEL * BLK
    rows = HEADS * BLK
    n_near, n_far = (x.shape[0] * x.shape[1] for x in (near, far))
    anywhere = pl.BlockSpec(memory_space=pl.ANY)
    attended, d_queries, part_near, part_far, own = pl.pallas_call(
        attend_kernel,
        grid_spec=pltpu.PrefetchScalarGridSpec(
            num_scalar_prefetch=1,
            grid=(LOCAL,),
            in_specs=[
                pl.BlockSpec((BLK, HEADS * DK), lambda b, src: (b, 0)),
                pl.BlockSpec((BLK, HEADS * DV), lambda b, src: (b, 0)),
                anywhere,
                anywhere,
                anywhere,
            ],
            out_specs=[
                pl.BlockSpec((BLK, HEADS * DV), lambda b, src: (b, 0)),
                pl.BlockSpec((BLK, HEADS * DK), lambda b, src: (b, 0)),
                anywhere,
                anywhere,
                pl.BlockSpec((LOCAL, ROWS, 128), lambda b, src: (0, 0, 0)),
            ],
            scratch_shapes=[
                pltpu.VMEM((n_near + n_far + LOCAL, ROWS, 128), BF),
                pltpu.VMEM((n_near + n_far + 1, ROWS, 128), BF),
                pltpu.VMEM((keys, 256), BF),
                pltpu.VMEM((keys, 256), BF),
                pltpu.VMEM((2, rows, 256), BF),
                pltpu.VMEM((rows, 256), BF),
                pltpu.VMEM((keys, rows), F32),
                pltpu.VMEM((keys, rows), BF),
                pltpu.VMEM((keys, 256), F32),
                pltpu.VMEM((keys, 128), F32),
                pltpu.SemaphoreType.DMA((3,)),
            ],
        ),
        out_shape=(
            jax.ShapeDtypeStruct((tokens, HEADS * DV), BF),
            jax.ShapeDtypeStruct((tokens, HEADS * DK), BF),
            jax.ShapeDtypeStruct((n_near, ROWS, 128), BF),
            jax.ShapeDtypeStruct((n_far, ROWS, 128), BF),
            jax.ShapeDtypeStruct((LOCAL, ROWS, 128), F32),
        ),
        compiler_params=params(),
        name="attend",
    )(
        src,
        queries,
        d_out,
        local,
        near.reshape(n_near, ROWS, 128),
        far.reshape(n_far, ROWS, 128),
    )
    return attended, d_queries, part_near.reshape(near.shape), part_far.reshape(far.shape), own


def shards(depth, plane, queries, keys, values, selected, d_out):
    me = lax.axis_index(("z", "y", "x"))
    z = lax.axis_index("z")
    seq_count = depth * plane
    per_half = LOCAL // 2
    half_index = selected // per_half
    is_late = half_index >= seq_count
    owners = jnp.where(is_late, 2 * seq_count - 1 - half_index, half_index)
    inner = selected % per_half + jnp.where(is_late, per_half, 0)
    remote = owners != me
    offset = (owners // plane - z + depth) % depth
    order = jnp.where(offset < 2, offset, jnp.where(offset == depth - 1, 2, offset + 1))
    in_plane = owners % plane
    slots = jnp.where(
        order < 3, in_plane * 3 + order, 3 * plane + in_plane * (depth - 3) + order - 3
    )
    src = jnp.where(remote, slots, seq_count + inner).astype(jnp.int32)
    flat = jnp.where(remote, in_plane * depth + order, -1).reshape(-1)
    hits = flat[:, None] == jnp.arange(seq_count, dtype=jnp.int32)[None, :]
    wanted = jnp.max(jnp.where(hits, inner.reshape(-1)[:, None] + 1, 0), axis=0)
    exchange = functools.partial(
        lax.all_to_all, axis_name=("y", "x"), split_axis=0, concat_axis=0, tiled=True
    )
    up = [(i, (i + 1) % depth) for i in range(depth)]
    down = [(i, (i - 1) % depth) for i in range(depth)]
    where_z = z.reshape(1).astype(jnp.int32)

    local = pack(keys, values)
    above = lax.ppermute(local, "z", down)
    below = lax.ppermute(local, "z", up)
    asked = exchange(wanted.reshape(plane, 1, depth)).reshape(plane, depth)
    column = lax.all_gather(local, "z")
    near = exchange(build(0, 3, where_z, asked, local, above, below))
    far = exchange(build(3, depth - 3, where_z, asked, column))
    attended, d_queries, part_near, part_far, own = attend(src, queries, d_out, local, near, far)
    back_far = exchange(part_far)
    far_sums, part_near = sum_far(depth, where_z, asked, back_far, part_near)
    mine = lax.psum_scatter(far_sums, "z", scatter_dimension=0)
    near_sums = sum_near(where_z, asked, exchange(part_near))
    from_below = lax.ppermute(near_sums[1], "z", up)
    from_above = lax.ppermute(near_sums[2], "z", down)
    d_keys, d_values = finish(own, near_sums[0], from_below, from_above, mine)
    return attended, d_queries, d_keys, d_values


def solution(mesh):
    grid = Mesh(mesh.devices.reshape(SIDES + (-1,)), ("z", "y", "x", "grp"))
    spec = P(("z", "y", "x"), "grp")
    return jax.shard_map(
        functools.partial(shards, SIDES[0], SIDES[1] * SIDES[2]),
        mesh=grid,
        in_specs=(spec,) * 5,
        out_specs=(spec,) * 4,
        check_vma=False,
    )
```

time: 312 us -> 258 us (0.83)
  waiting for transfers between devices: 70.7 us -> 22.6 us
  Pallas kernels: 79.3 us -> 65 us
  starting transfers between devices: 0.08 us -> 13.1 us
  blocking collectives: 142 us -> 132 us
  local copies, waits for them, and re-layouts: 3.77 us -> 8.78 us
    reduce_scatter x1, waiting for transfers between devices: 39.9 us -> 0.01 us  [shards(): mine = lax.psum_scatter(far_sums, 'z', scatter_dimension=0)]
    pallas_call x1, Pallas kernels: 58.5 us -> 33.8 us  [attend(): pl.pallas_call(attend_kernel, grid_spec=pltpu.PrefetchScalarGridSpec(num_...]
    all_gather x1, waiting for transfers between devices: 30.8 us -> 11.1 us  [shards(): column = lax.all_gather(local, 'z')]
    all_to_all x3 -> x4, blocking collectives: 142 us -> 132 us  [the longest x1 47.6 us: shards(): far = exchange(build(3, depth - 3, where_z, asked, column))]
    pallas_call x2 -> x4, Pallas kernels: 17 us -> 27.1 us  [the longest x2 15.5 us: build(): pl.pallas_call(functools.partial(build_kernel, first), grid_spec=pltpu.Pr...]
    ppermute x0 -> x4, starting transfers between devices: none -> 8.05 us  [the longest x1 4.03 us: shards(): above = lax.ppermute(local, 'z', down)]
    ppermute x0 -> x4, waiting for transfers between devices: none -> 6.26 us  [the longest x1 5.48 us: shards(): from_above = lax.ppermute(near_sums[2], 'z', down)]
    all_to_all x0 -> x1, waiting for transfers between devices: none -> 5.24 us  [shards(): near = exchange(build(0, 3, where_z, asked, local, above, below))]
  transfers between devices with their start and end apart: 2 -> 7, of which waited for: 2 -> 4; matrix products, arithmetic and copies ran while one was open for 0% -> 1% of each run, Pallas kernels for 0% -> 8%
where the time goes in v2:
time: 258 us; the launch traced here: 257 us
  blocking collectives  132 us (51%)
  Pallas kernels  65 us (25%)
  waiting for transfers between devices  22.6 us (9%)
  between operations  14.1 us (5%)
  starting transfers between devices  13.1 us (5%)
  local copies, waits for them, and re-layouts  8.78 us (3%)
    all_to_all x1, blocking collectives, shards(): far = exchange(build(3, depth - 3, where_z, asked, column))  47.6 us
    all_to_all x1, blocking collectives, shards(): back_far = exchange(part_far)  43 us
    pallas_call x1, Pallas kernels, attend(): pl.pallas_call(attend_kernel, grid_spec=pltpu.PrefetchScalarGridSpec(num_...  33.8 us
    all_to_all x1, blocking collectives, shards(): near_sums = sum_near(where_z, asked, exchange(part_near))  27.6 us
    pallas_call x2, Pallas kernels, build(): pl.pallas_call(functools.partial(build_kernel, first), grid_spec=pltpu.Pr...  15.5 us
    all_to_all x1, blocking collectives, shards(): asked = exchange(wanted.reshape(plane, 1, depth)).reshape(plane, depth)  13.4 us
    all_gather x1, waiting for transfers between devices, shards(): column = lax.all_gather(local, 'z')  11.1 us
    pallas_call x1, Pallas kernels, sum_far(): pl.pallas_call(sum_far_kernel, grid_spec=pltpu.PrefetchScalarGridSpec(num...  7.12 us
  transfers between devices with their start and end apart: 7, of which 4 were waited for; matrix products, arithmetic and copies ran while one was open for 1% of the time, Pallas kernels for 8%

profile of v2, /device:TPU:2, one launch (start us, length us, event | category | flops | bytes accessed | tf_op | source)
XLA Modules:
  0.0 256.7 jit_solution(13795153188411054424)
XLA Ops:
  7.2 0.0 all-gather.3.cloned.1.call-start
  7.2 1.8 copy.32.k_ref
  9.0 1.8 pack.1.refs_0_.local_hbm
  10.8 0.0 all-gather.3.cloned.1.call-update
  10.8 2.0 collective-permute-start.1
  12.8 4.0 %collective-permute-start = (bf16[8,160,128]{2,1,0:T(8,128)(2,1)}, bf16[8,160,128]{2,1,0:T(8,128)(2,1)S(1)}, u32[]{:S(2)}, u32[]{:S(2)}) collective-permute-start(bf16[8,160,128]{2,1,0:T(8,128)(2,1)} %pack.1.refs_0_.local_hbm), channel_id=1, source_target_pairs={{0,224},{32,0},{64,32},{96,64},{128,96},{160,128},{192,160},{224,1... | collective-permute-start | bytes 983048 | tf_op jit(solution)/shard_map/ppermute | solution.py:448
  16.8 1.3 add_select_fusion.5
  18.1 0.1 eq.24
  18.2 0.1 add.80
  18.3 0.1 select_reduce_fusion
  18.4 0.1 reshape.40
  18.5 13.4 %all_to_all.25 = s32[16,1,8]{2,1,0:T(1,128)} all-to-all(s32[16,1,8]{2,1,0:T(1,128)S(1)} %bitcast.25), channel_id=1, replica_groups=mesh['z'=8,'y'=4,'x'=4,'grp'=2] {'y','x'}, dimensions={0} | all-to-all | bytes 1024 | tf_op jit(solution)/shard_map/all_to_all | solution.py:450
  31.9 0.0 collective-permute-done.1.refs_2_
  31.9 0.0 copy-start.2
  31.9 0.0 collective-permute-done.refs_1_
  31.9 0.0 copy-start.3
  31.9 0.7 copy-done.2
  32.6 0.1 copy-done.3
  32.7 7.3 %build.2 = bf16[16,3,160,128]{3,2,1,0:T(8,128)(2,1)} custom-call(s32[1]{0:T(128)} %bitcast.z_ref, s32[16,8]{1,0:T(8,128)} %bitcast.21, bf16[8,160,128]{2,1,0:T(8,128)(2,1)} %pack.1.refs_0_.local_hbm, bf16[8,160,128]{2,1,0:T(8,128)(2,1)} %copy-done.3, bf16[8,160,128]{2,1,0:T(8,128)(2,1)} %copy-done.2), custom_call_target="tpu_custom_call" | custom-call | tf_op jit(solution)/shard_map/build/pallas_call | solution.py:63
  40.1 5.0 %all-to-all-start.1 = ((bf16[16,3,160,128]{3,2,1,0:T(8,128)(2,1)}), bf16[16,3,160,128]{3,2,1,0:T(8,128)(2,1)S(1)}, u32[]{:S(2)}, u32[]{:S(2)}) async-start(bf16[16,3,160,128]{3,2,1,0:T(8,128)(2,1)} %build.2), calls=%async_computation.1 | async-start | bytes 3932160 | tf_op jit(solution)/shard_map/all_to_all | solution.py:452
  45.0 0.0 reduce-scatter.2.cloned.1.call-start
  45.1 11.1 %all-gather.3.cloned.1.call-done = bf16[64,160,128]{2,1,0:T(8,128)(2,1)} async-done(((bf16[8,160,128]{2,1,0:T(8,128)(2,1)}), bf16[64,160,128]{2,1,0:T(8,128)(2,1)}) %all-gather.3.cloned.1.call-update) | async-done | bytes 2621456 | tf_op jit(solution)/shard_map/all_gather | solution.py:451
  56.2 8.2 %build.3 = bf16[16,5,160,128]{3,2,1,0:T(8,128)(2,1)} custom-call(s32[1]{0:T(128)} %bitcast.z_ref, s32[16,8]{1,0:T(8,128)} %bitcast.22, bf16[8,8,160,128]{3,2,1,0:T(8,128)(2,1)} %bitcast.19), custom_call_target="tpu_custom_call" | custom-call | tf_op jit(solution)/shard_map/build/pallas_call | solution.py:63
  64.3 5.2 %all-to-all-done.1 = bf16[16,3,160,128]{3,2,1,0:T(8,128)(2,1)S(1)} async-done(((bf16[16,3,160,128]{3,2,1,0:T(8,128)(2,1)}), bf16[16,3,160,128]{3,2,1,0:T(8,128)(2,1)S(1)}, u32[]{:S(2)}, u32[]{:S(2)}) %all-to-all-start.1) | async-done | bytes 1966112 | tf_op jit(solution)/shard_map/all_to_all | solution.py:452
  69.6 0.0 copy-start
  69.6 47.6 %all_to_all.26 = bf16[16,5,160,128]{3,2,1,0:T(8,128)(2,1)} all-to-all(bf16[16,5,160,128]{3,2,1,0:T(8,128)(2,1)} %build.3), channel_id=1, replica_groups=mesh['z'=8,'y'=4,'x'=4,'grp'=2] {'y','x'}, dimensions={0} | all-to-all | bytes 6553600 | tf_op jit(solution)/shard_map/all_to_all | solution.py:453
  117.2 0.0 copy-done
  117.2 33.8 %attend.1 = (bf16[512,1024]{1,0:T(8,128)(2,1)}, bf16[512,1536]{1,0:T(8,128)(2,1)}, bf16[48,160,128]{2,1,0:T(8,128)(2,1)}, bf16[80,160,128]{2,1,0:T(8,128)(2,1)}, f32[8,160,128]{2,1,0:T(8,128)}) custom-call(s32[8,16]{1,0:T(8,128)} %get-tuple-element.43.src_ref, bf16[512,1536]{1,0:T(8,128)(2,1)} %q_ref.1, bf16[512,1024]{1,0:T(8,128)(2,1)} %do_ref.1, ...), custom_call_target="tpu_custom_call" | custom-call | tf_op jit(solution)/shard_map/attend/pallas_call | solution.py:367
  151.0 43.0 %all_to_all.27.ret_ref = bf16[16,5,160,128]{3,2,1,0:T(8,128)(2,1)} all-to-all(bf16[16,5,160,128]{3,2,1,0:T(8,128)(2,1)} %bitcast.18), channel_id=1, replica_groups=mesh['z'=8,'y'=4,'x'=4,'grp'=2] {'y','x'}, dimensions={0} | all-to-all | bytes 6553600 | tf_op jit(solution)/shard_map/all_to_all | solution.py:455
  194.0 7.1 %sum_far.1 = (bf16[8,8,160,128]{3,2,1,0:T(8,128)(2,1)}, bf16[16,3,160,128]{3,2,1,0:T(8,128)(2,1)}) custom-call(s32[1]{0:T(128)} %bitcast.z_ref, s32[16,8]{1,0:T(8,128)} %bitcast.23, bf16[16,5,160,128]{3,2,1,0:T(8,128)(2,1)} %all_to_all.27.ret_ref, bf16[16,3,160,128]{3,2,1,0:T(8,128)(2,1)} %bitcast.17), custom_call_target="tpu_custom_call", output_to_operand_aliasing={{1}: (3, {})} | custom-call | tf_op jit(solution)/shard_map/sum_far/pallas_call | solution.py:132
  201.2 0.0 copy-start.1
  201.2 0.0 reduce-scatter.2.cloned.1.call-update
  201.2 1.5 copy-done.1
  202.7 27.6 %all_to_all.28.ret_ref = bf16[16,3,160,128]{3,2,1,0:T(8,128)(2,1)} all-to-all(bf16[16,3,160,128]{3,2,1,0:T(8,128)(2,1)S(1)} %copy-done.1), channel_id=1, replica_groups=mesh['z'=8,'y'=4,'x'=4,'grp'=2] {'y','x'}, dimensions={0} | all-to-all | bytes 3932160 | tf_op jit(solution)/shard_map/all_to_all | solution.py:458
  230.3 4.5 %sum_near.1 = bf16[3,8,160,128]{3,2,1,0:T(8,128)(2,1)} custom-call(s32[1]{0:T(128)} %bitcast.z_ref, s32[16,8]{1,0:T(8,128)} %bitcast.24, bf16[16,3,160,128]{3,2,1,0:T(8,128)(2,1)} %all_to_all.28.ret_ref), custom_call_target="tpu_custom_call" | custom-call | tf_op jit(solution)/shard_map/sum_near/pallas_call | solution.py:115
  234.8 2.0 slice_bitcast_fusion
  236.7 0.0 collective-permute-start.3
  236.7 2.0 collective-permute-start.2
  238.8 5.5 %collective-permute-done.3.refs_2_ = bf16[8,160,128]{2,1,0:T(8,128)(2,1)S(1)} collective-permute-done((bf16[8,160,128]{2,1,0:T(8,128)(2,1)S(1)}, bf16[8,160,128]{2,1,0:T(8,128)(2,1)S(1)}, u32[]{:S(2)}, u32[]{:S(2)}) %collective-permute-start.3) | collective-permute-done | bytes 327712 | tf_op jit(solution)/shard_map/ppermute | solution.py:460
  244.2 0.0 copy-start.4
  244.2 0.8 collective-permute-done.2.refs_1_
  245.0 0.0 copy-start.5
  245.0 0.0 reduce-scatter.2.cloned.1.call-done
  245.0 0.0 copy-done.4
  245.0 0.7 copy-done.5
  245.8 2.4 finish.1
  248.1 1.8 copy.39
Async XLA Ops:
  7.2 49.0 %all-gather.3.cloned.1.call-start = ((), (), s32[]{:S(2)}) async-start(), calls=%async_computation.7 | async-start | bytes 2949120 | tf_op jit(solution)/shard_map/all_gather | solution.py:451
  10.8 21.1 %collective-permute-start.1 = (bf16[8,160,128]{2,1,0:T(8,128)(2,1)}, bf16[8,160,128]{2,1,0:T(8,128)(2,1)S(1)}, u32[]{:S(2)}, u32[]{:S(2)}) collective-permute-start(bf16[8,160,128]{2,1,0:T(8,128)(2,1)} %pack.1.refs_0_.local_hbm), channel_id=1, source_target_pairs={{0,32},{32,64},{64,96},{96,128},{128,160},{160,192},{192,224},{224... | collective-permute-start | bytes 983048 | tf_op jit(solution)/shard_map/ppermute | solution.py:449
  12.8 19.1 %collective-permute-start = (bf16[8,160,128]{2,1,0:T(8,128)(2,1)}, bf16[8,160,128]{2,1,0:T(8,128)(2,1)S(1)}, u32[]{:S(2)}, u32[]{:S(2)}) collective-permute-start(bf16[8,160,128]{2,1,0:T(8,128)(2,1)} %pack.1.refs_0_.local_hbm), channel_id=1, source_target_pairs={{0,224},{32,0},{64,32},{96,64},{128,96},{160,128},{192,160},{224,1... | collective-permute-start | bytes 983048 | tf_op jit(solution)/shard_map/ppermute | solution.py:448
  31.9 0.7 copy-start.2
  31.9 0.8 copy-start.3
  40.1 29.5 %all-to-all-start.1 = ((bf16[16,3,160,128]{3,2,1,0:T(8,128)(2,1)}), bf16[16,3,160,128]{3,2,1,0:T(8,128)(2,1)S(1)}, u32[]{:S(2)}, u32[]{:S(2)}) async-start(bf16[16,3,160,128]{3,2,1,0:T(8,128)(2,1)} %build.2), calls=%async_computation.1 | async-start | bytes 3932160 | tf_op jit(solution)/shard_map/all_to_all | solution.py:452
  45.0 200.0 %reduce-scatter.2.cloned.1.call-start = ((), (), s32[]{:S(2)}) async-start(), calls=%async_computation.6 | async-start | bytes 2949120 | tf_op jit(solution)/shard_map/reduce_scatter | solution.py:457
  69.6 47.6 %copy-start = (bf16[16,3,160,128]{3,2,1,0:T(8,128)(2,1)}, bf16[16,3,160,128]{3,2,1,0:T(8,128)(2,1)S(1)}, u32[]{:S(2)}) copy-start(bf16[16,3,160,128]{3,2,1,0:T(8,128)(2,1)S(1)} %all-to-all-done.1) | copy-start | bytes 5898244
  201.2 1.5 copy-start.1
  236.7 7.5 %collective-permute-start.3 = (bf16[8,160,128]{2,1,0:T(8,128)(2,1)S(1)}, bf16[8,160,128]{2,1,0:T(8,128)(2,1)S(1)}, u32[]{:S(2)}, u32[]{:S(2)}) collective-permute-start(bf16[8,160,128]{2,1,0:T(8,128)(2,1)S(1)} %get-tuple-element.38), channel_id=1, source_target_pairs={{0,224},{32,0},{64,32},{96,64},{128,96},{160,128},{192,160},{224,1... | collective-permute-start | bytes 983048 | tf_op jit(solution)/shard_map/ppermute | solution.py:460
  236.7 8.3 %collective-permute-start.2 = (bf16[8,160,128]{2,1,0:T(8,128)(2,1)S(1)}, bf16[8,160,128]{2,1,0:T(8,128)(2,1)S(1)}, u32[]{:S(2)}, u32[]{:S(2)}) collective-permute-start(bf16[8,160,128]{2,1,0:T(8,128)(2,1)S(1)} %get-tuple-element.39), channel_id=1, source_target_pairs={{0,32},{32,64},{64,96},{96,128},{128,160},{160,192},{192,224},{224... | collective-permute-start | bytes 983048 | tf_op jit(solution)/shard_map/ppermute | solution.py:459
  244.2 0.8 copy-start.4
  245.0 0.7 copy-start.5
Sparse Core Ops, SparseCore 0:
  10.9 45.2 all-gather.2
  201.3 40.2 reduce-scatter.1

commit v3 on v2

v3 whole, which is shorter than its diff:
```python
import functools

import jax
import jax.numpy as jnp
from jax import lax
from jax.experimental import pallas as pl
from jax.experimental.pallas import tpu as pltpu
from jax.sharding import Mesh, PartitionSpec as P

BLK = 64
SEL = 16
HEADS = 8
DK = 192
DV = 128
ROWS = 160
SIDES = (8, 4, 4)
LOCAL = 8
LOG2E = 1.4426950408889634
NEG = -1e30
BF = jnp.bfloat16
F32 = jnp.float32


def params(mib=56):
    return pltpu.CompilerParams(vmem_limit_bytes=mib * 1024 * 1024)


def pack_kernel(k_ref, v_ref, out_ref):
    for b in range(0, LOCAL, 2):
        pair = jnp.transpose(k_ref[:, b * BLK : (b + 2) * BLK])
        for i in range(2):
            k = pair[i * BLK : (i + 1) * BLK]
            out_ref[b + i, 0:BLK] = v_ref[(b + i) * BLK : (b + i + 1) * BLK, :]
            out_ref[b + i, BLK : 2 * BLK] = k[:, :128]
            low = k[:, 128:]
            out_ref[b + i, 2 * BLK :] = jnp.concatenate([low[:32], low[32:]], axis=1)


def pack(keys_t, values):
    return pl.pallas_call(
        pack_kernel,
        out_shape=jax.ShapeDtypeStruct((LOCAL, ROWS, 128), BF),
        compiler_params=params(),
        name="pack",
    )(keys_t, values)


def build_kernel(first, z_ref, req_ref, *refs):
    tables, out_hbm = refs[: (len(refs) - 3) // 2], refs[(len(refs) - 3) // 2]
    held, (load_sems, sems) = refs[-2 - len(tables) : -2], refs[-2:]
    plane, count = out_hbm.shape[:2]
    loads = [
        pltpu.make_async_copy(t, h, load_sems.at[i]) for i, (t, h) in enumerate(zip(tables, held))
    ]
    for load in loads:
        load.start()
    sends = []
    for d in range(count):
        if d < len(loads):
            loads[d].wait()
        for c in range(plane):
            r = jnp.maximum(req_ref[c, first + d], 1) - 1
            if len(held) > 1:
                block = held[d].at[r]
            else:
                block = held[0].at[(z_ref[0] + d + 2) % held[0].shape[0], r]
            sends.append(pltpu.make_async_copy(block, out_hbm.at[c, d], sems.at[c, d]))
            sends[-1].start()
    for send in sends:
        send.wait()


def build(first, count, z, req, *tables):
    plane = req.shape[0]
    anywhere = pl.BlockSpec(memory_space=pl.ANY)
    return pl.pallas_call(
        functools.partial(build_kernel, first),
        grid_spec=pltpu.PrefetchScalarGridSpec(
            num_scalar_prefetch=2,
            grid=(1,),
            in_specs=[anywhere] * len(tables),
            out_specs=anywhere,
            scratch_shapes=[pltpu.VMEM(t.shape, BF) for t in tables]
            + [pltpu.SemaphoreType.DMA((len(tables),)), pltpu.SemaphoreType.DMA((plane, count))],
        ),
        out_shape=jax.ShapeDtypeStruct((plane, count, ROWS, 128), BF),
        compiler_params=params(),
        name="build",
    )(z, req, *tables)


def sum_blocks(first, req_ref, ret_hbm, buf, acc, staged, in_sems, out_sems, target):
    plane, count = ret_hbm.shape[:2]
    loads = [
        pltpu.make_async_copy(ret_hbm.at[:, d], buf.at[d], in_sems.at[d]) for d in range(count)
    ]
    for load in loads:
        load.start()
    stores = []
    for d in range(count):
        loads[d].wait()
        acc[...] = jnp.zeros_like(acc)
        for c in range(plane):
            acc[req_ref[c, first + d]] += buf[d, c].astype(F32)
        staged[d] = acc[1:].astype(BF)
        stores.append(pltpu.make_async_copy(staged.at[d], target(d), out_sems.at[d]))
        stores[-1].start()
    return stores


def sum_near_kernel(req_ref, ret_hbm, *refs):
    outs, (buf, acc, staged, in_sems, out_sems) = refs[:-5], refs[-5:]
    for store in sum_blocks(
        0, req_ref, ret_hbm, buf, acc, staged, in_sems, out_sems, lambda d: outs[d]
    ):
        store.wait()


def sum_far_kernel(
    z_ref, req_ref, ret_hbm, hold_ref, out_hbm, held_ref, buf, acc, staged, in_sems, out_sems
):
    depth, count = out_hbm.shape[0], ret_hbm.shape[1]
    near = depth - count
    z = z_ref[0]
    staged[count] = jnp.zeros_like(staged[count])
    zeros = [
        pltpu.make_async_copy(
            staged.at[count], out_hbm.at[(z + depth + i - 1) % depth], out_sems.at[count + i]
        )
        for i in range(near)
    ]
    for zero in zeros:
        zero.start()
    for store in zeros + sum_blocks(
        near,
        req_ref,
        ret_hbm,
        buf,
        acc,
        staged,
        in_sems,
        out_sems,
        lambda d: out_hbm.at[(z + d + 2) % depth],
    ):
        store.wait()


def sum_scratch(plane, count, depth):
    return [
        pltpu.VMEM((count, plane, ROWS, 128), BF),
        pltpu.VMEM((LOCAL + 1, ROWS, 128), F32),
        pltpu.VMEM((count + 1, LOCAL, ROWS, 128), BF),
        pltpu.SemaphoreType.DMA((count,)),
        pltpu.SemaphoreType.DMA((depth,)),
    ]


def sum_near(req, returned):
    plane, count = returned.shape[:2]
    anywhere = pl.BlockSpec(memory_space=pl.ANY)
    return pl.pallas_call(
        sum_near_kernel,
        grid_spec=pltpu.PrefetchScalarGridSpec(
            num_scalar_prefetch=1,
            grid=(1,),
            in_specs=[anywhere],
            out_specs=[anywhere] * count,
            scratch_shapes=sum_scratch(plane, count, count),
        ),
        out_shape=[jax.ShapeDtypeStruct((LOCAL, ROWS, 128), BF)] * count,
        compiler_params=params(),
        name="sum_near",
    )(req, returned)


def sum_far(depth, z, req, returned, held):
    plane, count = returned.shape[:2]
    anywhere = pl.BlockSpec(memory_space=pl.ANY)
    return pl.pallas_call(
        sum_far_kernel,
        grid_spec=pltpu.PrefetchScalarGridSpec(
            num_scalar_prefetch=2,
            grid=(1,),
            in_specs=[anywhere, anywhere],
            out_specs=[anywhere, anywhere],
            scratch_shapes=sum_scratch(plane, count, depth),
        ),
        out_shape=(
            jax.ShapeDtypeStruct((depth, LOCAL, ROWS, 128), BF),
            jax.ShapeDtypeStruct(held.shape, BF),
        ),
        input_output_aliases={3: 1},
        compiler_params=params(),
        name="sum_far",
    )(z, req, returned, held)


def finish_kernel(own_ref, *refs):
    got_refs, (dk_ref, dv_ref) = refs[:-2], refs[-2:]
    for b in range(0, LOCAL, 2):
        pair = []
        for i in range(b, b + 2):
            total = own_ref[i]
            for got_ref in got_refs:
                total = total + got_ref[i].astype(F32)
            dv_ref[i * BLK : (i + 1) * BLK, :] = total[0:BLK].astype(BF)
            low = total[2 * BLK :]
            low = jnp.concatenate([low[:, :64], low[:, 64:]], axis=0)
            pair.append(jnp.concatenate([total[BLK : 2 * BLK], low], axis=1))
        pair = jnp.concatenate(pair, axis=0)
        dk_ref[:, b * BLK : (b + 2) * BLK] = jnp.transpose(pair).astype(BF)


def finish(own, *got):
    return pl.pallas_call(
        finish_kernel,
        out_shape=(
            jax.ShapeDtypeStruct((DK, LOCAL * BLK), BF),
            jax.ShapeDtypeStruct((LOCAL * BLK, DV), BF),
        ),
        compiler_params=params(),
        name="finish",
    )(own, *got)


def dot(a, b, da, db):
    return lax.dot_general(a, b, (((da,), (db,)), ((), ())), preferred_element_type=F32)


def swap(x):
    return jnp.concatenate([x[:, 64:], x[:, :64]], axis=1)


HALF_BLK = BLK // 2
GROUP = SEL * HALF_BLK
PAIR = 4


def lane_ids(rows):
    return lax.broadcasted_iota(jnp.int32, (rows, 128), 1)


def attend_kernel(
    src_ref,
    q_ref,
    do_ref,
    local_hbm,
    near_hbm,
    far_hbm,
    att_ref,
    dq_ref,
    part_near_hbm,
    part_far_hbm,
    own_ref,
    table,
    part,
    k_bufs,
    v_bufs,
    q_bufs,
    do_bufs,
    p_bufs,
    pb_bufs,
    dk_bufs,
    dv_bufs,
    sems,
):
    step = pl.program_id(0)
    n_near, n_far = near_hbm.shape[0], far_hbm.shape[0]
    n_remote = n_near + n_far
    scale = DK**-0.5
    left = lane_ids(HALF_BLK) < 64
    lane = lane_ids(BLK)
    first = lane < 64
    groups = [slice(0, GROUP), slice(GROUP, 2 * GROUP)]

    @pl.when(step == 0)
    def _():
        places = ((near_hbm, 0, n_near), (far_hbm, n_near, n_far), (local_hbm, n_remote, LOCAL))
        copies = [
            pltpu.make_async_copy(ref, table.at[pl.ds(at, n)], sems.at[i])
            for i, (ref, at, n) in enumerate(places)
        ]
        for copy in copies:
            copy.start()
        own_ref[...] = jnp.zeros_like(own_ref)
        for i in range(PAIR):
            v_bufs[i, :, 128:] = jnp.ones((2 * GROUP, 128), BF)
        for copy in copies:
            copy.wait()

    class Block:
        def __init__(self, i):
            self.i, self.b = i, step * PAIR + i
            self.rows = slice(i * BLK, (i + 1) * BLK)
            self.k, self.v, self.q, self.do = (x.at[i] for x in (k_bufs, v_bufs, q_bufs, do_bufs))
            self.p, self.pb, self.dk, self.dv = (x.at[i] for x in (p_bufs, pb_bufs, dk_bufs, dv_bufs))

        def place_keys(self):
            key_id = lax.broadcasted_iota(jnp.int32, (HALF_BLK, 128), 0)
            query_id = lane_ids(HALF_BLK) % BLK
            none = jnp.zeros((HALF_BLK, 128), BF)
            masks = [
                jnp.where(key_id + g * HALF_BLK > query_id, NEG, 0.0).astype(BF) for g in range(2)
            ]
            for e in range(SEL):
                s = src_ref[self.b, e]
                mine = s == n_remote + self.b
                low = table[s, 2 * BLK :]
                for g in range(2):
                    at = g * GROUP + e * HALF_BLK
                    rows = slice(at, at + HALF_BLK)
                    self.v[rows, 0:128] = table[s, g * HALF_BLK : (g + 1) * HALF_BLK]
                    self.k[rows, 0:128] = table[s, BLK + g * HALF_BLK : BLK + (g + 1) * HALF_BLK]
                    mask = jnp.where(mine, masks[g], none)
                    both = (low, mask) if g == 0 else (mask, low)
                    self.k[rows, 128:] = jnp.where(left, *both)

        def place_queries(self):
            one_hot = (lax.broadcasted_iota(jnp.int32, (BLK, 128), 0) == lane % BLK).astype(BF)
            for h in range(0, HEADS, 2):
                t0, t1, t2 = (
                    q_ref[self.rows, h * DK + i * 128 : h * DK + (i + 1) * 128] for i in range(3)
                )
                r1, r2 = swap(t1), swap(t2)
                for k, (high, low, swapped) in enumerate(
                    ((t0, t1, r1), (jnp.where(first, r1, r2), r2, t2))
                ):
                    rows = slice((h + k) * BLK, (h + k + 1) * BLK)
                    for g in range(2):
                        self.q[g, rows, 0:128] = high
                    self.q[0, rows, 128:] = jnp.where(first, low, one_hot)
                    self.q[1, rows, 128:] = jnp.where(first, one_hot, swapped)

        def score(self):
            self.top = None
            for g, rows in enumerate(groups):
                s = dot(self.k[rows, :], self.q[g], 1, 1)
                self.p[rows, :] = s
                m = jnp.max(s, axis=0, keepdims=True)
                self.top = m if self.top is None else jnp.maximum(self.top, m)

        def weigh(self):
            self.out_t = None
            for rows in groups:
                p = jnp.exp2((self.p[rows, :] - self.top) * (scale * LOG2E))
                self.p[rows, :] = p
                pb = p.astype(BF)
                self.pb[rows, :] = pb
                o = dot(self.v[rows, :], pb, 0, 0)
                self.out_t = o if self.out_t is None else self.out_t + o

        def output(self):
            out = jnp.transpose(self.out_t[: DV + 8])
            inverse = 1.0 / out[:, 128:129]
            att = (out[:, :128] * inverse).astype(BF)
            for h in range(HEADS):
                rows = slice(h * BLK, (h + 1) * BLK)
                cols = slice(h * DV, (h + 1) * DV)
                att_ref[self.rows, cols] = att[rows]
                do = (do_ref[self.rows, cols].astype(F32) * inverse[rows]).astype(BF)
                delta = jnp.sum(do.astype(F32) * att[rows].astype(F32), axis=1, keepdims=True)
                delta = jnp.broadcast_to(-delta, (BLK, 128))
                high = delta.astype(BF).astype(F32)
                rest = delta - high
                mid = rest.astype(BF).astype(F32)
                extra = jnp.where(
                    lane == 0, high, jnp.where(lane == 1, mid, jnp.where(lane == 2, rest - mid, 0.0))
                )
                self.do[rows, 0:128] = do
                self.do[rows, 128:] = extra.astype(BF)

        def backward(self):
            do_all = self.do[...]
            self.dq_t = []
            for g, rows in enumerate(groups):
                dp = dot(self.v[rows, :], do_all, 1, 1)
                ds = (self.p[rows, :] * dp).astype(BF)
                self.dv[rows, :] = dot(self.pb[rows, :], self.do[:, 0:128], 1, 0)
                self.dk[rows, :] = dot(ds, self.q[g], 1, 0) * scale
                self.dq_t.append(dot(self.k[rows, :], ds, 0, 0))

        def packed(self, e):
            r1 = slice(e * HALF_BLK, (e + 1) * HALF_BLK)
            r2 = slice(GROUP + e * HALF_BLK, GROUP + (e + 1) * HALF_BLK)
            return (
                (slice(0, HALF_BLK), self.dv[r1, :]),
                (slice(HALF_BLK, BLK), self.dv[r2, :]),
                (slice(BLK, BLK + HALF_BLK), self.dk[r1, 0:128]),
                (slice(BLK + HALF_BLK, 2 * BLK), self.dk[r2, 0:128]),
                (slice(2 * BLK, ROWS), jnp.where(left, self.dk[r1, 128:], self.dk[r2, 128:])),
            )

        def store_parts(self):
            for e in range(SEL):
                at = jnp.minimum(src_ref[self.b, e], n_remote)
                for rows, x in self.packed(e):
                    part[at, rows] = x.astype(BF)

        def add_own(self):
            for rows, x in self.packed(0):
                own_ref[self.b, rows] += x
            for e in range(1, SEL):
                s = src_ref[self.b, e]

                @pl.when(s >= n_remote)
                def _():
                    for rows, x in self.packed(e):
                        own_ref[s - n_remote, rows] += x

        def query_grads(self):
            high = jnp.transpose(self.dq_t[0][:128] + self.dq_t[1][:128]) * scale
            low = self.dq_t[0][128:192] + self.dq_t[1][192:]
            low = jnp.transpose(jnp.concatenate([low, low], axis=0)) * scale
            for h in range(0, HEADS, 2):
                even, odd = slice(h * BLK, (h + 1) * BLK), slice((h + 1) * BLK, (h + 2) * BLK)
                turned = swap(high[odd])
                parts = (
                    high[even],
                    jnp.where(first, low[even], turned),
                    jnp.where(first, turned, low[odd]),
                )
                for i, x in enumerate(parts):
                    dq_ref[self.rows, h * DK + i * 128 : h * DK + (i + 1) * 128] = x.astype(BF)

    blocks = [Block(i) for i in range(PAIR)]
    for block in blocks:
        block.place_keys()
    for block in blocks:
        block.place_queries()
    for block in blocks:
        block.score()
    for block in blocks:
        block.weigh()
    for block in blocks:
        block.output()
    for block in blocks:
        block.backward()
    for block in blocks:
        block.store_parts()
    for block in blocks:
        block.query_grads()
    for block in blocks:
        block.add_own()

    @pl.when(step == LOCAL // PAIR - 1)
    def _():
        places = ((part_near_hbm, 0, n_near), (part_far_hbm, n_near, n_far))
        copies = [
            pltpu.make_async_copy(part.at[pl.ds(at, n)], ref, sems.at[i])
            for i, (ref, at, n) in enumerate(places)
        ]
        for copy in copies:
            copy.start()
        for copy in copies:
            copy.wait()


def attend(src, queries, d_out, local, near, far):
    tokens = LOCAL * BLK
    keys = SEL * BLK
    rows = HEADS * BLK
    n_near, n_far = (x.shape[0] * x.shape[1] for x in (near, far))
    anywhere = pl.BlockSpec(memory_space=pl.ANY)
    attended, d_queries, part_near, part_far, own = pl.pallas_call(
        attend_kernel,
        grid_spec=pltpu.PrefetchScalarGridSpec(
            num_scalar_prefetch=1,
            grid=(LOCAL // PAIR,),
            in_specs=[
                pl.BlockSpec((PAIR * BLK, HEADS * DK), lambda b, src: (b, 0)),
                pl.BlockSpec((PAIR * BLK, HEADS * DV), lambda b, src: (b, 0)),
                anywhere,
                anywhere,
                anywhere,
            ],
            out_specs=[
                pl.BlockSpec((PAIR * BLK, HEADS * DV), lambda b, src: (b, 0)),
                pl.BlockSpec((PAIR * BLK, HEADS * DK), lambda b, src: (b, 0)),
                anywhere,
                anywhere,
                pl.BlockSpec((LOCAL, ROWS, 128), lambda b, src: (0, 0, 0)),
            ],
            scratch_shapes=[
                pltpu.VMEM((n_near + n_far + LOCAL, ROWS, 128), BF),
                pltpu.VMEM((n_near + n_far + 1, ROWS, 128), BF),
                pltpu.VMEM((PAIR, keys, 256), BF),
                pltpu.VMEM((PAIR, keys, 256), BF),
                pltpu.VMEM((PAIR, 2, rows, 256), BF),
                pltpu.VMEM((PAIR, rows, 256), BF),
                pltpu.VMEM((PAIR, keys, rows), F32),
                pltpu.VMEM((PAIR, keys, rows), BF),
                pltpu.VMEM((PAIR, keys, 256), F32),
                pltpu.VMEM((PAIR, keys, 128), F32),
                pltpu.SemaphoreType.DMA((3,)),
            ],
        ),
        out_shape=(
            jax.ShapeDtypeStruct((tokens, HEADS * DV), BF),
            jax.ShapeDtypeStruct((tokens, HEADS * DK), BF),
            jax.ShapeDtypeStruct((n_near, ROWS, 128), BF),
            jax.ShapeDtypeStruct((n_far, ROWS, 128), BF),
            jax.ShapeDtypeStruct((LOCAL, ROWS, 128), F32),
        ),
        compiler_params=params(),
        name="attend",
    )(
        src,
        queries,
        d_out,
        local,
        near.reshape(n_near, ROWS, 128),
        far.reshape(n_far, ROWS, 128),
    )
    return attended, d_queries, part_near.reshape(near.shape), part_far.reshape(far.shape), own


def shards(depth, plane, queries, keys, values, selected, d_out):
    me = lax.axis_index(("z", "y", "x"))
    z = lax.axis_index("z")
    seq_count = depth * plane
    per_half = LOCAL // 2
    half_index = selected // per_half
    is_late = half_index >= seq_count
    owners = jnp.where(is_late, 2 * seq_count - 1 - half_index, half_index)
    inner = selected % per_half + jnp.where(is_late, per_half, 0)
    remote = owners != me
    offset = (owners // plane - z + depth) % depth
    order = jnp.where(offset < 2, offset, jnp.where(offset == depth - 1, 2, offset + 1))
    in_plane = owners % plane
    slots = jnp.where(
        order < 3, in_plane * 3 + order, 3 * plane + in_plane * (depth - 3) + order - 3
    )
    src = jnp.where(remote, slots, seq_count + inner).astype(jnp.int32)
    flat = jnp.where(remote, in_plane * depth + order, -1).reshape(-1)
    hits = flat[:, None] == jnp.arange(seq_count, dtype=jnp.int32)[None, :]
    wanted = jnp.max(jnp.where(hits, inner.reshape(-1)[:, None] + 1, 0), axis=0)
    exchange = functools.partial(
        lax.all_to_all, axis_name=("y", "x"), split_axis=0, concat_axis=0, tiled=True
    )
    up = [(i, (i + 1) % depth) for i in range(depth)]
    down = [(i, (i - 1) % depth) for i in range(depth)]
    where_z = z.reshape(1).astype(jnp.int32)

    local = pack(keys.T, values)
    above = lax.ppermute(local, "z", down)
    below = lax.ppermute(local, "z", up)
    asked = exchange(wanted.reshape(plane, 1, depth)).reshape(plane, depth)
    column = lax.all_gather(local, "z")
    near = exchange(build(0, 3, where_z, asked, local, above, below))
    far = exchange(build(3, depth - 3, where_z, asked, column))
    attended, d_queries, part_near, part_far, own = attend(src, queries, d_out, local, near, far)
    back_far = exchange(part_far)
    far_sums, part_near = sum_far(depth, where_z, asked, back_far, part_near)
    mine = lax.psum_scatter(far_sums, "z", scatter_dimension=0)
    here, to_above, to_below = sum_near(asked, exchange(part_near))
    from_below = lax.ppermute(to_above, "z", up)
    from_above = lax.ppermute(to_below, "z", down)
    d_keys_t, d_values = finish(own, here, from_below, from_above, mine)
    return attended, d_queries, d_keys_t.T, d_values


def solution(mesh):
    grid = Mesh(mesh.devices.reshape(SIDES + (-1,)), ("z", "y", "x", "grp"))
    spec = P(("z", "y", "x"), "grp")
    return jax.shard_map(
        functools.partial(shards, SIDES[0], SIDES[1] * SIDES[2]),
        mesh=grid,
        in_specs=(spec,) * 5,
        out_specs=(spec,) * 4,
        check_vma=False,
    )
```

time: 258 us -> 241 us (0.934)
  Pallas kernels: 65 us -> 47.9 us
  local copies, waits for them, and re-layouts: 8.78 us -> 3.39 us
  waiting for transfers between devices: 22.6 us -> 27.3 us
    pallas_call x2, Pallas kernels: 15.5 us -> 8.48 us  [build(): pl.pallas_call(functools.partial(build_kernel, first), grid_spec=pltpu.Pr...]
    pallas_call x1, Pallas kernels: 33.8 us -> 27.6 us  [attend(): pl.pallas_call(attend_kernel, grid_spec=pltpu.PrefetchScalarGridSpec(num_...]
    all_gather x1, waiting for transfers between devices: 11.1 us -> 15.3 us  [shards(): column = lax.all_gather(local, 'z')]
    unnamed x14 -> x12, local copies, waits for them, and re-layouts: 6.58 us -> 3.15 us
    pallas_call x1, Pallas kernels: 7.12 us -> 4.15 us  [sum_far(): pl.pallas_call(sum_far_kernel, grid_spec=pltpu.PrefetchScalarGridSpec(num...]
  transfers between devices with their start and end apart: 7 -> 7, of which waited for: 4 -> 3; matrix products, arithmetic and copies ran while one was open for 1% -> 1% of each run, Pallas kernels for 8% -> 5%
where the time goes in v3:
time: 241 us; the launch traced here: 240 us
  blocking collectives  132 us (55%)
  Pallas kernels  47.9 us (20%)
  waiting for transfers between devices  27.3 us (11%)
  starting transfers between devices  14.4 us (6%)
  between operations  14.1 us (6%)
  local copies, waits for them, and re-layouts  3.39 us (1%)
    all_to_all x1, blocking collectives, shards(): far = exchange(build(3, depth - 3, where_z, asked, column))  47.6 us
    all_to_all x1, blocking collectives, shards(): back_far = exchange(part_far)  43 us
    all_to_all x1, blocking collectives, shards(): here, to_above, to_below = sum_near(asked, exchange(part_near))  27.6 us
    pallas_call x1, Pallas kernels, attend(): pl.pallas_call(attend_kernel, grid_spec=pltpu.PrefetchScalarGridSpec(num_...  27.6 us
    all_gather x1, waiting for transfers between devices, shards(): column = lax.all_gather(local, 'z')  15.3 us
    all_to_all x1, blocking collectives, shards(): asked = exchange(wanted.reshape(plane, 1, depth)).reshape(plane, depth)  13.4 us
    pallas_call x2, Pallas kernels, build(): pl.pallas_call(functools.partial(build_kernel, first), grid_spec=pltpu.Pr...  8.48 us
    ppermute x1, waiting for transfers between devices, shards(): from_below = lax.ppermute(to_above, 'z', up)  7.7 us
  transfers between devices with their start and end apart: 7, of which 3 were waited for; matrix products, arithmetic and copies ran while one was open for 1% of the time, Pallas kernels for 5%

profile of v3, /device:TPU:2, one launch (start us, length us, event | category | flops | bytes accessed | tf_op | source)
XLA Modules:
  0.0 240.2 jit_solution(7174967034685143639)
XLA Ops:
  7.2 0.0 all-gather.3.cloned.1.call-start
  7.2 1.9 pack.1.refs_0_.local_hbm
  9.1 0.0 all-gather.3.cloned.1.call-update
  9.2 2.0 collective-permute-start.1
  11.2 4.0 %collective-permute-start = (bf16[8,160,128]{2,1,0:T(8,128)(2,1)}, bf16[8,160,128]{2,1,0:T(8,128)(2,1)S(1)}, u32[]{:S(2)}, u32[]{:S(2)}) collective-permute-start(bf16[8,160,128]{2,1,0:T(8,128)(2,1)} %pack.1.refs_0_.local_hbm), channel_id=1, source_target_pairs={{0,224},{32,0},{64,32},{96,64},{128,96},{160,128},{192,160},{224,1... | collective-permute-start | bytes 983048 | tf_op jit(solution)/shard_map/ppermute | solution.py:545
  15.2 1.3 add_select_fusion.5
  16.5 0.1 eq.24
  16.6 0.1 add.80
  16.6 0.1 select_reduce_fusion
  16.8 0.1 reshape.40
  16.9 13.4 %all_to_all.25 = s32[16,1,8]{2,1,0:T(1,128)} all-to-all(s32[16,1,8]{2,1,0:T(1,128)S(1)} %bitcast.22), channel_id=1, replica_groups=mesh['z'=8,'y'=4,'x'=4,'grp'=2] {'y','x'}, dimensions={0} | all-to-all | bytes 1024 | tf_op jit(solution)/shard_map/all_to_all | solution.py:547
  30.3 0.0 collective-permute-done.1.refs_2_
  30.3 0.0 copy-start.2
  30.3 0.0 collective-permute-done.refs_1_
  30.3 0.0 copy-start.3
  30.3 0.7 copy-done.2
  31.0 0.1 copy-done.3
  31.1 3.5 %build.2 = bf16[16,3,160,128]{3,2,1,0:T(8,128)(2,1)} custom-call(s32[1]{0:T(128)} %bitcast.1.z_ref, s32[16,8]{1,0:T(8,128)} %bitcast.17, bf16[8,160,128]{2,1,0:T(8,128)(2,1)} %pack.1.refs_0_.local_hbm, bf16[8,160,128]{2,1,0:T(8,128)(2,1)} %copy-done.3, bf16[8,160,128]{2,1,0:T(8,128)(2,1)} %copy-done.2), custom_call_target="tpu_custom_call" | custom-call | tf_op jit(solution)/shard_map/build/pallas_call | solution.py:76
  34.6 5.0 %all-to-all-start.1 = ((bf16[16,3,160,128]{3,2,1,0:T(8,128)(2,1)}), bf16[16,3,160,128]{3,2,1,0:T(8,128)(2,1)S(1)}, u32[]{:S(2)}, u32[]{:S(2)}) async-start(bf16[16,3,160,128]{3,2,1,0:T(8,128)(2,1)} %build.2), calls=%async_computation.1 | async-start | bytes 3932160 | tf_op jit(solution)/shard_map/all_to_all | solution.py:549
  39.6 0.0 reduce-scatter.2.cloned.1.call-start
  39.7 15.3 %all-gather.3.cloned.1.call-done = bf16[64,160,128]{2,1,0:T(8,128)(2,1)} async-done(((bf16[8,160,128]{2,1,0:T(8,128)(2,1)}), bf16[64,160,128]{2,1,0:T(8,128)(2,1)}) %all-gather.3.cloned.1.call-update) | async-done | bytes 2621456 | tf_op jit(solution)/shard_map/all_gather | solution.py:548
  55.0 5.0 %build.3 = bf16[16,5,160,128]{3,2,1,0:T(8,128)(2,1)} custom-call(s32[1]{0:T(128)} %bitcast.1.z_ref, s32[16,8]{1,0:T(8,128)} %bitcast.18, bf16[8,8,160,128]{3,2,1,0:T(8,128)(2,1)} %bitcast.15), custom_call_target="tpu_custom_call" | custom-call | tf_op jit(solution)/shard_map/build/pallas_call | solution.py:76
  59.9 4.2 %all-to-all-done.1 = bf16[16,3,160,128]{3,2,1,0:T(8,128)(2,1)S(1)} async-done(((bf16[16,3,160,128]{3,2,1,0:T(8,128)(2,1)}), bf16[16,3,160,128]{3,2,1,0:T(8,128)(2,1)S(1)}, u32[]{:S(2)}, u32[]{:S(2)}) %all-to-all-start.1) | async-done | bytes 1966112 | tf_op jit(solution)/shard_map/all_to_all | solution.py:549
  64.1 0.0 copy-start
  64.1 47.6 %all_to_all.26 = bf16[16,5,160,128]{3,2,1,0:T(8,128)(2,1)} all-to-all(bf16[16,5,160,128]{3,2,1,0:T(8,128)(2,1)} %build.3), channel_id=1, replica_groups=mesh['z'=8,'y'=4,'x'=4,'grp'=2] {'y','x'}, dimensions={0} | all-to-all | bytes 6553600 | tf_op jit(solution)/shard_map/all_to_all | solution.py:550
  111.7 0.0 copy-done
  111.7 27.6 %attend.1 = (bf16[512,1024]{1,0:T(8,128)(2,1)}, bf16[512,1536]{1,0:T(8,128)(2,1)}, bf16[48,160,128]{2,1,0:T(8,128)(2,1)}, bf16[80,160,128]{2,1,0:T(8,128)(2,1)}, f32[8,160,128]{2,1,0:T(8,128)}) custom-call(s32[8,16]{1,0:T(8,128)} %get-tuple-element.30.src_ref, bf16[512,1536]{1,0:T(8,128)(2,1)} %q_ref.1, bf16[512,1024]{1,0:T(8,128)(2,1)} %do_ref.1, ...), custom_call_target="tpu_custom_call" | custom-call | tf_op jit(solution)/shard_map/attend/pallas_call | solution.py:464
  139.3 43.0 %all_to_all.27.ret_hbm = bf16[16,5,160,128]{3,2,1,0:T(8,128)(2,1)} all-to-all(bf16[16,5,160,128]{3,2,1,0:T(8,128)(2,1)} %bitcast.14), channel_id=1, replica_groups=mesh['z'=8,'y'=4,'x'=4,'grp'=2] {'y','x'}, dimensions={0} | all-to-all | bytes 6553600 | tf_op jit(solution)/shard_map/all_to_all | solution.py:552
  182.4 4.1 %sum_far.1 = (bf16[8,8,160,128]{3,2,1,0:T(8,128)(2,1)}, bf16[16,3,160,128]{3,2,1,0:T(8,128)(2,1)}) custom-call(s32[1]{0:T(128)} %bitcast.1.z_ref, s32[16,8]{1,0:T(8,128)} %bitcast.19, bf16[16,5,160,128]{3,2,1,0:T(8,128)(2,1)} %all_to_all.27.ret_hbm, bf16[16,3,160,128]{3,2,1,0:T(8,128)(2,1)} %bitcast.13), custom_call_target="tpu_custom_call", output_to_operand_aliasing={{1}: (3, {})} | custom-call | tf_op jit(solution)/shard_map/sum_far/pallas_call | solution.py:179
  186.5 0.0 copy-start.1
  186.5 0.0 reduce-scatter.2.cloned.1.call-update
  186.5 1.5 copy-done.1
  188.1 27.6 %all_to_all.28.ret_hbm = bf16[16,3,160,128]{3,2,1,0:T(8,128)(2,1)} all-to-all(bf16[16,3,160,128]{3,2,1,0:T(8,128)(2,1)S(1)} %copy-done.1), channel_id=1, replica_groups=mesh['z'=8,'y'=4,'x'=4,'grp'=2] {'y','x'}, dimensions={0} | all-to-all | bytes 3932160 | tf_op jit(solution)/shard_map/all_to_all | solution.py:555
  215.7 3.3 %sum_near.1 = (bf16[8,160,128]{2,1,0:T(8,128)(2,1)}, bf16[8,160,128]{2,1,0:T(8,128)(2,1)}, bf16[8,160,128]{2,1,0:T(8,128)(2,1)}) custom-call(s32[16,8]{1,0:T(8,128)} %bitcast.20, bf16[16,3,160,128]{3,2,1,0:T(8,128)(2,1)} %all_to_all.28.ret_hbm), custom_call_target="tpu_custom_call" | custom-call | tf_op jit(solution)/shard_map/sum_near/pallas_call | solution.py:161
  219.0 0.1 collective-permute-start.2
  219.1 3.2 %collective-permute-start.3 = (bf16[8,160,128]{2,1,0:T(8,128)(2,1)}, bf16[8,160,128]{2,1,0:T(8,128)(2,1)S(1)}, u32[]{:S(2)}, u32[]{:S(2)}) collective-permute-start(bf16[8,160,128]{2,1,0:T(8,128)(2,1)} %get-tuple-element.24), channel_id=1, source_target_pairs={{0,224},{32,0},{64,32},{96,64},{128,96},{160,128},{192,160},{224,1... | collective-permute-start | bytes 983048 | tf_op jit(solution)/shard_map/ppermute | solution.py:557
  222.3 7.7 %collective-permute-done.2.refs_1_ = bf16[8,160,128]{2,1,0:T(8,128)(2,1)S(1)} collective-permute-done((bf16[8,160,128]{2,1,0:T(8,128)(2,1)}, bf16[8,160,128]{2,1,0:T(8,128)(2,1)S(1)}, u32[]{:S(2)}, u32[]{:S(2)}) %collective-permute-start.2) | collective-permute-done | bytes 327712 | tf_op jit(solution)/shard_map/ppermute | solution.py:556
  230.0 0.0 copy-start.4
  230.0 0.0 collective-permute-done.3.refs_2_
  230.0 0.0 copy-start.5
  230.0 0.0 reduce-scatter.2.cloned.1.call-done
  230.1 0.7 copy-done.4
  230.8 0.1 copy-done.5
  230.9 2.5 %finish.1 = (bf16[192,512]{1,0:T(8,128)(2,1)}, bf16[512,128]{1,0:T(8,128)(2,1)}) custom-call(f32[8,160,128]{2,1,0:T(8,128)} %get-tuple-element.18.own_ref, bf16[8,160,128]{2,1,0:T(8,128)(2,1)} %get-tuple-element.22.refs_0_, bf16[8,160,128]{2,1,0:T(8,128)(2,1)} %copy-done.4, bf16[8,160,128]{2,1,0:T(8,128)(2,1)} %copy-done.5, bf16[8,160,128]{2,1,0:T(8,128)(2,1)} %bitcast.16), custom_call_target="tpu_custom_call" | custom-call | tf_op jit(solution)/shard_map/finish/pallas_call | solution.py:215
Async XLA Ops:
  7.2 47.8 %all-gather.3.cloned.1.call-start = ((), (), s32[]{:S(2)}) async-start(), calls=%async_computation.7 | async-start | bytes 2949120 | tf_op jit(solution)/shard_map/all_gather | solution.py:548
  9.2 21.1 %collective-permute-start.1 = (bf16[8,160,128]{2,1,0:T(8,128)(2,1)}, bf16[8,160,128]{2,1,0:T(8,128)(2,1)S(1)}, u32[]{:S(2)}, u32[]{:S(2)}) collective-permute-start(bf16[8,160,128]{2,1,0:T(8,128)(2,1)} %pack.1.refs_0_.local_hbm), channel_id=1, source_target_pairs={{0,32},{32,64},{64,96},{96,128},{128,160},{160,192},{192,224},{224... | collective-permute-start | bytes 983048 | tf_op jit(solution)/shard_map/ppermute | solution.py:546
  11.2 19.1 %collective-permute-start = (bf16[8,160,128]{2,1,0:T(8,128)(2,1)}, bf16[8,160,128]{2,1,0:T(8,128)(2,1)S(1)}, u32[]{:S(2)}, u32[]{:S(2)}) collective-permute-start(bf16[8,160,128]{2,1,0:T(8,128)(2,1)} %pack.1.refs_0_.local_hbm), channel_id=1, source_target_pairs={{0,224},{32,0},{64,32},{96,64},{128,96},{160,128},{192,160},{224,1... | collective-permute-start | bytes 983048 | tf_op jit(solution)/shard_map/ppermute | solution.py:545
  30.3 0.7 copy-start.2
  30.3 0.8 copy-start.3
  34.6 29.5 %all-to-all-start.1 = ((bf16[16,3,160,128]{3,2,1,0:T(8,128)(2,1)}), bf16[16,3,160,128]{3,2,1,0:T(8,128)(2,1)S(1)}, u32[]{:S(2)}, u32[]{:S(2)}) async-start(bf16[16,3,160,128]{3,2,1,0:T(8,128)(2,1)} %build.2), calls=%async_computation.1 | async-start | bytes 3932160 | tf_op jit(solution)/shard_map/all_to_all | solution.py:549
  39.6 190.4 %reduce-scatter.2.cloned.1.call-start = ((), (), s32[]{:S(2)}) async-start(), calls=%async_computation.6 | async-start | bytes 2949120 | tf_op jit(solution)/shard_map/reduce_scatter | solution.py:554
  64.1 47.6 %copy-start = (bf16[16,3,160,128]{3,2,1,0:T(8,128)(2,1)}, bf16[16,3,160,128]{3,2,1,0:T(8,128)(2,1)S(1)}, u32[]{:S(2)}) copy-start(bf16[16,3,160,128]{3,2,1,0:T(8,128)(2,1)S(1)} %all-to-all-done.1) | copy-start | bytes 5898244
  186.5 1.5 copy-start.1
  219.0 11.0 %collective-permute-start.2 = (bf16[8,160,128]{2,1,0:T(8,128)(2,1)}, bf16[8,160,128]{2,1,0:T(8,128)(2,1)S(1)}, u32[]{:S(2)}, u32[]{:S(2)}) collective-permute-start(bf16[8,160,128]{2,1,0:T(8,128)(2,1)} %get-tuple-element.23), channel_id=1, source_target_pairs={{0,32},{32,64},{64,96},{96,128},{128,160},{160,192},{192,224},{224... | collective-permute-start | bytes 983048 | tf_op jit(solution)/shard_map/ppermute | solution.py:556
  219.1 10.9 %collective-permute-start.3 = (bf16[8,160,128]{2,1,0:T(8,128)(2,1)}, bf16[8,160,128]{2,1,0:T(8,128)(2,1)S(1)}, u32[]{:S(2)}, u32[]{:S(2)}) collective-permute-start(bf16[8,160,128]{2,1,0:T(8,128)(2,1)} %get-tuple-element.24), channel_id=1, source_target_pairs={{0,224},{32,0},{64,32},{96,64},{128,96},{160,128},{192,160},{224,1... | collective-permute-start | bytes 983048 | tf_op jit(solution)/shard_map/ppermute | solution.py:557
  230.0 0.7 copy-start.4
  230.0 0.8 copy-start.5
Sparse Core Ops, SparseCore 0:
  9.8 45.1 all-gather.2
  186.7 42.4 reduce-scatter.1

commit v4 on v3

--- a/solution.py
+++ b/solution.py
@@ -108,16 +108,16 @@
     return stores
 
 
-def sum_near_kernel(req_ref, ret_hbm, *refs):
+def sum_near_kernel(first, req_ref, ret_hbm, *refs):
     outs, (buf, acc, staged, in_sems, out_sems) = refs[:-5], refs[-5:]
     for store in sum_blocks(
-        0, req_ref, ret_hbm, buf, acc, staged, in_sems, out_sems, lambda d: outs[d]
+        first, req_ref, ret_hbm, buf, acc, staged, in_sems, out_sems, lambda d: outs[d]
     ):
         store.wait()
 
 
 def sum_far_kernel(
-    z_ref, req_ref, ret_hbm, hold_ref, out_hbm, held_ref, buf, acc, staged, in_sems, out_sems
+    z_ref, req_ref, ret_hbm, out_hbm, buf, acc, staged, in_sems, out_sems
 ):
     depth, count = out_hbm.shape[0], ret_hbm.shape[1]
     near = depth - count
@@ -155,11 +155,11 @@
     ]
 
 
-def sum_near(req, returned):
+def sum_near(first, req, returned):
     plane, count = returned.shape[:2]
     anywhere = pl.BlockSpec(memory_space=pl.ANY)
     return pl.pallas_call(
-        sum_near_kernel,
+        functools.partial(sum_near_kernel, first),
         grid_spec=pltpu.PrefetchScalarGridSpec(
             num_scalar_prefetch=1,
             grid=(1,),
@@ -173,7 +173,7 @@
     )(req, returned)
 
 
-def sum_far(depth, z, req, returned, held):
+def sum_far(depth, z, req, returned):
     plane, count = returned.shape[:2]
     anywhere = pl.BlockSpec(memory_space=pl.ANY)
     return pl.pallas_call(
@@ -181,18 +181,14 @@
         grid_spec=pltpu.PrefetchScalarGridSpec(
             num_scalar_prefetch=2,
             grid=(1,),
-            in_specs=[anywhere, anywhere],
-            out_specs=[anywhere, anywhere],
+            in_specs=[anywhere],
+            out_specs=anywhere,
             scratch_shapes=sum_scratch(plane, count, depth),
         ),
-        out_shape=(
-            jax.ShapeDtypeStruct((depth, LOCAL, ROWS, 128), BF),
-            jax.ShapeDtypeStruct(held.shape, BF),
-        ),
-        input_output_aliases={3: 1},
+        out_shape=jax.ShapeDtypeStruct((depth, LOCAL, ROWS, 128), BF),
         compiler_params=params(),
         name="sum_far",
-    )(z, req, returned, held)
+    )(z, req, returned)
 
 
 def finish_kernel(own_ref, *refs):
@@ -249,7 +245,8 @@
     far_hbm,
     att_ref,
     dq_ref,
-    part_near_hbm,
+    part_here_hbm,
+    part_side_hbm,
     part_far_hbm,
     own_ref,
     table,
@@ -265,7 +262,8 @@
     sems,
 ):
     step = pl.program_id(0)
-    n_near, n_far = near_hbm.shape[0], far_hbm.shape[0]
+    plane, n_far = near_hbm.shape[0], far_hbm.shape[0]
+    n_near = plane * near_hbm.shape[1]
     n_remote = n_near + n_far
     scale = DK**-0.5
     left = lane_ids(HALF_BLK) < 64
@@ -273,20 +271,28 @@
     first = lane < 64
     groups = [slice(0, GROUP), slice(GROUP, 2 * GROUP)]
 
+    loads = [(near_hbm.at[:, d], d * plane, plane) for d in range(near_hbm.shape[1])]
+    loads += [(local_hbm, n_remote, LOCAL), (far_hbm, n_near, n_far)]
+    loads = [
+        pltpu.make_async_copy(ref, table.at[pl.ds(at, n)], sems.at[i])
+        for i, (ref, at, n) in enumerate(loads)
+    ]
+    stores = [(part_far_hbm, n_near, n_far), (part_here_hbm, 0, plane)]
+    stores += [
+        (part_side_hbm.at[:, d], (d + 1) * plane, plane) for d in range(part_side_hbm.shape[1])
+    ]
+    stores = [
+        pltpu.make_async_copy(part.at[pl.ds(at, n)], ref, sems.at[i])
+        for i, (ref, at, n) in enumerate(stores)
+    ]
+
     @pl.when(step == 0)
     def _():
-        places = ((near_hbm, 0, n_near), (far_hbm, n_near, n_far), (local_hbm, n_remote, LOCAL))
-        copies = [
-            pltpu.make_async_copy(ref, table.at[pl.ds(at, n)], sems.at[i])
-            for i, (ref, at, n) in enumerate(places)
-        ]
-        for copy in copies:
-            copy.start()
+        for load in loads:
+            load.start()
         own_ref[...] = jnp.zeros_like(own_ref)
         for i in range(PAIR):
             v_bufs[i, :, 128:] = jnp.ones((2 * GROUP, 128), BF)
-        for copy in copies:
-            copy.wait()
 
     class Block:
         def __init__(self, i):
@@ -346,11 +352,11 @@
                 self.p[rows, :] = p
                 pb = p.astype(BF)
                 self.pb[rows, :] = pb
-                o = dot(self.v[rows, :], pb, 0, 0)
+                o = dot(self.v[rows, : DV + 16], pb, 0, 0)
                 self.out_t = o if self.out_t is None else self.out_t + o
 
         def output(self):
-            out = jnp.transpose(self.out_t[: DV + 8])
+            out = jnp.transpose(self.out_t)
             inverse = 1.0 / out[:, 128:129]
             att = (out[:, :128] * inverse).astype(BF)
             for h in range(HEADS):
@@ -424,35 +430,53 @@
 
     blocks = [Block(i) for i in range(PAIR)]
     for block in blocks:
-        block.place_keys()
-    for block in blocks:
         block.place_queries()
-    for block in blocks:
-        block.score()
-    for block in blocks:
-        block.weigh()
-    for block in blocks:
-        block.output()
-    for block in blocks:
-        block.backward()
-    for block in blocks:
-        block.store_parts()
+
+    @pl.when(step == 0)
+    def _():
+        for load in loads:
+            load.wait()
+
+    blocks[0].place_keys()
+    blocks[1].place_keys()
+    blocks[0].score()
+    blocks[2].place_keys()
+    blocks[1].score()
+    blocks[0].weigh()
+    blocks[3].place_keys()
+    blocks[2].score()
+    blocks[1].weigh()
+    blocks[0].output()
+    blocks[3].score()
+    blocks[2].weigh()
+    blocks[1].output()
+    blocks[0].backward()
+    blocks[3].weigh()
+    blocks[2].output()
+    blocks[1].backward()
+    blocks[0].store_parts()
+    blocks[3].output()
+    blocks[2].backward()
+    blocks[1].store_parts()
+    blocks[3].backward()
+    blocks[2].store_parts()
+    blocks[3].store_parts()
+    last = step == LOCAL // PAIR - 1
+
+    @pl.when(last)
+    def _():
+        for store in stores:
+            store.start()
+
     for block in blocks:
         block.query_grads()
     for block in blocks:
         block.add_own()
 
-    @pl.when(step == LOCAL // PAIR - 1)
+    @pl.when(last)
     def _():
-        places = ((part_near_hbm, 0, n_near), (part_far_hbm, n_near, n_far))
-        copies = [
-            pltpu.make_async_copy(part.at[pl.ds(at, n)], ref, sems.at[i])
-            for i, (ref, at, n) in enumerate(places)
-        ]
-        for copy in copies:
-            copy.start()
-        for copy in copies:
-            copy.wait()
+        for store in stores:
+            store.wait()
 
 
 def attend(src, queries, d_out, local, near, far):
@@ -461,7 +485,8 @@
     rows = HEADS * BLK
     n_near, n_far = (x.shape[0] * x.shape[1] for x in (near, far))
     anywhere = pl.BlockSpec(memory_space=pl.ANY)
-    attended, d_queries, part_near, part_far, own = pl.pallas_call(
+    plane = near.shape[0]
+    return pl.pallas_call(
         attend_kernel,
         grid_spec=pltpu.PrefetchScalarGridSpec(
             num_scalar_prefetch=1,
@@ -478,6 +503,7 @@
                 pl.BlockSpec((PAIR * BLK, HEADS * DK), lambda b, src: (b, 0)),
                 anywhere,
                 anywhere,
+                anywhere,
                 pl.BlockSpec((LOCAL, ROWS, 128), lambda b, src: (0, 0, 0)),
             ],
             scratch_shapes=[
@@ -491,13 +517,14 @@
                 pltpu.VMEM((PAIR, keys, rows), BF),
                 pltpu.VMEM((PAIR, keys, 256), F32),
                 pltpu.VMEM((PAIR, keys, 128), F32),
-                pltpu.SemaphoreType.DMA((3,)),
+                pltpu.SemaphoreType.DMA((5,)),
             ],
         ),
         out_shape=(
             jax.ShapeDtypeStruct((tokens, HEADS * DV), BF),
             jax.ShapeDtypeStruct((tokens, HEADS * DK), BF),
-            jax.ShapeDtypeStruct((n_near, ROWS, 128), BF),
+            jax.ShapeDtypeStruct((plane, ROWS, 128), BF),
+            jax.ShapeDtypeStruct((plane, 2, ROWS, 128), BF),
             jax.ShapeDtypeStruct((n_far, ROWS, 128), BF),
             jax.ShapeDtypeStruct((LOCAL, ROWS, 128), F32),
         ),
@@ -508,10 +535,9 @@
         queries,
         d_out,
         local,
-        near.reshape(n_near, ROWS, 128),
+        near,
         far.reshape(n_far, ROWS, 128),
     )
-    return attended, d_queries, part_near.reshape(near.shape), part_far.reshape(far.shape), own
 
 
 def shards(depth, plane, queries, keys, values, selected, d_out):
@@ -528,7 +554,7 @@
     order = jnp.where(offset < 2, offset, jnp.where(offset == depth - 1, 2, offset + 1))
     in_plane = owners % plane
     slots = jnp.where(
-        order < 3, in_plane * 3 + order, 3 * plane + in_plane * (depth - 3) + order - 3
+        order < 3, order * plane + in_plane, 3 * plane + in_plane * (depth - 3) + order - 3
     )
     src = jnp.where(remote, slots, seq_count + inner).astype(jnp.int32)
     flat = jnp.where(remote, in_plane * depth + order, -1).reshape(-1)
@@ -548,13 +574,17 @@
     column = lax.all_gather(local, "z")
     near = exchange(build(0, 3, where_z, asked, local, above, below))
     far = exchange(build(3, depth - 3, where_z, asked, column))
-    attended, d_queries, part_near, part_far, own = attend(src, queries, d_out, local, near, far)
-    back_far = exchange(part_far)
-    far_sums, part_near = sum_far(depth, where_z, asked, back_far, part_near)
+    attended, d_queries, part_here, part_side, part_far, own = attend(
+        src, queries, d_out, local, near, far
+    )
+    far_sums = sum_far(depth, where_z, asked, exchange(part_far.reshape(far.shape)))
+    far_sums, part_side = lax.optimization_barrier((far_sums, part_side))
     mine = lax.psum_scatter(far_sums, "z", scatter_dimension=0)
-    here, to_above, to_below = sum_near(asked, exchange(part_near))
+    to_above, to_below = sum_near(1, asked, exchange(part_side))
+    to_above, to_below, part_here = lax.optimization_barrier((to_above, to_below, part_here))
     from_below = lax.ppermute(to_above, "z", up)
     from_above = lax.ppermute(to_below, "z", down)
+    (here,) = sum_near(0, asked, exchange(part_here[:, None]))
     d_keys_t, d_values = finish(own, here, from_below, from_above, mine)
     return attended, d_queries, d_keys_t.T, d_values
 

time: 241 us -> 239 us (level)
  blocking collectives: 132 us -> 124 us
  starting transfers between devices: 14.4 us -> 19.1 us
    ppermute x1, waiting for transfers between devices: 7.7 us -> 0.48 us  [shards(): from_below = lax.ppermute(to_above, 'z', up)]
    all_to_all x2, blocking collectives: 70.7 us -> 63.6 us  [the longest x1 43.3 us: shards(): exchange(part_far.reshape(far.shape))]
    all_to_all x0 -> x1, waiting for transfers between devices: none -> 6.33 us  [shards(): here, = sum_near(0, asked, exchange(part_here[:, None]))]
    all_to_all x0 -> x1, starting transfers between devices: none -> 4.84 us  [shards(): here, = sum_near(0, asked, exchange(part_here[:, None]))]
    pallas_call x1 -> x2, Pallas kernels: 3.32 us -> 5.91 us  [sum_near(): pl.pallas_call(functools.partial(sum_near_kernel, first), grid_spec=pltpu...]
  transfers between devices with their start and end apart: 7 -> 8, of which waited for: 3 -> 4; matrix products, arithmetic and copies ran while one was open for 1% -> 1% of each run, Pallas kernels for 5% -> 6%
where the time goes in v4:
time: 239 us; the launch traced here: 238 us
  blocking collectives  124 us (52%)
  Pallas kernels  48.6 us (20%)
  waiting for transfers between devices  26.4 us (11%)
  starting transfers between devices  19.1 us (8%)
  between operations  14.1 us (6%)
  local copies, waits for them, and re-layouts  4.01 us (2%)
    all_to_all x1, blocking collectives, shards(): far = exchange(build(3, depth - 3, where_z, asked, column))  47.5 us
    all_to_all x1, blocking collectives, shards(): exchange(part_far.reshape(far.shape))  43.3 us
    pallas_call x1, Pallas kernels, attend(): pl.pallas_call(attend_kernel, grid_spec=pltpu.PrefetchScalarGridSpec(num_...  25.7 us
    all_to_all x1, blocking collectives, shards(): to_above, to_below = sum_near(1, asked, exchange(part_side))  20.3 us
    all_gather x1, waiting for transfers between devices, shards(): column = lax.all_gather(local, 'z')  15.4 us
    all_to_all x1, blocking collectives, shards(): asked = exchange(wanted.reshape(plane, 1, depth)).reshape(plane, depth)  13.4 us
    pallas_call x2, Pallas kernels, build(): pl.pallas_call(functools.partial(build_kernel, first), grid_spec=pltpu.Pr...  8.47 us
    all_to_all x1, waiting for transfers between devices, shards(): here, = sum_near(0, asked, exchange(part_here[:, None]))  6.33 us
  transfers between devices with their start and end apart: 8, of which 4 were waited for; matrix products, arithmetic and copies ran while one was open for 1% of the time, Pallas kernels for 6%

profile of v4, /device:TPU:2, one launch (start us, length us, event | category | flops | bytes accessed | tf_op | source)
XLA Modules:
  0.0 238.1 jit_solution(11939135756440034092)
XLA Ops:
  7.2 0.0 all-gather.3.cloned.1.call-start
  7.2 1.9 pack.1.refs_0_.local_hbm
  9.1 0.0 all-gather.3.cloned.1.call-update
  9.2 2.0 collective-permute-start.1
  11.2 4.0 %collective-permute-start = (bf16[8,160,128]{2,1,0:T(8,128)(2,1)}, bf16[8,160,128]{2,1,0:T(8,128)(2,1)S(1)}, u32[]{:S(2)}, u32[]{:S(2)}) collective-permute-start(bf16[8,160,128]{2,1,0:T(8,128)(2,1)} %pack.1.refs_0_.local_hbm), channel_id=1, source_target_pairs={{0,224},{32,0},{64,32},{96,64},{128,96},{160,128},{192,160},{224,1... | collective-permute-start | bytes 983048 | tf_op jit(solution)/shard_map/ppermute | solution.py:571
  15.2 1.3 add_select_fusion.5
  16.5 0.1 eq.24
  16.6 0.1 add.80
  16.6 0.1 select_reduce_fusion
  16.8 0.1 reshape.34
  16.9 13.4 %all_to_all.30 = s32[16,1,8]{2,1,0:T(1,128)} all-to-all(s32[16,1,8]{2,1,0:T(1,128)S(1)} %bitcast.20), channel_id=1, replica_groups=mesh['z'=8,'y'=4,'x'=4,'grp'=2] {'y','x'}, dimensions={0} | all-to-all | bytes 1024 | tf_op jit(solution)/shard_map/all_to_all | solution.py:573
  30.3 0.0 collective-permute-done.1.refs_2_
  30.3 0.0 copy-start.3
  30.3 0.0 collective-permute-done.refs_1_
  30.3 0.0 copy-start.4
  30.3 0.7 copy-done.3
  31.0 0.1 copy-done.4
  31.1 3.5 %build.2 = bf16[16,3,160,128]{3,2,1,0:T(8,128)(2,1)} custom-call(s32[1]{0:T(128)} %bitcast.1.z_ref, s32[16,8]{1,0:T(8,128)} %bitcast.14, bf16[8,160,128]{2,1,0:T(8,128)(2,1)} %pack.1.refs_0_.local_hbm, bf16[8,160,128]{2,1,0:T(8,128)(2,1)} %copy-done.4, bf16[8,160,128]{2,1,0:T(8,128)(2,1)} %copy-done.3), custom_call_target="tpu_custom_call" | custom-call | tf_op jit(solution)/shard_map/build/pallas_call | solution.py:76
  34.6 5.0 %all-to-all-start.1 = ((bf16[16,3,160,128]{3,2,1,0:T(8,128)(2,1)}), bf16[16,3,160,128]{3,2,1,0:T(8,128)(2,1)S(1)}, u32[]{:S(2)}, u32[]{:S(2)}) async-start(bf16[16,3,160,128]{3,2,1,0:T(8,128)(2,1)} %build.2), calls=%async_computation.1 | async-start | bytes 3932160 | tf_op jit(solution)/shard_map/all_to_all | solution.py:575
  39.6 0.0 reduce-scatter.2.cloned.1.call-start
  39.6 15.4 %all-gather.3.cloned.1.call-done = bf16[64,160,128]{2,1,0:T(8,128)(2,1)} async-done(((bf16[8,160,128]{2,1,0:T(8,128)(2,1)}), bf16[64,160,128]{2,1,0:T(8,128)(2,1)}) %all-gather.3.cloned.1.call-update) | async-done | bytes 2621456 | tf_op jit(solution)/shard_map/all_gather | solution.py:574
  55.1 5.0 %build.3 = bf16[16,5,160,128]{3,2,1,0:T(8,128)(2,1)} custom-call(s32[1]{0:T(128)} %bitcast.1.z_ref, s32[16,8]{1,0:T(8,128)} %bitcast.15, bf16[8,8,160,128]{3,2,1,0:T(8,128)(2,1)} %bitcast.12), custom_call_target="tpu_custom_call" | custom-call | tf_op jit(solution)/shard_map/build/pallas_call | solution.py:76
  60.0 4.1 %all-to-all-done.1.near_hbm = bf16[16,3,160,128]{3,2,1,0:T(8,128)(2,1)S(1)} async-done(((bf16[16,3,160,128]{3,2,1,0:T(8,128)(2,1)}), bf16[16,3,160,128]{3,2,1,0:T(8,128)(2,1)S(1)}, u32[]{:S(2)}, u32[]{:S(2)}) %all-to-all-start.1) | async-done | bytes 1966112 | tf_op jit(solution)/shard_map/all_to_all | solution.py:575
  64.1 0.0 copy-start
  64.1 47.5 %all_to_all.31 = bf16[16,5,160,128]{3,2,1,0:T(8,128)(2,1)} all-to-all(bf16[16,5,160,128]{3,2,1,0:T(8,128)(2,1)} %build.3), channel_id=1, replica_groups=mesh['z'=8,'y'=4,'x'=4,'grp'=2] {'y','x'}, dimensions={0} | all-to-all | bytes 6553600 | tf_op jit(solution)/shard_map/all_to_all | solution.py:576
  111.6 0.0 copy-done
  111.6 25.7 %attend.1 = (bf16[512,1024]{1,0:T(8,128)(2,1)}, bf16[512,1536]{1,0:T(8,128)(2,1)}, bf16[16,160,128]{2,1,0:T(8,128)(2,1)}, bf16[16,2,160,128]{3,2,1,0:T(8,128)(2,...) custom-call(s32[8,16]{1,0:T(8,128)} %get-tuple-element.36.src_ref, bf16[512,1536]{1,0:T(8,128)(2,1)} %q_ref.1, ...), custom_call_target="tpu_custom_call" | custom-call | tf_op jit(solution)/shard_map/attend/pallas_call | solution.py:489
  137.3 43.3 %all_to_all.32.ret_hbm = bf16[16,5,160,128]{3,2,1,0:T(8,128)(2,1)} all-to-all(bf16[16,5,160,128]{3,2,1,0:T(8,128)(2,1)} %bitcast.11), channel_id=1, replica_groups=mesh['z'=8,'y'=4,'x'=4,'grp'=2] {'y','x'}, dimensions={0} | all-to-all | bytes 6553600 | tf_op jit(solution)/shard_map/all_to_all | solution.py:580
  180.6 4.1 %sum_far.1 = bf16[8,8,160,128]{3,2,1,0:T(8,128)(2,1)} custom-call(s32[1]{0:T(128)} %bitcast.1.z_ref, s32[16,8]{1,0:T(8,128)} %bitcast.16, bf16[16,5,160,128]{3,2,1,0:T(8,128)(2,1)} %all_to_all.32.ret_hbm), custom_call_target="tpu_custom_call" | custom-call | tf_op jit(solution)/shard_map/sum_far/pallas_call | solution.py:179
  184.7 0.0 copy-start.2
  184.7 0.0 reduce-scatter.2.cloned.1.call-update
  184.7 1.3 copy-done.2
  186.0 20.3 %all_to_all.33.ret_hbm = bf16[16,2,160,128]{3,2,1,0:T(8,128)(2,1)} all-to-all(bf16[16,2,160,128]{3,2,1,0:T(8,128)(2,1)S(1)} %copy-done.2), channel_id=1, replica_groups=mesh['z'=8,'y'=4,'x'=4,'grp'=2] {'y','x'}, dimensions={0} | all-to-all | bytes 2621440 | tf_op jit(solution)/shard_map/all_to_all | solution.py:583
  206.3 3.1 %sum_near.2 = (bf16[8,160,128]{2,1,0:T(8,128)(2,1)}, bf16[8,160,128]{2,1,0:T(8,128)(2,1)}) custom-call(s32[16,8]{1,0:T(8,128)} %bitcast.17, bf16[16,2,160,128]{3,2,1,0:T(8,128)(2,1)} %all_to_all.33.ret_hbm), custom_call_target="tpu_custom_call" | custom-call | tf_op jit(solution)/shard_map/sum_near/pallas_call | solution.py:161
  209.4 4.8 %all-to-all-start.5 = ((bf16[16,1,160,128]{3,2,1,0:T(8,128)(2,1)}), bf16[16,1,160,128]{3,2,1,0:T(8,128)(2,1)S(1)}, u32[]{:S(2)}, u32[]{:S(2)}) async-start(bf16[16,1,160,128]{3,2,1,0:T(8,128)(2,1)} %bitcast.7), calls=%async_computation.5 | async-start | bytes 1310720 | tf_op jit(solution)/shard_map/all_to_all | solution.py:587
  214.2 0.0 collective-permute-start.2
  214.2 3.2 %collective-permute-start.3 = (bf16[8,160,128]{2,1,0:T(8,128)(2,1)}, bf16[8,160,128]{2,1,0:T(8,128)(2,1)S(1)}, u32[]{:S(2)}, u32[]{:S(2)}) collective-permute-start(bf16[8,160,128]{2,1,0:T(8,128)(2,1)} %get-tuple-element.30), channel_id=1, source_target_pairs={{0,224},{32,0},{64,32},{96,64},{128,96},{160,128},{192,160},{224,1... | collective-permute-start | bytes 983048 | tf_op jit(solution)/shard_map/ppermute | solution.py:586
  217.5 6.3 %all-to-all-done.5.ret_hbm = bf16[16,1,160,128]{3,2,1,0:T(8,128)(2,1)S(1)} async-done(((bf16[16,1,160,128]{3,2,1,0:T(8,128)(2,1)}), bf16[16,1,160,128]{3,2,1,0:T(8,128)(2,1)S(1)}, u32[]{:S(2)}, u32[]{:S(2)}) %all-to-all-start.5) | async-done | bytes 655392 | tf_op jit(solution)/shard_map/all_to_all | solution.py:587
  223.8 0.0 copy-start.1
  223.8 0.8 copy-done.1
  224.6 2.8 %sum_near.3.refs_0_ = bf16[8,160,128]{2,1,0:T(8,128)(2,1)} custom-call(s32[16,8]{1,0:T(8,128)} %bitcast.18, bf16[16,1,160,128]{3,2,1,0:T(8,128)(2,1)} %copy-done.1), custom_call_target="tpu_custom_call" | custom-call | tf_op jit(solution)/shard_map/sum_near/pallas_call | solution.py:161
  227.5 0.5 collective-permute-done.2.refs_1_
  228.0 0.0 copy-start.5
  228.0 0.0 collective-permute-done.3.refs_2_
  228.0 0.0 copy-start.6
  228.0 0.0 reduce-scatter.2.cloned.1.call-done
  228.0 0.7 copy-done.5
  228.7 0.1 copy-done.6
  228.8 2.5 %finish.1 = (bf16[192,512]{1,0:T(8,128)(2,1)}, bf16[512,128]{1,0:T(8,128)(2,1)}) custom-call(f32[8,160,128]{2,1,0:T(8,128)} %get-tuple-element.21.own_ref, bf16[8,160,128]{2,1,0:T(8,128)(2,1)} %sum_near.3.refs_0_, bf16[8,160,128]{2,1,0:T(8,128)(2,1)} %copy-done.5, bf16[8,160,128]{2,1,0:T(8,128)(2,1)} %copy-done.6, bf16[8,160,128]{2,1,0:T(8,128)(2,1)} %bitcast.13), custom_call_target="tpu_custom_call" | custom-call | tf_op jit(solution)/shard_map/finish/pallas_call | solution.py:211
Async XLA Ops:
  7.2 47.9 %all-gather.3.cloned.1.call-start = ((), (), s32[]{:S(2)}) async-start(), calls=%async_computation.8 | async-start | bytes 2949120 | tf_op jit(solution)/shard_map/all_gather | solution.py:574
  9.2 21.1 %collective-permute-start.1 = (bf16[8,160,128]{2,1,0:T(8,128)(2,1)}, bf16[8,160,128]{2,1,0:T(8,128)(2,1)S(1)}, u32[]{:S(2)}, u32[]{:S(2)}) collective-permute-start(bf16[8,160,128]{2,1,0:T(8,128)(2,1)} %pack.1.refs_0_.local_hbm), channel_id=1, source_target_pairs={{0,32},{32,64},{64,96},{96,128},{128,160},{160,192},{192,224},{224... | collective-permute-start | bytes 983048 | tf_op jit(solution)/shard_map/ppermute | solution.py:572
  11.2 19.1 %collective-permute-start = (bf16[8,160,128]{2,1,0:T(8,128)(2,1)}, bf16[8,160,128]{2,1,0:T(8,128)(2,1)S(1)}, u32[]{:S(2)}, u32[]{:S(2)}) collective-permute-start(bf16[8,160,128]{2,1,0:T(8,128)(2,1)} %pack.1.refs_0_.local_hbm), channel_id=1, source_target_pairs={{0,224},{32,0},{64,32},{96,64},{128,96},{160,128},{192,160},{224,1... | collective-permute-start | bytes 983048 | tf_op jit(solution)/shard_map/ppermute | solution.py:571
  30.3 0.7 copy-start.3
  30.3 0.8 copy-start.4
  34.6 29.5 %all-to-all-start.1 = ((bf16[16,3,160,128]{3,2,1,0:T(8,128)(2,1)}), bf16[16,3,160,128]{3,2,1,0:T(8,128)(2,1)S(1)}, u32[]{:S(2)}, u32[]{:S(2)}) async-start(bf16[16,3,160,128]{3,2,1,0:T(8,128)(2,1)} %build.2), calls=%async_computation.1 | async-start | bytes 3932160 | tf_op jit(solution)/shard_map/all_to_all | solution.py:575
  39.6 188.4 %reduce-scatter.2.cloned.1.call-start = ((), (), s32[]{:S(2)}) async-start(), calls=%async_computation.7 | async-start | bytes 2949120 | tf_op jit(solution)/shard_map/reduce_scatter | solution.py:582
  64.1 47.5 %copy-start = (bf16[16,3,160,128]{3,2,1,0:T(8,128)(2,1)}, bf16[16,3,160,128]{3,2,1,0:T(8,128)(2,1)S(1)}, u32[]{:S(2)}) copy-start(bf16[16,3,160,128]{3,2,1,0:T(8,128)(2,1)S(1)} %all-to-all-done.1.near_hbm) | copy-start | bytes 5898244
  184.7 1.3 copy-start.2
  209.4 14.4 %all-to-all-start.5 = ((bf16[16,1,160,128]{3,2,1,0:T(8,128)(2,1)}), bf16[16,1,160,128]{3,2,1,0:T(8,128)(2,1)S(1)}, u32[]{:S(2)}, u32[]{:S(2)}) async-start(bf16[16,1,160,128]{3,2,1,0:T(8,128)(2,1)} %bitcast.7), calls=%async_computation.5 | async-start | bytes 1310720 | tf_op jit(solution)/shard_map/all_to_all | solution.py:587
  214.2 13.7 %collective-permute-start.2 = (bf16[8,160,128]{2,1,0:T(8,128)(2,1)}, bf16[8,160,128]{2,1,0:T(8,128)(2,1)S(1)}, u32[]{:S(2)}, u32[]{:S(2)}) collective-permute-start(bf16[8,160,128]{2,1,0:T(8,128)(2,1)} %get-tuple-element.29), channel_id=1, source_target_pairs={{0,32},{32,64},{64,96},{96,128},{128,160},{160,192},{192,224},{224... | collective-permute-start | bytes 983048 | tf_op jit(solution)/shard_map/ppermute | solution.py:585
  214.2 13.7 %collective-permute-start.3 = (bf16[8,160,128]{2,1,0:T(8,128)(2,1)}, bf16[8,160,128]{2,1,0:T(8,128)(2,1)S(1)}, u32[]{:S(2)}, u32[]{:S(2)}) collective-permute-start(bf16[8,160,128]{2,1,0:T(8,128)(2,1)} %get-tuple-element.30), channel_id=1, source_target_pairs={{0,224},{32,0},{64,32},{96,64},{128,96},{160,128},{192,160},{224,1... | collective-permute-start | bytes 983048 | tf_op jit(solution)/shard_map/ppermute | solution.py:586
  223.8 0.9 copy-start.1
  228.0 0.7 copy-start.5
  228.0 0.8 copy-start.6
Sparse Core Ops, SparseCore 0:
  9.8 45.2 all-gather.2
  184.8 43.1 reduce-scatter.1

commit v5 on v4

--- a/solution.py
+++ b/solution.py
@@ -45,7 +45,7 @@
     )(keys_t, values)
 
 
-def build_kernel(first, z_ref, req_ref, *refs):
+def build_kernel(first, req_ref, *refs):
     tables, out_hbm = refs[: (len(refs) - 3) // 2], refs[(len(refs) - 3) // 2]
     held, (load_sems, sems) = refs[-2 - len(tables) : -2], refs[-2:]
     plane, count = out_hbm.shape[:2]
@@ -56,27 +56,22 @@
         load.start()
     sends = []
     for d in range(count):
-        if d < len(loads):
-            loads[d].wait()
+        loads[d].wait()
         for c in range(plane):
             r = jnp.maximum(req_ref[c, first + d], 1) - 1
-            if len(held) > 1:
-                block = held[d].at[r]
-            else:
-                block = held[0].at[(z_ref[0] + d + 2) % held[0].shape[0], r]
-            sends.append(pltpu.make_async_copy(block, out_hbm.at[c, d], sems.at[c, d]))
+            sends.append(pltpu.make_async_copy(held[d].at[r], out_hbm.at[c, d], sems.at[c, d]))
             sends[-1].start()
     for send in sends:
         send.wait()
 
 
-def build(first, count, z, req, *tables):
-    plane = req.shape[0]
+def build(first, req, *tables):
+    plane, count = req.shape[0], len(tables)
     anywhere = pl.BlockSpec(memory_space=pl.ANY)
     return pl.pallas_call(
         functools.partial(build_kernel, first),
         grid_spec=pltpu.PrefetchScalarGridSpec(
-            num_scalar_prefetch=2,
+            num_scalar_prefetch=1,
             grid=(1,),
             in_specs=[anywhere] * len(tables),
             out_specs=anywhere,
@@ -86,7 +81,7 @@
         out_shape=jax.ShapeDtypeStruct((plane, count, ROWS, 128), BF),
         compiler_params=params(),
         name="build",
-    )(z, req, *tables)
+    )(req, *tables)
 
 
 def sum_blocks(first, req_ref, ret_hbm, buf, acc, staged, in_sems, out_sems, target):
@@ -108,39 +103,10 @@
     return stores
 
 
-def sum_near_kernel(first, req_ref, ret_hbm, *refs):
+def sum_kernel(first, req_ref, ret_hbm, *refs):
     outs, (buf, acc, staged, in_sems, out_sems) = refs[:-5], refs[-5:]
     for store in sum_blocks(
         first, req_ref, ret_hbm, buf, acc, staged, in_sems, out_sems, lambda d: outs[d]
-    ):
-        store.wait()
-
-
-def sum_far_kernel(
-    z_ref, req_ref, ret_hbm, out_hbm, buf, acc, staged, in_sems, out_sems
-):
-    depth, count = out_hbm.shape[0], ret_hbm.shape[1]
-    near = depth - count
-    z = z_ref[0]
-    staged[count] = jnp.zeros_like(staged[count])
-    zeros = [
-        pltpu.make_async_copy(
-            staged.at[count], out_hbm.at[(z + depth + i - 1) % depth], out_sems.at[count + i]
-        )
-        for i in range(near)
-    ]
-    for zero in zeros:
-        zero.start()
-    for store in zeros + sum_blocks(
-        near,
-        req_ref,
-        ret_hbm,
-        buf,
-        acc,
-        staged,
-        in_sems,
-        out_sems,
-        lambda d: out_hbm.at[(z + d + 2) % depth],
     ):
         store.wait()
 
@@ -155,11 +121,11 @@
     ]
 
 
-def sum_near(first, req, returned):
+def sum_returned(first, req, returned):
     plane, count = returned.shape[:2]
     anywhere = pl.BlockSpec(memory_space=pl.ANY)
     return pl.pallas_call(
-        functools.partial(sum_near_kernel, first),
+        functools.partial(sum_kernel, first),
         grid_spec=pltpu.PrefetchScalarGridSpec(
             num_scalar_prefetch=1,
             grid=(1,),
@@ -169,26 +135,8 @@
         ),
         out_shape=[jax.ShapeDtypeStruct((LOCAL, ROWS, 128), BF)] * count,
         compiler_params=params(),
-        name="sum_near",
+        name="sum_returned",
     )(req, returned)
-
-
-def sum_far(depth, z, req, returned):
-    plane, count = returned.shape[:2]
-    anywhere = pl.BlockSpec(memory_space=pl.ANY)
-    return pl.pallas_call(
-        sum_far_kernel,
-        grid_spec=pltpu.PrefetchScalarGridSpec(
-            num_scalar_prefetch=2,
-            grid=(1,),
-            in_specs=[anywhere],
-            out_specs=anywhere,
-            scratch_shapes=sum_scratch(plane, count, depth),
-        ),
-        out_shape=jax.ShapeDtypeStruct((depth, LOCAL, ROWS, 128), BF),
-        compiler_params=params(),
-        name="sum_far",
-    )(z, req, returned)
 
 
 def finish_kernel(own_ref, *refs):
@@ -540,6 +488,14 @@
     )
 
 
+def pass_on(terms, perm):
+    total = lax.ppermute(terms[0], "z", perm)
+    for term in terms[1:]:
+        total = (total.astype(F32) + term.astype(F32)).astype(BF)
+        total = lax.ppermute(total, "z", perm)
+    return total
+
+
 def shards(depth, plane, queries, keys, values, selected, d_out):
     me = lax.axis_index(("z", "y", "x"))
     z = lax.axis_index("z")
@@ -565,27 +521,29 @@
     )
     up = [(i, (i + 1) % depth) for i in range(depth)]
     down = [(i, (i - 1) % depth) for i in range(depth)]
-    where_z = z.reshape(1).astype(jnp.int32)
 
     local = pack(keys.T, values)
-    above = lax.ppermute(local, "z", down)
-    below = lax.ppermute(local, "z", up)
+    above, below = [local], [local]
+    for _ in range(depth // 2):
+        above.append(lax.ppermute(above[-1], "z", down))
+    for _ in range(depth - 1 - depth // 2):
+        below.append(lax.ppermute(below[-1], "z", up))
     asked = exchange(wanted.reshape(plane, 1, depth)).reshape(plane, depth)
-    column = lax.all_gather(local, "z")
-    near = exchange(build(0, 3, where_z, asked, local, above, below))
-    far = exchange(build(3, depth - 3, where_z, asked, column))
+    near = exchange(build(0, asked, local, above[1], below[1]))
+    far = exchange(build(3, asked, *above[2:], *below[:1:-1]))
     attended, d_queries, part_here, part_side, part_far, own = attend(
         src, queries, d_out, local, near, far
     )
-    far_sums = sum_far(depth, where_z, asked, exchange(part_far.reshape(far.shape)))
-    far_sums, part_side = lax.optimization_barrier((far_sums, part_side))
-    mine = lax.psum_scatter(far_sums, "z", scatter_dimension=0)
-    to_above, to_below = sum_near(1, asked, exchange(part_side))
-    to_above, to_below, part_here = lax.optimization_barrier((to_above, to_below, part_here))
-    from_below = lax.ppermute(to_above, "z", up)
-    from_above = lax.ppermute(to_below, "z", down)
-    (here,) = sum_near(0, asked, exchange(part_here[:, None]))
-    d_keys_t, d_values = finish(own, here, from_below, from_above, mine)
+    far_sums = sum_returned(3, asked, exchange(part_far.reshape(far.shape)))
+    *far_sums, part_side = lax.optimization_barrier((*far_sums, part_side))
+    n_above = depth // 2 - 1
+    to_above, to_below = far_sums[:n_above][::-1], far_sums[n_above:]
+    side_above, side_below = sum_returned(1, asked, exchange(part_side))
+    *sides, part_here = lax.optimization_barrier((side_above, side_below, part_here))
+    rising = pass_on(to_above + sides[:1], up)
+    falling = pass_on(to_below + sides[1:], down)
+    (here,) = sum_returned(0, asked, exchange(part_here[:, None]))
+    d_keys_t, d_values = finish(own, here, rising, falling)
     return attended, d_queries, d_keys_t.T, d_values
 
 

time: 239 us -> 227 us (0.950)
  blocking collectives: 124 us -> 96 us
  starting transfers between devices: 19.1 us -> 40.5 us
  between operations: 14.1 us -> 0.93 us
  waiting for transfers between devices: 26.4 us -> 33.8 us
    all_to_all x3 -> x2, blocking collectives: 111 us -> 82.6 us  [the longest x1 42.6 us: shards(): far = exchange(build(3, asked, *above[2:], *below[:1:-1]))]
    ppermute x4 -> x14, waiting for transfers between devices: 0.49 us -> 28.8 us  [the longest x4 15.8 us: shards(): above.append(lax.ppermute(above[-1], 'z', down))]
    all_gather x1 -> x0, waiting for transfers between devices: 15.4 us -> none  [shards(): column = lax.all_gather(local, 'z')]
    ppermute x4 -> x14, starting transfers between devices: 9.25 us -> 24.6 us  [the longest x4 11.8 us: shards(): above.append(lax.ppermute(above[-1], 'z', down))]
    all_to_all x2 -> x3, starting transfers between devices: 9.81 us -> 15.9 us  [the longest x1 5.89 us: shards(): here, = sum_returned(0, asked, exchange(part_here[:, None]))]
    all_to_all x2 -> x3, waiting for transfers between devices: 10.4 us -> 4.93 us  [the longest x1 4.92 us: shards(): here, = sum_returned(0, asked, exchange(part_here[:, None]))]
  transfers between devices with their start and end apart: 8 -> 17, of which waited for: 4 -> 6; matrix products, arithmetic and copies ran while one was open for 1% -> 1% of each run, Pallas kernels for 6% -> 4%
where the time goes in v5:
time: 227 us; the launch traced here: 226 us
  blocking collectives  96 us (42%)
  Pallas kernels  47.3 us (21%)
  starting transfers between devices  40.5 us (18%)
  waiting for transfers between devices  33.8 us (15%)
  local copies, waits for them, and re-layouts  4.6 us (2%)
  other arithmetic  2.85 us (1%)
    all_to_all x1, blocking collectives, shards(): far = exchange(build(3, asked, *above[2:], *below[:1:-1]))  42.6 us
    all_to_all x1, blocking collectives, shards(): far_sums = sum_returned(3, asked, exchange(part_far.reshape(far.shape)))  40 us
    pallas_call x1, Pallas kernels, attend(): pl.pallas_call(attend_kernel, grid_spec=pltpu.PrefetchScalarGridSpec(num_...  25.6 us
    ppermute x4, waiting for transfers between devices, shards(): above.append(lax.ppermute(above[-1], 'z', down))  15.8 us
    all_to_all x1, blocking collectives, shards(): asked = exchange(wanted.reshape(plane, 1, depth)).reshape(plane, depth)  13.4 us
    ppermute x4, starting transfers between devices, shards(): above.append(lax.ppermute(above[-1], 'z', down))  11.8 us
    pallas_call x3, Pallas kernels, sum_returned(): pl.pallas_call(functools.partial(sum_kernel, first), grid_spec=pltpu.Pref...  9.61 us
    pallas_call x2, Pallas kernels, build(): pl.pallas_call(functools.partial(build_kernel, first), grid_spec=pltpu.Pr...  7.78 us
  transfers between devices with their start and end apart: 17, of which 6 were waited for; matrix products, arithmetic and copies ran while one was open for 1% of the time, Pallas kernels for 4%

profile of v5, /device:TPU:2, one launch (start us, length us, event | category | flops | bytes accessed | tf_op | source)
XLA Modules:
  0.0 225.9 jit_solution(8965373179734670861)
XLA Ops:
  0.6 1.9 pack.1.refs_0_.local_hbm
  2.5 1.9 collective-permute-start.1
  4.5 3.9 %collective-permute-start = (bf16[8,160,128]{2,1,0:T(8,128)(2,1)}, bf16[8,160,128]{2,1,0:T(8,128)(2,1)S(1)}, u32[]{:S(2)}, u32[]{:S(2)}) collective-permute-start(bf16[8,160,128]{2,1,0:T(8,128)(2,1)} %pack.1.refs_0_.local_hbm), channel_id=1, source_target_pairs={{0,224},{32,0},{64,32},{96,64},{128,96},{160,128},{192,160},{224,1... | collective-permute-start | bytes 983048 | tf_op jit(solution)/shard_map/ppermute | solution.py:528
  8.4 1.3 add_select_fusion.5
  9.7 0.1 eq.24
  9.8 0.1 add.93
  9.9 0.1 select_reduce_fusion
  10.0 0.1 reshape.30
  10.1 13.4 %all_to_all.30 = s32[16,1,8]{2,1,0:T(1,128)} all-to-all(s32[16,1,8]{2,1,0:T(1,128)S(1)} %bitcast.15), channel_id=1, replica_groups=mesh['z'=8,'y'=4,'x'=4,'grp'=2] {'y','x'}, dimensions={0} | all-to-all | bytes 1024 | tf_op jit(solution)/shard_map/all_to_all | solution.py:531
  23.5 0.0 collective-permute-done.1.refs_2_
  23.5 0.0 collective-permute-done.refs_1_
  23.5 0.0 copy-start.16
  23.5 0.7 copy-done.14
  24.2 0.1 copy-done.16
  24.3 3.5 %build.2 = bf16[16,3,160,128]{3,2,1,0:T(8,128)(2,1)} custom-call(s32[16,8]{1,0:T(8,128)} %bitcast.9, bf16[8,160,128]{2,1,0:T(8,128)(2,1)} %pack.1.refs_0_.local_hbm, bf16[8,160,128]{2,1,0:T(8,128)(2,1)} %copy-done.16, bf16[8,160,128]{2,1,0:T(8,128)(2,1)} %copy-done.14), custom_call_target="tpu_custom_call" | custom-call | tf_op jit(solution)/shard_map/build/pallas_call | solution.py:71
  27.9 0.0 copy-start.17
  27.9 0.0 copy-start.15
  27.9 5.1 %all-to-all-start.1 = ((bf16[16,3,160,128]{3,2,1,0:T(8,128)(2,1)}), bf16[16,3,160,128]{3,2,1,0:T(8,128)(2,1)S(1)}, u32[]{:S(2)}, u32[]{:S(2)}) async-start(bf16[16,3,160,128]{3,2,1,0:T(8,128)(2,1)} %build.2), calls=%async_computation.1 | async-start | bytes 3932160 | tf_op jit(solution)/shard_map/all_to_all | solution.py:532
  33.0 2.1 collective-permute-start.2
  35.1 0.0 collective-permute-start.5
  35.1 5.8 %collective-permute-done.2.refs_0_ = bf16[8,160,128]{2,1,0:T(8,128)(2,1)S(1)} collective-permute-done((bf16[8,160,128]{2,1,0:T(8,128)(2,1)S(1)}, bf16[8,160,128]{2,1,0:T(8,128)(2,1)S(1)}, u32[]{:S(2)}, u32[]{:S(2)}) %collective-permute-start.2) | collective-permute-done | bytes 327712 | tf_op jit(solution)/shard_map/ppermute | solution.py:528
  41.0 2.7 %collective-permute-start.3 = (bf16[8,160,128]{2,1,0:T(8,128)(2,1)S(1)}, bf16[8,160,128]{2,1,0:T(8,128)(2,1)S(1)}, u32[]{:S(2)}, u32[]{:S(2)}) collective-permute-start(bf16[8,160,128]{2,1,0:T(8,128)(2,1)S(1)} %collective-permute-done.2.refs_0_), channel_id=1, source_target_pairs={{0,224},{32,0},{64,32},{96,64},{128,96},{160,128},{192,160},{224,1... | collective-permute-start | bytes 983048 | tf_op jit(solution)/shard_map/ppermute | solution.py:528
  43.7 0.0 collective-permute-done.5.refs_4_
  43.7 0.0 collective-permute-start.6
  43.7 5.4 %collective-permute-done.3.refs_1_ = bf16[8,160,128]{2,1,0:T(8,128)(2,1)S(1)} collective-permute-done((bf16[8,160,128]{2,1,0:T(8,128)(2,1)S(1)}, bf16[8,160,128]{2,1,0:T(8,128)(2,1)S(1)}, u32[]{:S(2)}, u32[]{:S(2)}) %collective-permute-start.3) | collective-permute-done | bytes 327712 | tf_op jit(solution)/shard_map/ppermute | solution.py:528
  49.1 3.0 %collective-permute-start.4 = (bf16[8,160,128]{2,1,0:T(8,128)(2,1)S(1)}, bf16[8,160,128]{2,1,0:T(8,128)(2,1)S(1)}, u32[]{:S(2)}, u32[]{:S(2)}) collective-permute-start(bf16[8,160,128]{2,1,0:T(8,128)(2,1)S(1)} %collective-permute-done.3.refs_1_), channel_id=1, source_target_pairs={{0,224},{32,0},{64,32},{96,64},{128,96},{160,128},{192,160},{224,1... | collective-permute-start | bytes 983048 | tf_op jit(solution)/shard_map/ppermute | solution.py:528
  52.1 0.0 collective-permute-done.6.refs_3_
  52.1 4.6 %collective-permute-done.4.refs_2_ = bf16[8,160,128]{2,1,0:T(8,128)(2,1)S(1)} collective-permute-done((bf16[8,160,128]{2,1,0:T(8,128)(2,1)S(1)}, bf16[8,160,128]{2,1,0:T(8,128)(2,1)S(1)}, u32[]{:S(2)}, u32[]{:S(2)}) %collective-permute-start.4) | collective-permute-done | bytes 327712 | tf_op jit(solution)/shard_map/ppermute | solution.py:528
  56.7 0.7 copy-done.7
  57.5 4.3 %build.3 = bf16[16,5,160,128]{3,2,1,0:T(8,128)(2,1)} custom-call(s32[16,8]{1,0:T(8,128)} %bitcast.10, bf16[8,160,128]{2,1,0:T(8,128)(2,1)} %copy-done.3, bf16[8,160,128]{2,1,0:T(8,128)(2,1)} %copy-done.5, bf16[8,160,128]{2,1,0:T(8,128)(2,1)} %copy-done.7, bf16[8,160,128]{2,1,0:T(8,128)(2,1)} %copy-done.6, bf16[8,160,128]{2,1,0:T(8,128)(2,1)} %copy-done.4), custom_call_target="tpu_custom_call" | custom-call | tf_op jit(solution)/shard_map/build/pallas_call | solution.py:71
  61.7 0.0 all-to-all-done.1.near_hbm
  61.7 42.6 %all_to_all.31 = bf16[16,5,160,128]{3,2,1,0:T(8,128)(2,1)} all-to-all(bf16[16,5,160,128]{3,2,1,0:T(8,128)(2,1)} %build.3), channel_id=1, replica_groups=mesh['z'=8,'y'=4,'x'=4,'grp'=2] {'y','x'}, dimensions={0} | all-to-all | bytes 6553600 | tf_op jit(solution)/shard_map/all_to_all | solution.py:533
  104.4 25.6 %attend.1 = (bf16[512,1024]{1,0:T(8,128)(2,1)}, bf16[512,1536]{1,0:T(8,128)(2,1)}, bf16[16,160,128]{2,1,0:T(8,128)(2,1)}, bf16[16,2,160,128]{3,2,1,0:T(8,128)(2,...) custom-call(s32[8,16]{1,0:T(8,128)} %get-tuple-element.54.src_ref, bf16[512,1536]{1,0:T(8,128)(2,1)} %q_ref.1, ...), custom_call_target="tpu_custom_call" | custom-call | tf_op jit(solution)/shard_map/attend/pallas_call | solution.py:437
  130.0 40.0 %all_to_all.32.ret_hbm = bf16[16,5,160,128]{3,2,1,0:T(8,128)(2,1)} all-to-all(bf16[16,5,160,128]{3,2,1,0:T(8,128)(2,1)} %bitcast.8), channel_id=1, replica_groups=mesh['z'=8,'y'=4,'x'=4,'grp'=2] {'y','x'}, dimensions={0} | all-to-all | bytes 6553600 | tf_op jit(solution)/shard_map/all_to_all | solution.py:537
  170.0 3.7 %sum_returned.3 = (bf16[8,160,128]{2,1,0:T(8,128)(2,1)}, bf16[8,160,128]{2,1,0:T(8,128)(2,1)}, bf16[8,160,128]{2,1,0:T(8,128)(2,1)}, bf16[8,160,128]{2,1,0:T(8,128)(2,1)}, bf16[8,160,128]{2,1,0:T(8,128)(2,1)}) custom-call(s32[16,8]{1,0:T(8,128)} %bitcast.11, bf16[16,5,160,128]{3,2,1,0:T(8,128)(2,1)} %all_to_all.32.ret_hbm), custom_call_target="tpu_custom_call" | custom-call | tf_op jit(solution)/shard_map/sum_returned/pallas_call | solution.py:127
  173.8 0.6 collective-permute-start.7
  174.4 4.9 %all-to-all-start.4 = ((bf16[16,2,160,128]{3,2,1,0:T(8,128)(2,1)}), bf16[16,2,160,128]{3,2,1,0:T(8,128)(2,1)S(1)}, u32[]{:S(2)}, u32[]{:S(2)}) async-start(bf16[16,2,160,128]{3,2,1,0:T(8,128)(2,1)} %get-tuple-element.38), calls=%async_computation.4 | async-start | bytes 2621440 | tf_op jit(solution)/shard_map/all_to_all | solution.py:541
  179.3 6.0 %collective-permute-done.7 = bf16[8,160,128]{2,1,0:T(8,128)(2,1)S(1)} collective-permute-done((bf16[8,160,128]{2,1,0:T(8,128)(2,1)}, bf16[8,160,128]{2,1,0:T(8,128)(2,1)S(1)}, u32[]{:S(2)}, u32[]{:S(2)}) %collective-permute-start.7) | collective-permute-done | bytes 327712 | tf_op jit(solution)/shard_map/ppermute | solution.py:492
  185.3 0.1 add_convert_fusion.4
  185.4 0.3 collective-permute-start.8
  185.7 3.2 %collective-permute-start.11 = (bf16[8,160,128]{2,1,0:T(8,128)(2,1)S(1)}, bf16[8,160,128]{2,1,0:T(8,128)(2,1)S(1)}, u32[]{:S(2)}, u32[]{:S(2)}) collective-permute-start(bf16[8,160,128]{2,1,0:T(8,128)(2,1)S(1)} %copy-done.18), channel_id=1, source_target_pairs={{0,224},{32,0},{64,32},{96,64},{128,96},{160,128},{192,160},{224,1... | collective-permute-start | bytes 983048 | tf_op jit(solution)/shard_map/ppermute | solution.py:492
  188.9 7.0 %collective-permute-done.8 = bf16[8,160,128]{2,1,0:T(8,128)(2,1)S(1)} collective-permute-done((bf16[8,160,128]{2,1,0:T(8,128)(2,1)S(1)}, bf16[8,160,128]{2,1,0:T(8,128)(2,1)S(1)}, u32[]{:S(2)}, u32[]{:S(2)}) %collective-permute-start.8) | collective-permute-done | bytes 327712 | tf_op jit(solution)/shard_map/ppermute | solution.py:495
  195.9 0.1 add_convert_fusion.3
  196.0 0.1 collective-permute-start.9
  196.1 0.0 collective-permute-done.11
  196.1 0.1 add_convert_fusion.1
  196.2 3.3 %collective-permute-start.12 = (bf16[8,160,128]{2,1,0:T(8,128)(2,1)S(1)}, bf16[8,160,128]{2,1,0:T(8,128)(2,1)S(1)}, u32[]{:S(2)}, u32[]{:S(2)}) collective-permute-start(bf16[8,160,128]{2,1,0:T(8,128)(2,1)S(1)} %add_convert_fusion.1), channel_id=1, source_target_pairs={{0,224},{32,0},{64,32},{96,64},{128,96},{160,128},{192,160},{224,1... | collective-permute-start | bytes 983048 | tf_op jit(solution)/shard_map/ppermute | solution.py:495
  199.5 0.0 all-to-all-done.4.ret_hbm
  199.5 1.1 copy-done.1
  200.6 3.1 %sum_returned.4 = (bf16[8,160,128]{2,1,0:T(8,128)(2,1)}, bf16[8,160,128]{2,1,0:T(8,128)(2,1)}) custom-call(s32[16,8]{1,0:T(8,128)} %bitcast.12, bf16[16,2,160,128]{3,2,1,0:T(8,128)(2,1)} %copy-done.1), custom_call_target="tpu_custom_call" | custom-call | tf_op jit(solution)/shard_map/sum_returned/pallas_call | solution.py:127
  203.7 5.9 %all-to-all-start.5 = ((bf16[16,1,160,128]{3,2,1,0:T(8,128)(2,1)}), bf16[16,1,160,128]{3,2,1,0:T(8,128)(2,1)S(1)}, u32[]{:S(2)}, u32[]{:S(2)}) async-start(bf16[16,1,160,128]{3,2,1,0:T(8,128)(2,1)} %bitcast.5), calls=%async_computation.5 | async-start | bytes 1310720 | tf_op jit(solution)/shard_map/all_to_all | solution.py:545
  209.5 0.0 collective-permute-done.9
  209.5 1.1 add_convert_fusion.2
  210.6 0.1 collective-permute-start.10
  210.7 0.0 collective-permute-done.12
  210.7 0.1 add_convert_fusion
  210.8 3.3 %collective-permute-start.13 = (bf16[8,160,128]{2,1,0:T(8,128)(2,1)S(1)}, bf16[8,160,128]{2,1,0:T(8,128)(2,1)S(1)}, u32[]{:S(2)}, u32[]{:S(2)}) collective-permute-start(bf16[8,160,128]{2,1,0:T(8,128)(2,1)S(1)} %add_convert_fusion), channel_id=1, source_target_pairs={{0,224},{32,0},{64,32},{96,64},{128,96},{160,128},{192,160},{224,1... | collective-permute-start | bytes 983048 | tf_op jit(solution)/shard_map/ppermute | solution.py:495
  214.1 4.9 %all-to-all-done.5.ret_hbm = bf16[16,1,160,128]{3,2,1,0:T(8,128)(2,1)S(1)} async-done(((bf16[16,1,160,128]{3,2,1,0:T(8,128)(2,1)}), bf16[16,1,160,128]{3,2,1,0:T(8,128)(2,1)S(1)}, u32[]{:S(2)}, u32[]{:S(2)}) %all-to-all-start.5) | async-done | bytes 655392 | tf_op jit(solution)/shard_map/all_to_all | solution.py:545
  219.0 0.8 copy-done.2
  219.9 2.8 %sum_returned.5.refs_0_ = bf16[8,160,128]{2,1,0:T(8,128)(2,1)} custom-call(s32[16,8]{1,0:T(8,128)} %bitcast.13, bf16[16,1,160,128]{3,2,1,0:T(8,128)(2,1)} %copy-done.2), custom_call_target="tpu_custom_call" | custom-call | tf_op jit(solution)/shard_map/sum_returned/pallas_call | solution.py:127
  222.7 0.0 collective-permute-done.13.refs_2_
  222.8 0.7 copy-done.10
  223.5 0.1 copy-done.12
  223.6 2.3 %finish.1 = (bf16[192,512]{1,0:T(8,128)(2,1)}, bf16[512,128]{1,0:T(8,128)(2,1)}) custom-call(f32[8,160,128]{2,1,0:T(8,128)} %get-tuple-element.30.own_ref, bf16[8,160,128]{2,1,0:T(8,128)(2,1)} %sum_returned.5.refs_0_, bf16[8,160,128]{2,1,0:T(8,128)(2,1)} %copy-done.10, bf16[8,160,128]{2,1,0:T(8,128)(2,1)} %copy-done.12), custom_call_target="tpu_custom_call" | custom-call | tf_op jit(solution)/shard_map/finish/pallas_call | solution.py:159
  (29 shorter events, 0.1 us)
Async XLA Ops:
  2.5 21.0 %collective-permute-start.1 = (bf16[8,160,128]{2,1,0:T(8,128)(2,1)}, bf16[8,160,128]{2,1,0:T(8,128)(2,1)S(1)}, u32[]{:S(2)}, u32[]{:S(2)}) collective-permute-start(bf16[8,160,128]{2,1,0:T(8,128)(2,1)} %pack.1.refs_0_.local_hbm), channel_id=1, source_target_pairs={{0,32},{32,64},{64,96},{96,128},{128,160},{160,192},{192,224},{224... | collective-permute-start | bytes 983048 | tf_op jit(solution)/shard_map/ppermute | solution.py:530
  4.5 19.0 %collective-permute-start = (bf16[8,160,128]{2,1,0:T(8,128)(2,1)}, bf16[8,160,128]{2,1,0:T(8,128)(2,1)S(1)}, u32[]{:S(2)}, u32[]{:S(2)}) collective-permute-start(bf16[8,160,128]{2,1,0:T(8,128)(2,1)} %pack.1.refs_0_.local_hbm), channel_id=1, source_target_pairs={{0,224},{32,0},{64,32},{96,64},{128,96},{160,128},{192,160},{224,1... | collective-permute-start | bytes 983048 | tf_op jit(solution)/shard_map/ppermute | solution.py:528
  23.5 0.7 copy-start.14
  23.5 0.8 copy-start.16
  27.9 5.1 %copy-start.17 = (bf16[8,160,128]{2,1,0:T(8,128)(2,1)S(1)}, bf16[8,160,128]{2,1,0:T(8,128)(2,1)}, u32[]{:S(2)}) copy-start(bf16[8,160,128]{2,1,0:T(8,128)(2,1)} %copy-done.16) | copy-start | bytes 983044
  27.9 7.2 %copy-start.15 = (bf16[8,160,128]{2,1,0:T(8,128)(2,1)S(1)}, bf16[8,160,128]{2,1,0:T(8,128)(2,1)}, u32[]{:S(2)}) copy-start(bf16[8,160,128]{2,1,0:T(8,128)(2,1)} %copy-done.14) | copy-start | bytes 983044
  27.9 33.8 %all-to-all-start.1 = ((bf16[16,3,160,128]{3,2,1,0:T(8,128)(2,1)}), bf16[16,3,160,128]{3,2,1,0:T(8,128)(2,1)S(1)}, u32[]{:S(2)}, u32[]{:S(2)}) async-start(bf16[16,3,160,128]{3,2,1,0:T(8,128)(2,1)} %build.2), calls=%async_computation.1 | async-start | bytes 3932160 | tf_op jit(solution)/shard_map/all_to_all | solution.py:532
  33.0 7.9 %collective-permute-start.2 = (bf16[8,160,128]{2,1,0:T(8,128)(2,1)S(1)}, bf16[8,160,128]{2,1,0:T(8,128)(2,1)S(1)}, u32[]{:S(2)}, u32[]{:S(2)}) collective-permute-start(bf16[8,160,128]{2,1,0:T(8,128)(2,1)S(1)} %copy-done.17), channel_id=1, source_target_pairs={{0,224},{32,0},{64,32},{96,64},{128,96},{160,128},{192,160},{224,1... | collective-permute-start | bytes 983048 | tf_op jit(solution)/shard_map/ppermute | solution.py:528
  35.1 8.5 %collective-permute-start.5 = (bf16[8,160,128]{2,1,0:T(8,128)(2,1)S(1)}, bf16[8,160,128]{2,1,0:T(8,128)(2,1)S(1)}, u32[]{:S(2)}, u32[]{:S(2)}) collective-permute-start(bf16[8,160,128]{2,1,0:T(8,128)(2,1)S(1)} %copy-done.15), channel_id=1, source_target_pairs={{0,32},{32,64},{64,96},{96,128},{128,160},{160,192},{192,224},{224... | collective-permute-start | bytes 983048 | tf_op jit(solution)/shard_map/ppermute | solution.py:530
  41.0 15.8 %copy-start.3 = (bf16[8,160,128]{2,1,0:T(8,128)(2,1)}, bf16[8,160,128]{2,1,0:T(8,128)(2,1)S(1)}, u32[]{:S(2)}) copy-start(bf16[8,160,128]{2,1,0:T(8,128)(2,1)S(1)} %collective-permute-done.2.refs_0_) | copy-start | bytes 983044
  41.0 8.1 %collective-permute-start.3 = (bf16[8,160,128]{2,1,0:T(8,128)(2,1)S(1)}, bf16[8,160,128]{2,1,0:T(8,128)(2,1)S(1)}, u32[]{:S(2)}, u32[]{:S(2)}) collective-permute-start(bf16[8,160,128]{2,1,0:T(8,128)(2,1)S(1)} %collective-permute-done.2.refs_0_), channel_id=1, source_target_pairs={{0,224},{32,0},{64,32},{96,64},{128,96},{160,128},{192,160},{224,1... | collective-permute-start | bytes 983048 | tf_op jit(solution)/shard_map/ppermute | solution.py:528
  43.7 13.1 %copy-start.4 = (bf16[8,160,128]{2,1,0:T(8,128)(2,1)}, bf16[8,160,128]{2,1,0:T(8,128)(2,1)S(1)}, u32[]{:S(2)}) copy-start(bf16[8,160,128]{2,1,0:T(8,128)(2,1)S(1)} %collective-permute-done.5.refs_4_) | copy-start | bytes 983044
  43.7 8.5 %collective-permute-start.6 = (bf16[8,160,128]{2,1,0:T(8,128)(2,1)S(1)}, bf16[8,160,128]{2,1,0:T(8,128)(2,1)S(1)}, u32[]{:S(2)}, u32[]{:S(2)}) collective-permute-start(bf16[8,160,128]{2,1,0:T(8,128)(2,1)S(1)} %collective-permute-done.5.refs_4_), channel_id=1, source_target_pairs={{0,32},{32,64},{64,96},{96,128},{128,160},{160,192},{192,224},{224... | collective-permute-start | bytes 983048 | tf_op jit(solution)/shard_map/ppermute | solution.py:530
  49.1 7.6 %copy-start.5 = (bf16[8,160,128]{2,1,0:T(8,128)(2,1)}, bf16[8,160,128]{2,1,0:T(8,128)(2,1)S(1)}, u32[]{:S(2)}) copy-start(bf16[8,160,128]{2,1,0:T(8,128)(2,1)S(1)} %collective-permute-done.3.refs_1_) | copy-start | bytes 983044
  49.1 7.6 %collective-permute-start.4 = (bf16[8,160,128]{2,1,0:T(8,128)(2,1)S(1)}, bf16[8,160,128]{2,1,0:T(8,128)(2,1)S(1)}, u32[]{:S(2)}, u32[]{:S(2)}) collective-permute-start(bf16[8,160,128]{2,1,0:T(8,128)(2,1)S(1)} %collective-permute-done.3.refs_1_), channel_id=1, source_target_pairs={{0,224},{32,0},{64,32},{96,64},{128,96},{160,128},{192,160},{224,1... | collective-permute-start | bytes 983048 | tf_op jit(solution)/shard_map/ppermute | solution.py:528
  52.1 4.6 %copy-start.6 = (bf16[8,160,128]{2,1,0:T(8,128)(2,1)}, bf16[8,160,128]{2,1,0:T(8,128)(2,1)S(1)}, u32[]{:S(2)}) copy-start(bf16[8,160,128]{2,1,0:T(8,128)(2,1)S(1)} %collective-permute-done.6.refs_3_) | copy-start | bytes 983044
  56.7 0.7 copy-start.7
  61.7 42.7 %copy-start = (bf16[16,3,160,128]{3,2,1,0:T(8,128)(2,1)}, bf16[16,3,160,128]{3,2,1,0:T(8,128)(2,1)S(1)}, u32[]{:S(2)}) copy-start(bf16[16,3,160,128]{3,2,1,0:T(8,128)(2,1)S(1)} %all-to-all-done.1.near_hbm) | copy-start | bytes 5898244
  173.7 11.6 %copy-start.13 = (bf16[8,160,128]{2,1,0:T(8,128)(2,1)S(1)}, bf16[8,160,128]{2,1,0:T(8,128)(2,1)}, u32[]{:S(2)}) copy-start(bf16[8,160,128]{2,1,0:T(8,128)(2,1)} %get-tuple-element.44) | copy-start | bytes 983044
  173.7 12.0 %copy-start.18 = (bf16[8,160,128]{2,1,0:T(8,128)(2,1)S(1)}, bf16[8,160,128]{2,1,0:T(8,128)(2,1)}, u32[]{:S(2)}) copy-start(bf16[8,160,128]{2,1,0:T(8,128)(2,1)} %get-tuple-element.47) | copy-start | bytes 983044
  173.8 22.1 %copy-start.9 = (bf16[8,160,128]{2,1,0:T(8,128)(2,1)S(1)}, bf16[8,160,128]{2,1,0:T(8,128)(2,1)}, u32[]{:S(2)}) copy-start(bf16[8,160,128]{2,1,0:T(8,128)(2,1)} %get-tuple-element.45) | copy-start | bytes 983044
  173.8 22.3 %copy-start.8 = (bf16[8,160,128]{2,1,0:T(8,128)(2,1)S(1)}, bf16[8,160,128]{2,1,0:T(8,128)(2,1)}, u32[]{:S(2)}) copy-start(bf16[8,160,128]{2,1,0:T(8,128)(2,1)} %get-tuple-element.48) | copy-start | bytes 983044
  173.8 11.5 %collective-permute-start.7 = (bf16[8,160,128]{2,1,0:T(8,128)(2,1)}, bf16[8,160,128]{2,1,0:T(8,128)(2,1)S(1)}, u32[]{:S(2)}, u32[]{:S(2)}) collective-permute-start(bf16[8,160,128]{2,1,0:T(8,128)(2,1)} %get-tuple-element.43), channel_id=1, source_target_pairs={{0,32},{32,64},{64,96},{96,128},{128,160},{160,192},{192,224},{224... | collective-permute-start | bytes 983048 | tf_op jit(solution)/shard_map/ppermute | solution.py:492
  174.4 25.1 %all-to-all-start.4 = ((bf16[16,2,160,128]{3,2,1,0:T(8,128)(2,1)}), bf16[16,2,160,128]{3,2,1,0:T(8,128)(2,1)S(1)}, u32[]{:S(2)}, u32[]{:S(2)}) async-start(bf16[16,2,160,128]{3,2,1,0:T(8,128)(2,1)} %get-tuple-element.38), calls=%async_computation.4 | async-start | bytes 2621440 | tf_op jit(solution)/shard_map/all_to_all | solution.py:541
  185.4 10.5 %collective-permute-start.8 = (bf16[8,160,128]{2,1,0:T(8,128)(2,1)S(1)}, bf16[8,160,128]{2,1,0:T(8,128)(2,1)S(1)}, u32[]{:S(2)}, u32[]{:S(2)}) collective-permute-start(bf16[8,160,128]{2,1,0:T(8,128)(2,1)S(1)} %add_convert_fusion.4), channel_id=1, source_target_pairs={{0,32},{32,64},{64,96},{96,128},{128,160},{160,192},{192,224},{224... | collective-permute-start | bytes 983048 | tf_op jit(solution)/shard_map/ppermute | solution.py:495
  185.7 10.4 %collective-permute-start.11 = (bf16[8,160,128]{2,1,0:T(8,128)(2,1)S(1)}, bf16[8,160,128]{2,1,0:T(8,128)(2,1)S(1)}, u32[]{:S(2)}, u32[]{:S(2)}) collective-permute-start(bf16[8,160,128]{2,1,0:T(8,128)(2,1)S(1)} %copy-done.18), channel_id=1, source_target_pairs={{0,224},{32,0},{64,32},{96,64},{128,96},{160,128},{192,160},{224,1... | collective-permute-start | bytes 983048 | tf_op jit(solution)/shard_map/ppermute | solution.py:492
  196.0 13.6 %collective-permute-start.9 = (bf16[8,160,128]{2,1,0:T(8,128)(2,1)S(1)}, bf16[8,160,128]{2,1,0:T(8,128)(2,1)S(1)}, u32[]{:S(2)}, u32[]{:S(2)}) collective-permute-start(bf16[8,160,128]{2,1,0:T(8,128)(2,1)S(1)} %add_convert_fusion.3), channel_id=1, source_target_pairs={{0,32},{32,64},{64,96},{96,128},{128,160},{160,192},{192,224},{224... | collective-permute-start | bytes 983048 | tf_op jit(solution)/shard_map/ppermute | solution.py:495
  196.2 14.5 %collective-permute-start.12 = (bf16[8,160,128]{2,1,0:T(8,128)(2,1)S(1)}, bf16[8,160,128]{2,1,0:T(8,128)(2,1)S(1)}, u32[]{:S(2)}, u32[]{:S(2)}) collective-permute-start(bf16[8,160,128]{2,1,0:T(8,128)(2,1)S(1)} %add_convert_fusion.1), channel_id=1, source_target_pairs={{0,224},{32,0},{64,32},{96,64},{128,96},{160,128},{192,160},{224,1... | collective-permute-start | bytes 983048 | tf_op jit(solution)/shard_map/ppermute | solution.py:495
  199.5 1.1 copy-start.1
  203.6 7.1 %copy-start.11 = (bf16[8,160,128]{2,1,0:T(8,128)(2,1)S(1)}, bf16[8,160,128]{2,1,0:T(8,128)(2,1)}, u32[]{:S(2)}) copy-start(bf16[8,160,128]{2,1,0:T(8,128)(2,1)} %get-tuple-element.49) | copy-start | bytes 983044
  203.7 15.4 %all-to-all-start.5 = ((bf16[16,1,160,128]{3,2,1,0:T(8,128)(2,1)}), bf16[16,1,160,128]{3,2,1,0:T(8,128)(2,1)S(1)}, u32[]{:S(2)}, u32[]{:S(2)}) async-start(bf16[16,1,160,128]{3,2,1,0:T(8,128)(2,1)} %bitcast.5), calls=%async_computation.5 | async-start | bytes 1310720 | tf_op jit(solution)/shard_map/all_to_all | solution.py:545
  210.6 12.1 %collective-permute-start.10 = (bf16[8,160,128]{2,1,0:T(8,128)(2,1)S(1)}, bf16[8,160,128]{2,1,0:T(8,128)(2,1)S(1)}, u32[]{:S(2)}, u32[]{:S(2)}) collective-permute-start(bf16[8,160,128]{2,1,0:T(8,128)(2,1)S(1)} %add_convert_fusion.2), channel_id=1, source_target_pairs={{0,32},{32,64},{64,96},{96,128},{128,160},{160,192},{192,224},{224... | collective-permute-start | bytes 983048 | tf_op jit(solution)/shard_map/ppermute | solution.py:495
  210.8 11.9 %collective-permute-start.13 = (bf16[8,160,128]{2,1,0:T(8,128)(2,1)S(1)}, bf16[8,160,128]{2,1,0:T(8,128)(2,1)S(1)}, u32[]{:S(2)}, u32[]{:S(2)}) collective-permute-start(bf16[8,160,128]{2,1,0:T(8,128)(2,1)S(1)} %add_convert_fusion), channel_id=1, source_target_pairs={{0,224},{32,0},{64,32},{96,64},{128,96},{160,128},{192,160},{224,1... | collective-permute-start | bytes 983048 | tf_op jit(solution)/shard_map/ppermute | solution.py:495
  219.0 0.9 copy-start.2
  222.7 0.7 copy-start.10
  222.7 0.8 copy-start.12

commit v6 on v5

--- a/solution.py
+++ b/solution.py
@@ -40,7 +40,7 @@
     return pl.pallas_call(
         pack_kernel,
         out_shape=jax.ShapeDtypeStruct((LOCAL, ROWS, 128), BF),
-        compiler_params=params(),
+        compiler_params=params(16),
         name="pack",
     )(keys_t, values)
 
@@ -65,7 +65,7 @@
         send.wait()
 
 
-def build(first, req, *tables):
+def build(first, mib, req, *tables):
     plane, count = req.shape[0], len(tables)
     anywhere = pl.BlockSpec(memory_space=pl.ANY)
     return pl.pallas_call(
@@ -79,7 +79,7 @@
             + [pltpu.SemaphoreType.DMA((len(tables),)), pltpu.SemaphoreType.DMA((plane, count))],
         ),
         out_shape=jax.ShapeDtypeStruct((plane, count, ROWS, 128), BF),
-        compiler_params=params(),
+        compiler_params=params(mib),
         name="build",
     )(req, *tables)
 
@@ -134,19 +134,19 @@
             scratch_shapes=sum_scratch(plane, count, count),
         ),
         out_shape=[jax.ShapeDtypeStruct((LOCAL, ROWS, 128), BF)] * count,
-        compiler_params=params(),
+        compiler_params=params(16),
         name="sum_returned",
     )(req, returned)
 
 
-def finish_kernel(own_ref, *refs):
-    got_refs, (dk_ref, dv_ref) = refs[:-2], refs[-2:]
+def finish_kernel(req_ref, own_ref, ret_ref, rising_ref, falling_ref, dk_ref, dv_ref, acc):
+    acc[1:] = own_ref[...] + rising_ref[...].astype(F32) + falling_ref[...].astype(F32)
+    for c in range(ret_ref.shape[0]):
+        acc[req_ref[c, 0]] += ret_ref[c, 0].astype(F32)
     for b in range(0, LOCAL, 2):
         pair = []
         for i in range(b, b + 2):
-            total = own_ref[i]
-            for got_ref in got_refs:
-                total = total + got_ref[i].astype(F32)
+            total = acc[i + 1]
             dv_ref[i * BLK : (i + 1) * BLK, :] = total[0:BLK].astype(BF)
             low = total[2 * BLK :]
             low = jnp.concatenate([low[:, :64], low[:, 64:]], axis=0)
@@ -155,16 +155,24 @@
         dk_ref[:, b * BLK : (b + 2) * BLK] = jnp.transpose(pair).astype(BF)
 
 
-def finish(own, *got):
+def finish(req, own, returned, rising, falling):
+    def whole(dims):
+        return pl.BlockSpec(dims, lambda i, req: (0,) * len(dims))
+
+    outs = ((DK, LOCAL * BLK), (LOCAL * BLK, DV))
     return pl.pallas_call(
         finish_kernel,
-        out_shape=(
-            jax.ShapeDtypeStruct((DK, LOCAL * BLK), BF),
-            jax.ShapeDtypeStruct((LOCAL * BLK, DV), BF),
+        grid_spec=pltpu.PrefetchScalarGridSpec(
+            num_scalar_prefetch=1,
+            grid=(1,),
+            in_specs=[whole(x.shape) for x in (own, returned, rising, falling)],
+            out_specs=[whole(dims) for dims in outs],
+            scratch_shapes=[pltpu.VMEM((LOCAL + 1, ROWS, 128), F32)],
         ),
-        compiler_params=params(),
+        out_shape=[jax.ShapeDtypeStruct(dims, BF) for dims in outs],
+        compiler_params=params(16),
         name="finish",
-    )(own, *got)
+    )(req, own, returned, rising, falling)
 
 
 def dot(a, b, da, db):
@@ -529,8 +537,8 @@
     for _ in range(depth - 1 - depth // 2):
         below.append(lax.ppermute(below[-1], "z", up))
     asked = exchange(wanted.reshape(plane, 1, depth)).reshape(plane, depth)
-    near = exchange(build(0, asked, local, above[1], below[1]))
-    far = exchange(build(3, asked, *above[2:], *below[:1:-1]))
+    near = exchange(build(0, 16, asked, local, above[1], below[1]))
+    far = exchange(build(3, 56, asked, *above[2:], *below[:1:-1]))
     attended, d_queries, part_here, part_side, part_far, own = attend(
         src, queries, d_out, local, near, far
     )
@@ -542,8 +550,7 @@
     *sides, part_here = lax.optimization_barrier((side_above, side_below, part_here))
     rising = pass_on(to_above + sides[:1], up)
     falling = pass_on(to_below + sides[1:], down)
-    (here,) = sum_returned(0, asked, exchange(part_here[:, None]))
-    d_keys_t, d_values = finish(own, here, rising, falling)
+    d_keys_t, d_values = finish(asked, own, exchange(part_here[:, None]), rising, falling)
     return attended, d_queries, d_keys_t.T, d_values
 
 

time: 227 us -> 219 us (0.965)
  Pallas kernels: 47.3 us -> 38.8 us
    pallas_call x3 -> x2, Pallas kernels: 9.61 us -> 4 us  [sum_returned(): pl.pallas_call(functools.partial(sum_kernel, first), grid_spec=pltpu.Pref...]
    ppermute x5, waiting for transfers between devices: 6.98 us -> 11.9 us  [pass_on(): total = lax.ppermute(total, 'z', perm)]
    all_to_all x2, waiting for transfers between devices: 4.92 us -> 0.01 us  [the longest x1 0.01 us: shards(): exchange(part_here[:, None])]
  transfers between devices with their start and end apart: 17 -> 17, of which waited for: 6 -> 8; matrix products, arithmetic and copies ran while one was open for 1% -> 2% of each run, Pallas kernels for 4% -> 3%
where the time goes in v6:
time: 219 us; the launch traced here: 216 us
  blocking collectives  95.5 us (44%)
  starting transfers between devices  40.8 us (19%)
  Pallas kernels  38.8 us (18%)
  waiting for transfers between devices  33.3 us (15%)
  other arithmetic  3.85 us (2%)
  local copies, waits for them, and re-layouts  2.8 us (1%)
    all_to_all x1, blocking collectives, shards(): far = exchange(build(3, 56, asked, *above[2:], *below[:1:-1]))  42.7 us
    all_to_all x1, blocking collectives, shards(): far_sums = sum_returned(3, asked, exchange(part_far.reshape(far.shape)))  39.3 us
    pallas_call x1, Pallas kernels, attend(): pl.pallas_call(attend_kernel, grid_spec=pltpu.PrefetchScalarGridSpec(num_...  25.7 us
    ppermute x4, waiting for transfers between devices, shards(): above.append(lax.ppermute(above[-1], 'z', down))  16.1 us
    all_to_all x1, blocking collectives, shards(): asked = exchange(wanted.reshape(plane, 1, depth)).reshape(plane, depth)  13.5 us
    ppermute x5, waiting for transfers between devices, pass_on(): total = lax.ppermute(total, 'z', perm)  11.9 us
    ppermute x4, starting transfers between devices, shards(): above.append(lax.ppermute(above[-1], 'z', down))  11.1 us
    ppermute x5, starting transfers between devices, pass_on(): total = lax.ppermute(total, 'z', perm)  7.37 us
  transfers between devices with their start and end apart: 17, of which 8 were waited for; matrix products, arithmetic and copies ran while one was open for 2% of the time, Pallas kernels for 3%

profile of v6, /device:TPU:2, one launch (start us, length us, event | category | flops | bytes accessed | tf_op | source)
XLA Modules:
  0.0 215.8 jit_solution(8419318934183539849)
XLA Ops:
  0.6 0.0 copy-start.4
  0.6 0.9 copy-done.4
  1.6 0.9 copy-done.5
  2.5 0.2 pack.1.refs_0_.local_hbm
  2.7 0.0 copy-start
  2.7 2.0 collective-permute-start.1
  4.7 4.0 %collective-permute-start = (bf16[8,160,128]{2,1,0:T(8,128)(2,1)S(1)}, bf16[8,160,128]{2,1,0:T(8,128)(2,1)S(1)}, u32[]{:S(2)}, u32[]{:S(2)}) collective-permute-start(bf16[8,160,128]{2,1,0:T(8,128)(2,1)S(1)} %pack.1.refs_0_.local_hbm), channel_id=1, source_target_pairs={{0,224},{32,0},{64,32},{96,64},{128,96},{160,128},{192,160},{224,1... | collective-permute-start | bytes 983048 | tf_op jit(solution)/shard_map/ppermute | solution.py:536
  8.7 1.3 add_select_fusion.5
  10.0 0.1 eq.24
  10.1 0.1 add.93
  10.2 0.1 select_reduce_fusion
  10.3 0.1 reshape.30
  10.4 13.5 %all_to_all.30 = s32[16,1,8]{2,1,0:T(1,128)S(1)} all-to-all(s32[16,1,8]{2,1,0:T(1,128)S(1)} %bitcast.15), channel_id=1, replica_groups=mesh['z'=8,'y'=4,'x'=4,'grp'=2] {'y','x'}, dimensions={0} | all-to-all | bytes 1024 | tf_op jit(solution)/shard_map/all_to_all | solution.py:539
  23.8 0.0 collective-permute-done.1.refs_2_
  23.8 0.0 collective-permute-done.refs_1_
  23.9 2.7 %build.2 = bf16[16,3,160,128]{3,2,1,0:T(8,128)(2,1)} custom-call(s32[16,8]{1,0:T(8,128)S(1)} %bitcast.7, bf16[8,160,128]{2,1,0:T(8,128)(2,1)S(1)} %pack.1.refs_0_.local_hbm, bf16[8,160,128]{2,1,0:T(8,128)(2,1)S(1)} %collective-permute-done.refs_1_, bf16[8,160,128]{2,1,0:T(8,128)(2,1)S(1)} %collective-permute-done.1.refs_2_), custom_call_target="tpu_custom_call" | custom-call | tf_op jit(solution)/shard_map/build/pallas_call | solution.py:71
  26.6 5.6 %all-to-all-start.1 = ((bf16[16,3,160,128]{3,2,1,0:T(8,128)(2,1)}), bf16[16,3,160,128]{3,2,1,0:T(8,128)(2,1)}, u32[]{:S(2)}, u32[]{:S(2)}) async-start(bf16[16,3,160,128]{3,2,1,0:T(8,128)(2,1)} %build.2), calls=%async_computation.1 | async-start | bytes 3932160 | tf_op jit(solution)/shard_map/all_to_all | solution.py:540
  32.3 1.9 collective-permute-start.2
  34.2 0.1 collective-permute-start.5
  34.3 5.8 %collective-permute-done.2.refs_0_ = bf16[8,160,128]{2,1,0:T(8,128)(2,1)S(1)} collective-permute-done((bf16[8,160,128]{2,1,0:T(8,128)(2,1)S(1)}, bf16[8,160,128]{2,1,0:T(8,128)(2,1)S(1)}, u32[]{:S(2)}, u32[]{:S(2)}) %collective-permute-start.2) | collective-permute-done | bytes 327712 | tf_op jit(solution)/shard_map/ppermute | solution.py:536
  40.1 2.5 %collective-permute-start.3 = (bf16[8,160,128]{2,1,0:T(8,128)(2,1)S(1)}, bf16[8,160,128]{2,1,0:T(8,128)(2,1)S(1)}, u32[]{:S(2)}, u32[]{:S(2)}) collective-permute-start(bf16[8,160,128]{2,1,0:T(8,128)(2,1)S(1)} %collective-permute-done.2.refs_0_), channel_id=1, source_target_pairs={{0,224},{32,0},{64,32},{96,64},{128,96},{160,128},{192,160},{224,1... | collective-permute-start | bytes 983048 | tf_op jit(solution)/shard_map/ppermute | solution.py:536
  42.6 0.0 collective-permute-done.5.refs_4_
  42.6 0.0 collective-permute-start.6
  42.6 5.7 %collective-permute-done.3.refs_1_ = bf16[8,160,128]{2,1,0:T(8,128)(2,1)S(1)} collective-permute-done((bf16[8,160,128]{2,1,0:T(8,128)(2,1)S(1)}, bf16[8,160,128]{2,1,0:T(8,128)(2,1)S(1)}, u32[]{:S(2)}, u32[]{:S(2)}) %collective-permute-start.3) | collective-permute-done | bytes 327712 | tf_op jit(solution)/shard_map/ppermute | solution.py:536
  48.3 2.7 %collective-permute-start.4 = (bf16[8,160,128]{2,1,0:T(8,128)(2,1)S(1)}, bf16[8,160,128]{2,1,0:T(8,128)(2,1)S(1)}, u32[]{:S(2)}, u32[]{:S(2)}) collective-permute-start(bf16[8,160,128]{2,1,0:T(8,128)(2,1)S(1)} %collective-permute-done.3.refs_1_), channel_id=1, source_target_pairs={{0,224},{32,0},{64,32},{96,64},{128,96},{160,128},{192,160},{224,1... | collective-permute-start | bytes 983048 | tf_op jit(solution)/shard_map/ppermute | solution.py:536
  51.0 0.0 collective-permute-done.6.refs_3_
  51.0 4.6 %collective-permute-done.4.refs_2_ = bf16[8,160,128]{2,1,0:T(8,128)(2,1)S(1)} collective-permute-done((bf16[8,160,128]{2,1,0:T(8,128)(2,1)S(1)}, bf16[8,160,128]{2,1,0:T(8,128)(2,1)S(1)}, u32[]{:S(2)}, u32[]{:S(2)}) %collective-permute-start.4) | collective-permute-done | bytes 327712 | tf_op jit(solution)/shard_map/ppermute | solution.py:536
  55.6 0.0 copy-done.8
  55.6 0.7 copy-done.10
  56.3 4.3 %build.3 = bf16[16,5,160,128]{3,2,1,0:T(8,128)(2,1)} custom-call(s32[16,8]{1,0:T(8,128)} %bitcast.8, bf16[8,160,128]{2,1,0:T(8,128)(2,1)} %copy-done.6, bf16[8,160,128]{2,1,0:T(8,128)(2,1)} %copy-done.8, bf16[8,160,128]{2,1,0:T(8,128)(2,1)} %copy-done.10, bf16[8,160,128]{2,1,0:T(8,128)(2,1)} %copy-done.9, bf16[8,160,128]{2,1,0:T(8,128)(2,1)} %copy-done.7), custom_call_target="tpu_custom_call" | custom-call | tf_op jit(solution)/shard_map/build/pallas_call | solution.py:71
  60.6 0.0 all-to-all-done.1.near_hbm
  60.6 42.7 %all_to_all.31 = bf16[16,5,160,128]{3,2,1,0:T(8,128)(2,1)} all-to-all(bf16[16,5,160,128]{3,2,1,0:T(8,128)(2,1)} %build.3), channel_id=1, replica_groups=mesh['z'=8,'y'=4,'x'=4,'grp'=2] {'y','x'}, dimensions={0} | all-to-all | bytes 6553600 | tf_op jit(solution)/shard_map/all_to_all | solution.py:541
  103.4 25.7 %attend.1 = (bf16[512,1024]{1,0:T(8,128)(2,1)}, bf16[512,1536]{1,0:T(8,128)(2,1)}, bf16[16,160,128]{2,1,0:T(8,128)(2,1)}, bf16[16,2,160,128]{3,2,1,0:T(8,128)(2,...) custom-call(s32[8,16]{1,0:T(8,128)} %get-tuple-element.54.src_ref, bf16[512,1536]{1,0:T(8,128)(2,1)} %q_ref.1, ...), custom_call_target="tpu_custom_call" | custom-call | tf_op jit(solution)/shard_map/attend/pallas_call | solution.py:445
  129.0 0.0 copy-start.3
  129.1 39.3 %all_to_all.32.ret_hbm = bf16[16,5,160,128]{3,2,1,0:T(8,128)(2,1)S(1)} all-to-all(bf16[16,5,160,128]{3,2,1,0:T(8,128)(2,1)} %bitcast.14), channel_id=1, replica_groups=mesh['z'=8,'y'=4,'x'=4,'grp'=2] {'y','x'}, dimensions={0} | all-to-all | bytes 6553600 | tf_op jit(solution)/shard_map/all_to_all | solution.py:545
  168.3 0.0 copy-done.3
  168.3 2.6 %sum_returned.2 = (bf16[8,160,128]{2,1,0:T(8,128)(2,1)S(1)}, bf16[8,160,128]{2,1,0:T(8,128)(2,1)S(1)}, bf16[8,160,128]{2,1,0:T(8,128)(2,1)S(1)}, bf16[8,160,128]...) custom-call(s32[16,8]{1,0:T(8,128)S(1)} %bitcast.9, bf16[16,5,160,128]{3,2,1,0:T(8,128)(2,1)S(1)} %all_to_all.32.ret_hbm), custom_call_target="tpu_custom_call" | custom-call | tf_op jit(solution)/shard_map/sum_returned/pallas_call | solution.py:127
  170.9 1.3 collective-permute-start.7
  172.2 4.9 %all-to-all-start.4 = ((bf16[16,2,160,128]{3,2,1,0:T(8,128)(2,1)}), bf16[16,2,160,128]{3,2,1,0:T(8,128)(2,1)S(1)}, u32[]{:S(2)}, u32[]{:S(2)}) async-start(bf16[16,2,160,128]{3,2,1,0:T(8,128)(2,1)} %get-tuple-element.38), calls=%async_computation.4 | async-start | bytes 2621440 | tf_op jit(solution)/shard_map/all_to_all | solution.py:549
  177.1 5.2 %collective-permute-done.7 = bf16[8,160,128]{2,1,0:T(8,128)(2,1)S(1)} collective-permute-done((bf16[8,160,128]{2,1,0:T(8,128)(2,1)S(1)}, bf16[8,160,128]{2,1,0:T(8,128)(2,1)S(1)}, u32[]{:S(2)}, u32[]{:S(2)}) %collective-permute-start.7) | collective-permute-done | bytes 327712 | tf_op jit(solution)/shard_map/ppermute | solution.py:500
  182.3 0.1 add_convert_fusion.4
  182.4 0.6 collective-permute-start.8
  183.1 2.9 %collective-permute-start.11 = (bf16[8,160,128]{2,1,0:T(8,128)(2,1)S(1)}, bf16[8,160,128]{2,1,0:T(8,128)(2,1)S(1)}, u32[]{:S(2)}, u32[]{:S(2)}) collective-permute-start(bf16[8,160,128]{2,1,0:T(8,128)(2,1)S(1)} %get-tuple-element.47), channel_id=1, source_target_pairs={{0,224},{32,0},{64,32},{96,64},{128,96},{160,128},{192,160},{224,1... | collective-permute-start | bytes 983048 | tf_op jit(solution)/shard_map/ppermute | solution.py:500
  186.0 7.1 %collective-permute-done.8 = bf16[8,160,128]{2,1,0:T(8,128)(2,1)S(1)} collective-permute-done((bf16[8,160,128]{2,1,0:T(8,128)(2,1)S(1)}, bf16[8,160,128]{2,1,0:T(8,128)(2,1)S(1)}, u32[]{:S(2)}, u32[]{:S(2)}) %collective-permute-start.8) | collective-permute-done | bytes 327712 | tf_op jit(solution)/shard_map/ppermute | solution.py:503
  193.1 0.1 add_convert_fusion.3
  193.2 0.1 collective-permute-start.9
  193.3 0.0 collective-permute-done.11
  193.3 0.1 add_convert_fusion.1
  193.4 3.3 %collective-permute-start.12 = (bf16[8,160,128]{2,1,0:T(8,128)(2,1)S(1)}, bf16[8,160,128]{2,1,0:T(8,128)(2,1)}, u32[]{:S(2)}, u32[]{:S(2)}) collective-permute-start(bf16[8,160,128]{2,1,0:T(8,128)(2,1)S(1)} %add_convert_fusion.1), channel_id=1, source_target_pairs={{0,224},{32,0},{64,32},{96,64},{128,96},{160,128},{192,160},{224,1... | collective-permute-start | bytes 983048 | tf_op jit(solution)/shard_map/ppermute | solution.py:503
  196.7 0.0 all-to-all-done.4.ret_hbm
  196.7 1.4 sum_returned.3
  198.1 0.0 copy-start.1
  198.1 5.4 %all-to-all-start.5 = ((bf16[16,1,160,128]{3,2,1,0:T(8,128)(2,1)}), bf16[16,1,160,128]{3,2,1,0:T(8,128)(2,1)S(1)}, u32[]{:S(2)}, u32[]{:S(2)}) async-start(bf16[16,1,160,128]{3,2,1,0:T(8,128)(2,1)} %bitcast.5), calls=%async_computation.5 | async-start | bytes 1310720 | tf_op jit(solution)/shard_map/all_to_all | solution.py:553
  203.6 0.2 collective-permute-done.9
  203.8 1.1 add_convert_fusion.2
  204.9 0.1 collective-permute-start.10
  205.0 0.0 collective-permute-done.12
  205.0 1.1 add_convert_fusion
  206.0 3.3 %collective-permute-start.13 = (bf16[8,160,128]{2,1,0:T(8,128)(2,1)S(1)}, bf16[8,160,128]{2,1,0:T(8,128)(2,1)S(1)}, u32[]{:S(2)}, u32[]{:S(2)}) collective-permute-start(bf16[8,160,128]{2,1,0:T(8,128)(2,1)S(1)} %add_convert_fusion), channel_id=1, source_target_pairs={{0,224},{32,0},{64,32},{96,64},{128,96},{160,128},{192,160},{224,1... | collective-permute-start | bytes 983048 | tf_op jit(solution)/shard_map/ppermute | solution.py:503
  209.3 3.9 %collective-permute-done.10.rising_ref = bf16[8,160,128]{2,1,0:T(8,128)(2,1)S(1)} collective-permute-done((bf16[8,160,128]{2,1,0:T(8,128)(2,1)S(1)}, bf16[8,160,128]{2,1,0:T(8,128)(2,1)S(1)}, u32[]{:S(2)}, u32[]{:S(2)}) %collective-permute-start.10) | collective-permute-done | bytes 327712 | tf_op jit(solution)/shard_map/ppermute | solution.py:503
  213.2 0.7 collective-permute-done.13.falling_ref
  213.9 0.0 all-to-all-done.5.ret_ref
  213.9 0.0 copy-done.1
  213.9 1.9 finish.1
  (12 shorter events, 0.0 us)
Async XLA Ops:
  0.6 0.9 copy-start.4
  1.6 0.9 copy-start.5
  2.7 23.9 %copy-start = (bf16[8,160,128]{2,1,0:T(8,128)(2,1)}, bf16[8,160,128]{2,1,0:T(8,128)(2,1)S(1)}, u32[]{:S(2)}) copy-start(bf16[8,160,128]{2,1,0:T(8,128)(2,1)S(1)} %pack.1.refs_0_.local_hbm) | copy-start | bytes 983044
  2.7 21.2 %collective-permute-start.1 = (bf16[8,160,128]{2,1,0:T(8,128)(2,1)S(1)}, bf16[8,160,128]{2,1,0:T(8,128)(2,1)S(1)}, u32[]{:S(2)}, u32[]{:S(2)}) collective-permute-start(bf16[8,160,128]{2,1,0:T(8,128)(2,1)S(1)} %pack.1.refs_0_.local_hbm), channel_id=1, source_target_pairs={{0,32},{32,64},{64,96},{96,128},{128,160},{160,192},{192,224},{224... | collective-permute-start | bytes 983048 | tf_op jit(solution)/shard_map/ppermute | solution.py:538
  4.7 19.2 %collective-permute-start = (bf16[8,160,128]{2,1,0:T(8,128)(2,1)S(1)}, bf16[8,160,128]{2,1,0:T(8,128)(2,1)S(1)}, u32[]{:S(2)}, u32[]{:S(2)}) collective-permute-start(bf16[8,160,128]{2,1,0:T(8,128)(2,1)S(1)} %pack.1.refs_0_.local_hbm), channel_id=1, source_target_pairs={{0,224},{32,0},{64,32},{96,64},{128,96},{160,128},{192,160},{224,1... | collective-permute-start | bytes 983048 | tf_op jit(solution)/shard_map/ppermute | solution.py:536
  23.8 2.8 %copy-start.2 = (s32[16,1,8]{2,1,0:T(1,128)}, s32[16,1,8]{2,1,0:T(1,128)S(1)}, u32[]{:S(2)}) copy-start(s32[16,1,8]{2,1,0:T(1,128)S(1)} %all_to_all.30) | copy-start | bytes 1540
  26.6 34.0 %all-to-all-start.1 = ((bf16[16,3,160,128]{3,2,1,0:T(8,128)(2,1)}), bf16[16,3,160,128]{3,2,1,0:T(8,128)(2,1)}, u32[]{:S(2)}, u32[]{:S(2)}) async-start(bf16[16,3,160,128]{3,2,1,0:T(8,128)(2,1)} %build.2), calls=%async_computation.1 | async-start | bytes 3932160 | tf_op jit(solution)/shard_map/all_to_all | solution.py:540
  32.3 7.9 %collective-permute-start.2 = (bf16[8,160,128]{2,1,0:T(8,128)(2,1)S(1)}, bf16[8,160,128]{2,1,0:T(8,128)(2,1)S(1)}, u32[]{:S(2)}, u32[]{:S(2)}) collective-permute-start(bf16[8,160,128]{2,1,0:T(8,128)(2,1)S(1)} %collective-permute-done.refs_1_), channel_id=1, source_target_pairs={{0,224},{32,0},{64,32},{96,64},{128,96},{160,128},{192,160},{224,1... | collective-permute-start | bytes 983048 | tf_op jit(solution)/shard_map/ppermute | solution.py:536
  34.2 8.4 %collective-permute-start.5 = (bf16[8,160,128]{2,1,0:T(8,128)(2,1)S(1)}, bf16[8,160,128]{2,1,0:T(8,128)(2,1)S(1)}, u32[]{:S(2)}, u32[]{:S(2)}) collective-permute-start(bf16[8,160,128]{2,1,0:T(8,128)(2,1)S(1)} %collective-permute-done.1.refs_2_), channel_id=1, source_target_pairs={{0,32},{32,64},{64,96},{96,128},{128,160},{160,192},{192,224},{224... | collective-permute-start | bytes 983048 | tf_op jit(solution)/shard_map/ppermute | solution.py:538
  40.1 15.5 %copy-start.6 = (bf16[8,160,128]{2,1,0:T(8,128)(2,1)}, bf16[8,160,128]{2,1,0:T(8,128)(2,1)S(1)}, u32[]{:S(2)}) copy-start(bf16[8,160,128]{2,1,0:T(8,128)(2,1)S(1)} %collective-permute-done.2.refs_0_) | copy-start | bytes 983044
  40.1 8.2 %collective-permute-start.3 = (bf16[8,160,128]{2,1,0:T(8,128)(2,1)S(1)}, bf16[8,160,128]{2,1,0:T(8,128)(2,1)S(1)}, u32[]{:S(2)}, u32[]{:S(2)}) collective-permute-start(bf16[8,160,128]{2,1,0:T(8,128)(2,1)S(1)} %collective-permute-done.2.refs_0_), channel_id=1, source_target_pairs={{0,224},{32,0},{64,32},{96,64},{128,96},{160,128},{192,160},{224,1... | collective-permute-start | bytes 983048 | tf_op jit(solution)/shard_map/ppermute | solution.py:536
  42.6 13.0 %copy-start.7 = (bf16[8,160,128]{2,1,0:T(8,128)(2,1)}, bf16[8,160,128]{2,1,0:T(8,128)(2,1)S(1)}, u32[]{:S(2)}) copy-start(bf16[8,160,128]{2,1,0:T(8,128)(2,1)S(1)} %collective-permute-done.5.refs_4_) | copy-start | bytes 983044
  42.6 8.4 %collective-permute-start.6 = (bf16[8,160,128]{2,1,0:T(8,128)(2,1)S(1)}, bf16[8,160,128]{2,1,0:T(8,128)(2,1)S(1)}, u32[]{:S(2)}, u32[]{:S(2)}) collective-permute-start(bf16[8,160,128]{2,1,0:T(8,128)(2,1)S(1)} %collective-permute-done.5.refs_4_), channel_id=1, source_target_pairs={{0,32},{32,64},{64,96},{96,128},{128,160},{160,192},{192,224},{224... | collective-permute-start | bytes 983048 | tf_op jit(solution)/shard_map/ppermute | solution.py:538
  48.3 7.3 %copy-start.8 = (bf16[8,160,128]{2,1,0:T(8,128)(2,1)}, bf16[8,160,128]{2,1,0:T(8,128)(2,1)S(1)}, u32[]{:S(2)}) copy-start(bf16[8,160,128]{2,1,0:T(8,128)(2,1)S(1)} %collective-permute-done.3.refs_1_) | copy-start | bytes 983044
  48.3 7.3 %collective-permute-start.4 = (bf16[8,160,128]{2,1,0:T(8,128)(2,1)S(1)}, bf16[8,160,128]{2,1,0:T(8,128)(2,1)S(1)}, u32[]{:S(2)}, u32[]{:S(2)}) collective-permute-start(bf16[8,160,128]{2,1,0:T(8,128)(2,1)S(1)} %collective-permute-done.3.refs_1_), channel_id=1, source_target_pairs={{0,224},{32,0},{64,32},{96,64},{128,96},{160,128},{192,160},{224,1... | collective-permute-start | bytes 983048 | tf_op jit(solution)/shard_map/ppermute | solution.py:536
  51.0 4.6 %copy-start.9 = (bf16[8,160,128]{2,1,0:T(8,128)(2,1)}, bf16[8,160,128]{2,1,0:T(8,128)(2,1)S(1)}, u32[]{:S(2)}) copy-start(bf16[8,160,128]{2,1,0:T(8,128)(2,1)S(1)} %collective-permute-done.6.refs_3_) | copy-start | bytes 983044
  55.6 0.7 copy-start.10
  129.0 39.3 %copy-start.3 = (s32[16,1,8]{2,1,0:T(1,128)S(1)}, s32[16,1,8]{2,1,0:T(1,128)}, u32[]{:S(2)}) copy-start(s32[16,1,8]{2,1,0:T(1,128)} %copy-done.2) | copy-start | bytes 1540
  170.9 11.4 %collective-permute-start.7 = (bf16[8,160,128]{2,1,0:T(8,128)(2,1)S(1)}, bf16[8,160,128]{2,1,0:T(8,128)(2,1)S(1)}, u32[]{:S(2)}, u32[]{:S(2)}) collective-permute-start(bf16[8,160,128]{2,1,0:T(8,128)(2,1)S(1)} %get-tuple-element.43), channel_id=1, source_target_pairs={{0,32},{32,64},{64,96},{96,128},{128,160},{160,192},{192,224},{224... | collective-permute-start | bytes 983048 | tf_op jit(solution)/shard_map/ppermute | solution.py:500
  172.2 24.5 %all-to-all-start.4 = ((bf16[16,2,160,128]{3,2,1,0:T(8,128)(2,1)}), bf16[16,2,160,128]{3,2,1,0:T(8,128)(2,1)S(1)}, u32[]{:S(2)}, u32[]{:S(2)}) async-start(bf16[16,2,160,128]{3,2,1,0:T(8,128)(2,1)} %get-tuple-element.38), calls=%async_computation.4 | async-start | bytes 2621440 | tf_op jit(solution)/shard_map/all_to_all | solution.py:549
  182.4 10.7 %collective-permute-start.8 = (bf16[8,160,128]{2,1,0:T(8,128)(2,1)S(1)}, bf16[8,160,128]{2,1,0:T(8,128)(2,1)S(1)}, u32[]{:S(2)}, u32[]{:S(2)}) collective-permute-start(bf16[8,160,128]{2,1,0:T(8,128)(2,1)S(1)} %add_convert_fusion.4), channel_id=1, source_target_pairs={{0,32},{32,64},{64,96},{96,128},{128,160},{160,192},{192,224},{224... | collective-permute-start | bytes 983048 | tf_op jit(solution)/shard_map/ppermute | solution.py:503
  183.1 10.2 %collective-permute-start.11 = (bf16[8,160,128]{2,1,0:T(8,128)(2,1)S(1)}, bf16[8,160,128]{2,1,0:T(8,128)(2,1)S(1)}, u32[]{:S(2)}, u32[]{:S(2)}) collective-permute-start(bf16[8,160,128]{2,1,0:T(8,128)(2,1)S(1)} %get-tuple-element.47), channel_id=1, source_target_pairs={{0,224},{32,0},{64,32},{96,64},{128,96},{160,128},{192,160},{224,1... | collective-permute-start | bytes 983048 | tf_op jit(solution)/shard_map/ppermute | solution.py:500
  193.2 10.6 %collective-permute-start.9 = (bf16[8,160,128]{2,1,0:T(8,128)(2,1)S(1)}, bf16[8,160,128]{2,1,0:T(8,128)(2,1)}, u32[]{:S(2)}, u32[]{:S(2)}) collective-permute-start(bf16[8,160,128]{2,1,0:T(8,128)(2,1)S(1)} %add_convert_fusion.3), channel_id=1, source_target_pairs={{0,32},{32,64},{64,96},{96,128},{128,160},{160,192},{192,224},{224... | collective-permute-start | bytes 983048 | tf_op jit(solution)/shard_map/ppermute | solution.py:503
  193.4 11.6 %collective-permute-start.12 = (bf16[8,160,128]{2,1,0:T(8,128)(2,1)S(1)}, bf16[8,160,128]{2,1,0:T(8,128)(2,1)}, u32[]{:S(2)}, u32[]{:S(2)}) collective-permute-start(bf16[8,160,128]{2,1,0:T(8,128)(2,1)S(1)} %add_convert_fusion.1), channel_id=1, source_target_pairs={{0,224},{32,0},{64,32},{96,64},{128,96},{160,128},{192,160},{224,1... | collective-permute-start | bytes 983048 | tf_op jit(solution)/shard_map/ppermute | solution.py:503
  198.1 15.8 %copy-start.1 = (f32[8,160,128]{2,1,0:T(8,128)S(1)}, f32[8,160,128]{2,1,0:T(8,128)}, u32[]{:S(2)}) copy-start(f32[8,160,128]{2,1,0:T(8,128)} %get-tuple-element.30.own_ref) | copy-start | bytes 1966084
  198.1 15.8 %all-to-all-start.5 = ((bf16[16,1,160,128]{3,2,1,0:T(8,128)(2,1)}), bf16[16,1,160,128]{3,2,1,0:T(8,128)(2,1)S(1)}, u32[]{:S(2)}, u32[]{:S(2)}) async-start(bf16[16,1,160,128]{3,2,1,0:T(8,128)(2,1)} %bitcast.5), calls=%async_computation.5 | async-start | bytes 1310720 | tf_op jit(solution)/shard_map/all_to_all | solution.py:553
  204.9 8.4 %collective-permute-start.10 = (bf16[8,160,128]{2,1,0:T(8,128)(2,1)S(1)}, bf16[8,160,128]{2,1,0:T(8,128)(2,1)S(1)}, u32[]{:S(2)}, u32[]{:S(2)}) collective-permute-start(bf16[8,160,128]{2,1,0:T(8,128)(2,1)S(1)} %add_convert_fusion.2), channel_id=1, source_target_pairs={{0,32},{32,64},{64,96},{96,128},{128,160},{160,192},{192,224},{224... | collective-permute-start | bytes 983048 | tf_op jit(solution)/shard_map/ppermute | solution.py:503
  206.0 7.9 %collective-permute-start.13 = (bf16[8,160,128]{2,1,0:T(8,128)(2,1)S(1)}, bf16[8,160,128]{2,1,0:T(8,128)(2,1)S(1)}, u32[]{:S(2)}, u32[]{:S(2)}) collective-permute-start(bf16[8,160,128]{2,1,0:T(8,128)(2,1)S(1)} %add_convert_fusion), channel_id=1, source_target_pairs={{0,224},{32,0},{64,32},{96,64},{128,96},{160,128},{192,160},{224,1... | collective-permute-start | bytes 983048 | tf_op jit(solution)/shard_map/ppermute | solution.py:503

commit v7 on v6

--- a/solution.py
+++ b/solution.py
@@ -484,7 +484,7 @@
             jax.ShapeDtypeStruct((n_far, ROWS, 128), BF),
             jax.ShapeDtypeStruct((LOCAL, ROWS, 128), F32),
         ),
-        compiler_params=params(),
+        compiler_params=params(48),
         name="attend",
     )(
         src,

time: 219 us -> 213 us (0.973); the launches traced: 216 us -> 212 us
  other arithmetic: 3.85 us -> 1.32 us
  transfers between devices with their start and end apart: 17 -> 17, of which waited for: 8 -> 7; matrix products, arithmetic and copies ran while one was open for 2% -> 1% of each run, Pallas kernels for 3% -> 3%
where the time goes in v7:
time: 213 us; the launch traced here: 212 us
  blocking collectives  95.8 us (45%)
  starting transfers between devices  40.6 us (19%)
  Pallas kernels  36.9 us (17%)
  waiting for transfers between devices  34 us (16%)
  local copies, waits for them, and re-layouts  2.83 us (1%)
    all_to_all x1, blocking collectives, shards(): far = exchange(build(3, 56, asked, *above[2:], *below[:1:-1]))  42.9 us
    all_to_all x1, blocking collectives, shards(): far_sums = sum_returned(3, asked, exchange(part_far.reshape(far.shape)))  39.4 us
    pallas_call x1, Pallas kernels, attend(): pl.pallas_call(attend_kernel, grid_spec=pltpu.PrefetchScalarGridSpec(num_...  23.9 us
    ppermute x4, waiting for transfers between devices, shards(): above.append(lax.ppermute(above[-1], 'z', down))  16.1 us
    all_to_all x1, blocking collectives, shards(): asked = exchange(wanted.reshape(plane, 1, depth)).reshape(plane, depth)  13.5 us
    ppermute x5, waiting for transfers between devices, pass_on(): total = lax.ppermute(total, 'z', perm)  11.8 us
    ppermute x4, starting transfers between devices, shards(): above.append(lax.ppermute(above[-1], 'z', down))  11.1 us
    ppermute x5, starting transfers between devices, pass_on(): total = lax.ppermute(total, 'z', perm)  7.58 us
  transfers between devices with their start and end apart: 17, of which 7 were waited for; matrix products, arithmetic and copies ran while one was open for 1% of the time, Pallas kernels for 3%

profile of v7, /device:TPU:2, one launch (start us, length us, event | category | flops | bytes accessed | tf_op | source)
XLA Modules:
  0.0 212.3 jit_solution(10639310350011484349)
XLA Ops:
  0.6 0.9 copy-done.6
  1.6 0.9 copy-done.7
  2.5 0.2 pack.1.refs_0_.local_hbm
  2.7 2.0 collective-permute-start.1
  4.7 4.0 %collective-permute-start = (bf16[8,160,128]{2,1,0:T(8,128)(2,1)S(1)}, bf16[8,160,128]{2,1,0:T(8,128)(2,1)S(1)}, u32[]{:S(2)}, u32[]{:S(2)}) collective-permute-start(bf16[8,160,128]{2,1,0:T(8,128)(2,1)S(1)} %pack.1.refs_0_.local_hbm), channel_id=1, source_target_pairs={{0,224},{32,0},{64,32},{96,64},{128,96},{160,128},{192,160},{224,1... | collective-permute-start | bytes 983048 | tf_op jit(solution)/shard_map/ppermute | solution.py:536
  8.7 0.7 add_select_fusion.5
  9.4 0.1 eq.24
  9.5 0.1 add.93
  9.6 0.1 select_reduce_fusion
  9.7 0.1 reshape.30
  9.8 13.5 %all_to_all.30 = s32[16,1,8]{2,1,0:T(1,128)S(1)} all-to-all(s32[16,1,8]{2,1,0:T(1,128)S(1)} %bitcast.15), channel_id=1, replica_groups=mesh['z'=8,'y'=4,'x'=4,'grp'=2] {'y','x'}, dimensions={0} | all-to-all | bytes 1024 | tf_op jit(solution)/shard_map/all_to_all | solution.py:539
  23.2 0.0 collective-permute-done.1.refs_2_
  23.2 0.0 collective-permute-done.refs_1_
  23.2 2.8 %build.2 = bf16[16,3,160,128]{3,2,1,0:T(8,128)(2,1)} custom-call(s32[16,8]{1,0:T(8,128)S(1)} %bitcast.7, bf16[8,160,128]{2,1,0:T(8,128)(2,1)S(1)} %pack.1.refs_0_.local_hbm, bf16[8,160,128]{2,1,0:T(8,128)(2,1)S(1)} %collective-permute-done.refs_1_, bf16[8,160,128]{2,1,0:T(8,128)(2,1)S(1)} %collective-permute-done.1.refs_2_), custom_call_target="tpu_custom_call" | custom-call | tf_op jit(solution)/shard_map/build/pallas_call | solution.py:71
  26.0 5.6 %all-to-all-start.1 = ((bf16[16,3,160,128]{3,2,1,0:T(8,128)(2,1)}), bf16[16,3,160,128]{3,2,1,0:T(8,128)(2,1)}, u32[]{:S(2)}, u32[]{:S(2)}) async-start(bf16[16,3,160,128]{3,2,1,0:T(8,128)(2,1)} %build.2), calls=%async_computation.1 | async-start | bytes 3932160 | tf_op jit(solution)/shard_map/all_to_all | solution.py:540
  31.7 1.9 collective-permute-start.2
  33.6 0.1 collective-permute-start.5
  33.7 5.8 %collective-permute-done.2.refs_0_ = bf16[8,160,128]{2,1,0:T(8,128)(2,1)S(1)} collective-permute-done((bf16[8,160,128]{2,1,0:T(8,128)(2,1)S(1)}, bf16[8,160,128]{2,1,0:T(8,128)(2,1)S(1)}, u32[]{:S(2)}, u32[]{:S(2)}) %collective-permute-start.2) | collective-permute-done | bytes 327712 | tf_op jit(solution)/shard_map/ppermute | solution.py:536
  39.5 2.5 %collective-permute-start.3 = (bf16[8,160,128]{2,1,0:T(8,128)(2,1)S(1)}, bf16[8,160,128]{2,1,0:T(8,128)(2,1)S(1)}, u32[]{:S(2)}, u32[]{:S(2)}) collective-permute-start(bf16[8,160,128]{2,1,0:T(8,128)(2,1)S(1)} %collective-permute-done.2.refs_0_), channel_id=1, source_target_pairs={{0,224},{32,0},{64,32},{96,64},{128,96},{160,128},{192,160},{224,1... | collective-permute-start | bytes 983048 | tf_op jit(solution)/shard_map/ppermute | solution.py:536
  42.0 0.0 collective-permute-done.5.refs_4_
  42.0 0.0 collective-permute-start.6
  42.0 5.7 %collective-permute-done.3.refs_1_ = bf16[8,160,128]{2,1,0:T(8,128)(2,1)S(1)} collective-permute-done((bf16[8,160,128]{2,1,0:T(8,128)(2,1)S(1)}, bf16[8,160,128]{2,1,0:T(8,128)(2,1)S(1)}, u32[]{:S(2)}, u32[]{:S(2)}) %collective-permute-start.3) | collective-permute-done | bytes 327712 | tf_op jit(solution)/shard_map/ppermute | solution.py:536
  47.7 2.7 %collective-permute-start.4 = (bf16[8,160,128]{2,1,0:T(8,128)(2,1)S(1)}, bf16[8,160,128]{2,1,0:T(8,128)(2,1)S(1)}, u32[]{:S(2)}, u32[]{:S(2)}) collective-permute-start(bf16[8,160,128]{2,1,0:T(8,128)(2,1)S(1)} %collective-permute-done.3.refs_1_), channel_id=1, source_target_pairs={{0,224},{32,0},{64,32},{96,64},{128,96},{160,128},{192,160},{224,1... | collective-permute-start | bytes 983048 | tf_op jit(solution)/shard_map/ppermute | solution.py:536
  50.4 0.0 collective-permute-done.6.refs_3_
  50.4 4.6 %collective-permute-done.4.refs_2_ = bf16[8,160,128]{2,1,0:T(8,128)(2,1)S(1)} collective-permute-done((bf16[8,160,128]{2,1,0:T(8,128)(2,1)S(1)}, bf16[8,160,128]{2,1,0:T(8,128)(2,1)S(1)}, u32[]{:S(2)}, u32[]{:S(2)}) %collective-permute-start.4) | collective-permute-done | bytes 327712 | tf_op jit(solution)/shard_map/ppermute | solution.py:536
  55.0 0.0 copy-done.8
  55.0 0.0 copy-start.12
  55.0 0.7 copy-done.12
  55.7 4.2 %build.3 = bf16[16,5,160,128]{3,2,1,0:T(8,128)(2,1)} custom-call(s32[16,8]{1,0:T(8,128)} %bitcast.8, bf16[8,160,128]{2,1,0:T(8,128)(2,1)} %copy-done.8, bf16[8,160,128]{2,1,0:T(8,128)(2,1)} %copy-done.10, bf16[8,160,128]{2,1,0:T(8,128)(2,1)} %copy-done.12, bf16[8,160,128]{2,1,0:T(8,128)(2,1)} %copy-done.11, bf16[8,160,128]{2,1,0:T(8,128)(2,1)} %copy-done.9), custom_call_target="tpu_custom_call" | custom-call | tf_op jit(solution)/shard_map/build/pallas_call | solution.py:71
  59.9 0.0 copy-start
  59.9 0.0 copy-start.1
  60.0 0.0 all-to-all-done.1.near_hbm
  60.0 42.9 %all_to_all.31 = bf16[16,5,160,128]{3,2,1,0:T(8,128)(2,1)} all-to-all(bf16[16,5,160,128]{3,2,1,0:T(8,128)(2,1)} %build.3), channel_id=1, replica_groups=mesh['z'=8,'y'=4,'x'=4,'grp'=2] {'y','x'}, dimensions={0} | all-to-all | bytes 6553600 | tf_op jit(solution)/shard_map/all_to_all | solution.py:541
  102.8 0.0 copy-done.1
  102.8 23.9 %attend.1 = (bf16[512,1024]{1,0:T(8,128)(2,1)}, bf16[512,1536]{1,0:T(8,128)(2,1)}, bf16[16,160,128]{2,1,0:T(8,128)(2,1)}, bf16[16,2,160,128]{3,2,1,0:T(8,128)(2,...) custom-call(s32[8,16]{1,0:T(8,128)S(1)} %get-tuple-element.54.src_ref, bf16[512,1536]{1,0:T(8,128)(2,1)S(1)} %copy-done, ...), custom_call_target="tpu_custom_call" | custom-call | tf_op jit(solution)/shard_map/attend/pallas_call | solution.py:445
  126.7 0.0 copy-start.2
  126.8 0.0 copy-start.5
  126.8 39.4 %all_to_all.32.ret_hbm = bf16[16,5,160,128]{3,2,1,0:T(8,128)(2,1)S(1)} all-to-all(bf16[16,5,160,128]{3,2,1,0:T(8,128)(2,1)} %bitcast.14), channel_id=1, replica_groups=mesh['z'=8,'y'=4,'x'=4,'grp'=2] {'y','x'}, dimensions={0} | all-to-all | bytes 6553600 | tf_op jit(solution)/shard_map/all_to_all | solution.py:545
  166.2 2.6 %sum_returned.2 = (bf16[8,160,128]{2,1,0:T(8,128)(2,1)S(1)}, bf16[8,160,128]{2,1,0:T(8,128)(2,1)S(1)}, bf16[8,160,128]{2,1,0:T(8,128)(2,1)S(1)}, bf16[8,160,128]...) custom-call(s32[16,8]{1,0:T(8,128)S(1)} %bitcast.9, bf16[16,5,160,128]{3,2,1,0:T(8,128)(2,1)S(1)} %all_to_all.32.ret_hbm), custom_call_target="tpu_custom_call" | custom-call | tf_op jit(solution)/shard_map/sum_returned/pallas_call | solution.py:127
  168.8 1.3 collective-permute-start.7
  170.1 4.9 %all-to-all-start.4 = ((bf16[16,2,160,128]{3,2,1,0:T(8,128)(2,1)}), bf16[16,2,160,128]{3,2,1,0:T(8,128)(2,1)S(1)}, u32[]{:S(2)}, u32[]{:S(2)}) async-start(bf16[16,2,160,128]{3,2,1,0:T(8,128)(2,1)} %get-tuple-element.38), calls=%async_computation.4 | async-start | bytes 2621440 | tf_op jit(solution)/shard_map/all_to_all | solution.py:549
  175.0 5.0 %collective-permute-done.7 = bf16[8,160,128]{2,1,0:T(8,128)(2,1)S(1)} collective-permute-done((bf16[8,160,128]{2,1,0:T(8,128)(2,1)S(1)}, bf16[8,160,128]{2,1,0:T(8,128)(2,1)S(1)}, u32[]{:S(2)}, u32[]{:S(2)}) %collective-permute-start.7) | collective-permute-done | bytes 327712 | tf_op jit(solution)/shard_map/ppermute | solution.py:500
  180.1 0.1 add_convert_fusion.4
  180.2 0.8 collective-permute-start.8
  181.0 2.7 %collective-permute-start.11 = (bf16[8,160,128]{2,1,0:T(8,128)(2,1)S(1)}, bf16[8,160,128]{2,1,0:T(8,128)(2,1)S(1)}, u32[]{:S(2)}, u32[]{:S(2)}) collective-permute-start(bf16[8,160,128]{2,1,0:T(8,128)(2,1)S(1)} %get-tuple-element.47), channel_id=1, source_target_pairs={{0,224},{32,0},{64,32},{96,64},{128,96},{160,128},{192,160},{224,1... | collective-permute-start | bytes 983048 | tf_op jit(solution)/shard_map/ppermute | solution.py:500
  183.7 6.9 %collective-permute-done.8 = bf16[8,160,128]{2,1,0:T(8,128)(2,1)S(1)} collective-permute-done((bf16[8,160,128]{2,1,0:T(8,128)(2,1)S(1)}, bf16[8,160,128]{2,1,0:T(8,128)(2,1)S(1)}, u32[]{:S(2)}, u32[]{:S(2)}) %collective-permute-start.8) | collective-permute-done | bytes 327712 | tf_op jit(solution)/shard_map/ppermute | solution.py:503
  190.6 0.1 add_convert_fusion.3
  190.7 0.1 collective-permute-start.9
  190.8 0.0 collective-permute-done.11
  190.8 0.1 add_convert_fusion.1
  190.9 3.3 %collective-permute-start.12 = (bf16[8,160,128]{2,1,0:T(8,128)(2,1)S(1)}, bf16[8,160,128]{2,1,0:T(8,128)(2,1)S(1)}, u32[]{:S(2)}, u32[]{:S(2)}) collective-permute-start(bf16[8,160,128]{2,1,0:T(8,128)(2,1)S(1)} %add_convert_fusion.1), channel_id=1, source_target_pairs={{0,224},{32,0},{64,32},{96,64},{128,96},{160,128},{192,160},{224,1... | collective-permute-start | bytes 983048 | tf_op jit(solution)/shard_map/ppermute | solution.py:503
  194.2 0.0 all-to-all-done.4.ret_hbm
  194.2 1.4 sum_returned.3
  195.6 5.3 %all-to-all-start.5 = ((bf16[16,1,160,128]{3,2,1,0:T(8,128)(2,1)}), bf16[16,1,160,128]{3,2,1,0:T(8,128)(2,1)S(1)}, u32[]{:S(2)}, u32[]{:S(2)}) async-start(bf16[16,1,160,128]{3,2,1,0:T(8,128)(2,1)} %bitcast.5), calls=%async_computation.5 | async-start | bytes 1310720 | tf_op jit(solution)/shard_map/all_to_all | solution.py:553
  200.9 0.0 collective-permute-done.9
  200.9 0.1 add_convert_fusion.2
  201.0 0.3 collective-permute-start.10
  201.3 0.0 collective-permute-done.12
  201.3 0.1 add_convert_fusion
  201.4 3.1 %collective-permute-start.13 = (bf16[8,160,128]{2,1,0:T(8,128)(2,1)S(1)}, bf16[8,160,128]{2,1,0:T(8,128)(2,1)S(1)}, u32[]{:S(2)}, u32[]{:S(2)}) collective-permute-start(bf16[8,160,128]{2,1,0:T(8,128)(2,1)S(1)} %add_convert_fusion), channel_id=1, source_target_pairs={{0,224},{32,0},{64,32},{96,64},{128,96},{160,128},{192,160},{224,1... | collective-permute-start | bytes 983048 | tf_op jit(solution)/shard_map/ppermute | solution.py:503
  204.5 4.9 %collective-permute-done.10.rising_ref = bf16[8,160,128]{2,1,0:T(8,128)(2,1)S(1)} collective-permute-done((bf16[8,160,128]{2,1,0:T(8,128)(2,1)S(1)}, bf16[8,160,128]{2,1,0:T(8,128)(2,1)S(1)}, u32[]{:S(2)}, u32[]{:S(2)}) %collective-permute-start.10) | collective-permute-done | bytes 327712 | tf_op jit(solution)/shard_map/ppermute | solution.py:503
  209.4 0.0 collective-permute-done.13.falling_ref
  209.4 1.0 all-to-all-done.5.ret_ref
  210.4 1.9 finish.1
  (16 shorter events, 0.0 us)
Async XLA Ops:
  0.6 0.9 copy-start.6
  1.6 0.9 copy-start.7
  2.7 20.6 %collective-permute-start.1 = (bf16[8,160,128]{2,1,0:T(8,128)(2,1)S(1)}, bf16[8,160,128]{2,1,0:T(8,128)(2,1)S(1)}, u32[]{:S(2)}, u32[]{:S(2)}) collective-permute-start(bf16[8,160,128]{2,1,0:T(8,128)(2,1)S(1)} %pack.1.refs_0_.local_hbm), channel_id=1, source_target_pairs={{0,32},{32,64},{64,96},{96,128},{128,160},{160,192},{192,224},{224... | collective-permute-start | bytes 983048 | tf_op jit(solution)/shard_map/ppermute | solution.py:538
  4.7 18.6 %collective-permute-start = (bf16[8,160,128]{2,1,0:T(8,128)(2,1)S(1)}, bf16[8,160,128]{2,1,0:T(8,128)(2,1)S(1)}, u32[]{:S(2)}, u32[]{:S(2)}) collective-permute-start(bf16[8,160,128]{2,1,0:T(8,128)(2,1)S(1)} %pack.1.refs_0_.local_hbm), channel_id=1, source_target_pairs={{0,224},{32,0},{64,32},{96,64},{128,96},{160,128},{192,160},{224,1... | collective-permute-start | bytes 983048 | tf_op jit(solution)/shard_map/ppermute | solution.py:536
  23.2 2.8 %copy-start.4 = (s32[16,1,8]{2,1,0:T(1,128)}, s32[16,1,8]{2,1,0:T(1,128)S(1)}, u32[]{:S(2)}) copy-start(s32[16,1,8]{2,1,0:T(1,128)S(1)} %all_to_all.30) | copy-start | bytes 1540
  26.0 33.9 %all-to-all-start.1 = ((bf16[16,3,160,128]{3,2,1,0:T(8,128)(2,1)}), bf16[16,3,160,128]{3,2,1,0:T(8,128)(2,1)}, u32[]{:S(2)}, u32[]{:S(2)}) async-start(bf16[16,3,160,128]{3,2,1,0:T(8,128)(2,1)} %build.2), calls=%async_computation.1 | async-start | bytes 3932160 | tf_op jit(solution)/shard_map/all_to_all | solution.py:540
  31.7 7.9 %collective-permute-start.2 = (bf16[8,160,128]{2,1,0:T(8,128)(2,1)S(1)}, bf16[8,160,128]{2,1,0:T(8,128)(2,1)S(1)}, u32[]{:S(2)}, u32[]{:S(2)}) collective-permute-start(bf16[8,160,128]{2,1,0:T(8,128)(2,1)S(1)} %collective-permute-done.refs_1_), channel_id=1, source_target_pairs={{0,224},{32,0},{64,32},{96,64},{128,96},{160,128},{192,160},{224,1... | collective-permute-start | bytes 983048 | tf_op jit(solution)/shard_map/ppermute | solution.py:536
  33.6 8.4 %collective-permute-start.5 = (bf16[8,160,128]{2,1,0:T(8,128)(2,1)S(1)}, bf16[8,160,128]{2,1,0:T(8,128)(2,1)S(1)}, u32[]{:S(2)}, u32[]{:S(2)}) collective-permute-start(bf16[8,160,128]{2,1,0:T(8,128)(2,1)S(1)} %collective-permute-done.1.refs_2_), channel_id=1, source_target_pairs={{0,32},{32,64},{64,96},{96,128},{128,160},{160,192},{192,224},{224... | collective-permute-start | bytes 983048 | tf_op jit(solution)/shard_map/ppermute | solution.py:538
  39.5 15.5 %copy-start.8 = (bf16[8,160,128]{2,1,0:T(8,128)(2,1)}, bf16[8,160,128]{2,1,0:T(8,128)(2,1)S(1)}, u32[]{:S(2)}) copy-start(bf16[8,160,128]{2,1,0:T(8,128)(2,1)S(1)} %collective-permute-done.2.refs_0_) | copy-start | bytes 983044
  39.5 8.2 %collective-permute-start.3 = (bf16[8,160,128]{2,1,0:T(8,128)(2,1)S(1)}, bf16[8,160,128]{2,1,0:T(8,128)(2,1)S(1)}, u32[]{:S(2)}, u32[]{:S(2)}) collective-permute-start(bf16[8,160,128]{2,1,0:T(8,128)(2,1)S(1)} %collective-permute-done.2.refs_0_), channel_id=1, source_target_pairs={{0,224},{32,0},{64,32},{96,64},{128,96},{160,128},{192,160},{224,1... | collective-permute-start | bytes 983048 | tf_op jit(solution)/shard_map/ppermute | solution.py:536
  42.0 13.0 %copy-start.9 = (bf16[8,160,128]{2,1,0:T(8,128)(2,1)}, bf16[8,160,128]{2,1,0:T(8,128)(2,1)S(1)}, u32[]{:S(2)}) copy-start(bf16[8,160,128]{2,1,0:T(8,128)(2,1)S(1)} %collective-permute-done.5.refs_4_) | copy-start | bytes 983044
  42.0 8.4 %collective-permute-start.6 = (bf16[8,160,128]{2,1,0:T(8,128)(2,1)S(1)}, bf16[8,160,128]{2,1,0:T(8,128)(2,1)S(1)}, u32[]{:S(2)}, u32[]{:S(2)}) collective-permute-start(bf16[8,160,128]{2,1,0:T(8,128)(2,1)S(1)} %collective-permute-done.5.refs_4_), channel_id=1, source_target_pairs={{0,32},{32,64},{64,96},{96,128},{128,160},{160,192},{192,224},{224... | collective-permute-start | bytes 983048 | tf_op jit(solution)/shard_map/ppermute | solution.py:538
  47.7 7.3 %copy-start.10 = (bf16[8,160,128]{2,1,0:T(8,128)(2,1)}, bf16[8,160,128]{2,1,0:T(8,128)(2,1)S(1)}, u32[]{:S(2)}) copy-start(bf16[8,160,128]{2,1,0:T(8,128)(2,1)S(1)} %collective-permute-done.3.refs_1_) | copy-start | bytes 983044
  47.7 7.3 %collective-permute-start.4 = (bf16[8,160,128]{2,1,0:T(8,128)(2,1)S(1)}, bf16[8,160,128]{2,1,0:T(8,128)(2,1)S(1)}, u32[]{:S(2)}, u32[]{:S(2)}) collective-permute-start(bf16[8,160,128]{2,1,0:T(8,128)(2,1)S(1)} %collective-permute-done.3.refs_1_), channel_id=1, source_target_pairs={{0,224},{32,0},{64,32},{96,64},{128,96},{160,128},{192,160},{224,1... | collective-permute-start | bytes 983048 | tf_op jit(solution)/shard_map/ppermute | solution.py:536
  50.4 4.6 %copy-start.11 = (bf16[8,160,128]{2,1,0:T(8,128)(2,1)}, bf16[8,160,128]{2,1,0:T(8,128)(2,1)S(1)}, u32[]{:S(2)}) copy-start(bf16[8,160,128]{2,1,0:T(8,128)(2,1)S(1)} %collective-permute-done.6.refs_3_) | copy-start | bytes 983044
  55.0 0.7 copy-start.12
  59.9 42.9 %copy-start = (bf16[512,1536]{1,0:T(8,128)(2,1)S(1)}, bf16[512,1536]{1,0:T(8,128)(2,1)}, u32[]{:S(2)}) copy-start(bf16[512,1536]{1,0:T(8,128)(2,1)} %q_ref.1) | copy-start | bytes 4718596
  59.9 42.9 %copy-start.1 = (bf16[512,1024]{1,0:T(8,128)(2,1)S(1)}, bf16[512,1024]{1,0:T(8,128)(2,1)}, u32[]{:S(2)}) copy-start(bf16[512,1024]{1,0:T(8,128)(2,1)} %do_ref.1) | copy-start | bytes 3145732
  126.7 39.4 %copy-start.2 = (f32[8,160,128]{2,1,0:T(8,128)}, f32[8,160,128]{2,1,0:T(8,128)S(1)}, u32[]{:S(2)}) copy-start(f32[8,160,128]{2,1,0:T(8,128)S(1)} %get-tuple-element.30.own_ref) | copy-start | bytes 1966084
  126.8 39.4 %copy-start.5 = (s32[16,1,8]{2,1,0:T(1,128)S(1)}, s32[16,1,8]{2,1,0:T(1,128)}, u32[]{:S(2)}) copy-start(s32[16,1,8]{2,1,0:T(1,128)} %copy-done.4) | copy-start | bytes 1540
  168.8 11.3 %collective-permute-start.7 = (bf16[8,160,128]{2,1,0:T(8,128)(2,1)S(1)}, bf16[8,160,128]{2,1,0:T(8,128)(2,1)S(1)}, u32[]{:S(2)}, u32[]{:S(2)}) collective-permute-start(bf16[8,160,128]{2,1,0:T(8,128)(2,1)S(1)} %get-tuple-element.43), channel_id=1, source_target_pairs={{0,32},{32,64},{64,96},{96,128},{128,160},{160,192},{192,224},{224... | collective-permute-start | bytes 983048 | tf_op jit(solution)/shard_map/ppermute | solution.py:500
  170.1 24.1 %all-to-all-start.4 = ((bf16[16,2,160,128]{3,2,1,0:T(8,128)(2,1)}), bf16[16,2,160,128]{3,2,1,0:T(8,128)(2,1)S(1)}, u32[]{:S(2)}, u32[]{:S(2)}) async-start(bf16[16,2,160,128]{3,2,1,0:T(8,128)(2,1)} %get-tuple-element.38), calls=%async_computation.4 | async-start | bytes 2621440 | tf_op jit(solution)/shard_map/all_to_all | solution.py:549
  180.2 10.4 %collective-permute-start.8 = (bf16[8,160,128]{2,1,0:T(8,128)(2,1)S(1)}, bf16[8,160,128]{2,1,0:T(8,128)(2,1)S(1)}, u32[]{:S(2)}, u32[]{:S(2)}) collective-permute-start(bf16[8,160,128]{2,1,0:T(8,128)(2,1)S(1)} %add_convert_fusion.4), channel_id=1, source_target_pairs={{0,32},{32,64},{64,96},{96,128},{128,160},{160,192},{192,224},{224... | collective-permute-start | bytes 983048 | tf_op jit(solution)/shard_map/ppermute | solution.py:503
  181.0 9.8 %collective-permute-start.11 = (bf16[8,160,128]{2,1,0:T(8,128)(2,1)S(1)}, bf16[8,160,128]{2,1,0:T(8,128)(2,1)S(1)}, u32[]{:S(2)}, u32[]{:S(2)}) collective-permute-start(bf16[8,160,128]{2,1,0:T(8,128)(2,1)S(1)} %get-tuple-element.47), channel_id=1, source_target_pairs={{0,224},{32,0},{64,32},{96,64},{128,96},{160,128},{192,160},{224,1... | collective-permute-start | bytes 983048 | tf_op jit(solution)/shard_map/ppermute | solution.py:500
  190.7 10.2 %collective-permute-start.9 = (bf16[8,160,128]{2,1,0:T(8,128)(2,1)S(1)}, bf16[8,160,128]{2,1,0:T(8,128)(2,1)S(1)}, u32[]{:S(2)}, u32[]{:S(2)}) collective-permute-start(bf16[8,160,128]{2,1,0:T(8,128)(2,1)S(1)} %add_convert_fusion.3), channel_id=1, source_target_pairs={{0,32},{32,64},{64,96},{96,128},{128,160},{160,192},{192,224},{224... | collective-permute-start | bytes 983048 | tf_op jit(solution)/shard_map/ppermute | solution.py:503
  190.9 10.4 %collective-permute-start.12 = (bf16[8,160,128]{2,1,0:T(8,128)(2,1)S(1)}, bf16[8,160,128]{2,1,0:T(8,128)(2,1)S(1)}, u32[]{:S(2)}, u32[]{:S(2)}) collective-permute-start(bf16[8,160,128]{2,1,0:T(8,128)(2,1)S(1)} %add_convert_fusion.1), channel_id=1, source_target_pairs={{0,224},{32,0},{64,32},{96,64},{128,96},{160,128},{192,160},{224,1... | collective-permute-start | bytes 983048 | tf_op jit(solution)/shard_map/ppermute | solution.py:503
  195.6 14.8 %copy-start.3 = (f32[8,160,128]{2,1,0:T(8,128)S(1)}, f32[8,160,128]{2,1,0:T(8,128)}, u32[]{:S(2)}) copy-start(f32[8,160,128]{2,1,0:T(8,128)} %copy-done.2) | copy-start | bytes 1966084
  195.6 14.7 %all-to-all-start.5 = ((bf16[16,1,160,128]{3,2,1,0:T(8,128)(2,1)}), bf16[16,1,160,128]{3,2,1,0:T(8,128)(2,1)S(1)}, u32[]{:S(2)}, u32[]{:S(2)}) async-start(bf16[16,1,160,128]{3,2,1,0:T(8,128)(2,1)} %bitcast.5), calls=%async_computation.5 | async-start | bytes 1310720 | tf_op jit(solution)/shard_map/all_to_all | solution.py:553
  201.0 8.4 %collective-permute-start.10 = (bf16[8,160,128]{2,1,0:T(8,128)(2,1)S(1)}, bf16[8,160,128]{2,1,0:T(8,128)(2,1)S(1)}, u32[]{:S(2)}, u32[]{:S(2)}) collective-permute-start(bf16[8,160,128]{2,1,0:T(8,128)(2,1)S(1)} %add_convert_fusion.2), channel_id=1, source_target_pairs={{0,32},{32,64},{64,96},{96,128},{128,160},{160,192},{192,224},{224... | collective-permute-start | bytes 983048 | tf_op jit(solution)/shard_map/ppermute | solution.py:503
  201.4 8.0 %collective-permute-start.13 = (bf16[8,160,128]{2,1,0:T(8,128)(2,1)S(1)}, bf16[8,160,128]{2,1,0:T(8,128)(2,1)S(1)}, u32[]{:S(2)}, u32[]{:S(2)}) collective-permute-start(bf16[8,160,128]{2,1,0:T(8,128)(2,1)S(1)} %add_convert_fusion), channel_id=1, source_target_pairs={{0,224},{32,0},{64,32},{96,64},{128,96},{160,128},{192,160},{224,1... | collective-permute-start | bytes 983048 | tf_op jit(solution)/shard_map/ppermute | solution.py:503
